TPU v7x, 32 devices: a whole 2x2x4 slice. The times are simulated.
32 devices in a mesh: dp: 8 (over z, y), tensor: 4 (over x, core).
Axes of the slice: x: 2, y: 2, z: 4, core: 2. Of those that a mesh axis runs over, the one named last changes fastest.
Arguments:
- tokens: bfloat16 [32, 1024, 768], P('dp', 'tensor'), may hold values from -6 to 6
- lengths: int32 [32, 2], P('dp'), may hold values from 1 to 1023, as said below
- cotangent: bfloat16 [32, 1024, 768], P('dp', 'tensor'), may hold values from -6 to 6
- norm_gain: float32 [768], replicated, may hold values from 0.5 to 1.5
- w_z: bfloat16 [768, 1536], P('dp', 'tensor'), may hold values from -0.21875 to 0.21875
- w_x: bfloat16 [768, 1536], P('dp', 'tensor'), may hold values from -0.21875 to 0.21875
- w_bc: bfloat16 [768, 256], P('dp'), may hold values from -0.21875 to 0.21875
- w_dt: bfloat16 [768, 24], P('dp', 'tensor'), may hold values from -0.21875 to 0.21875
- conv_x: float32 [4, 1536], P(None, 'tensor'), may hold values from -3 to 3
- bias_x: float32 [1536], P('tensor'), may hold values from -1.5 to 1.5
- conv_bc: float32 [4, 256], replicated, may hold values from -3 to 3
- bias_bc: float32 [256], replicated, may hold values from -1.5 to 1.5
- dt_bias: float32 [24], P('tensor'), may hold values from -7 to -2
- a_log: float32 [24], P('tensor'), may hold values from 0 to 2.8
- skip_d: float32 [24], P('tensor'), may hold values from 0.5 to 1.5
- out_gain: float32 [1536], P('tensor'), may hold values from 0.5 to 1.5
- w_out: bfloat16 [768, 1536], P('dp', 'tensor'), may hold values from -0.15625 to 0.15625
Outputs:
- output: bfloat16 [32, 1024, 768], P('dp', 'tensor')
- input_grad: bfloat16 [32, 1024, 768], P('dp', 'tensor')
- grad_norm_gain: float32 [768], replicated
- grad_w_z: float32 [768, 1536], P('dp', 'tensor')
- grad_w_x: float32 [768, 1536], P('dp', 'tensor')
- grad_w_bc: float32 [768, 256], P(('dp', 'tensor'))
- grad_w_dt: float32 [768, 24], P('dp', 'tensor')
- grad_conv_x: float32 [4, 1536], P(None, 'tensor')
- grad_bias_x: float32 [1536], P('tensor')
- grad_conv_bc: float32 [4, 256], replicated
- grad_bias_bc: float32 [256], replicated
- grad_dt_bias: float32 [24], P('tensor')
- grad_a_log: float32 [24], P('tensor')
- grad_skip_d: float32 [24], P('tensor')
- grad_out_gain: float32 [1536], P('tensor')
- grad_w_out: float32 [768, 1536], P('dp', 'tensor')
Inputs may be any that keep to these rules, and one draw needn't show every extreme that they name: Each row holds the lengths of the two sequences packed from a slot's first position, together at most 1024; the rest of the slot is padding. One of the two is longer than 768.
All inputs are finite; a program needn't handle non-finite values.
Results may differ from a plain program's by a relative error of at most 0.015.
Values may be sent and summed in bfloat16 or wider, within the bound.
No kernel may reach another device: no remote copies, remote signals or barrier semaphores. Data moves between devices by JAX's collectives and lax.ppermute only.
A program may use at most 256 MiB of HBM per device.

v0:
```python
import jax
import jax.numpy as jnp
from jax import lax
from jax.sharding import PartitionSpec as P

INNER = 1536
GROUP = 256


EPS = 1e-05


def split_up(value, dim, length):
    dims = value.shape
    parts = value.reshape(*dims[:dim], length, dims[dim] // length, *dims[dim + 1 :])
    return jnp.moveaxis(parts, dim, 0)


def sent_and_summed(value, axis, dim):
    parts = split_up(value, dim, lax.axis_size(axis))
    arrived = lax.all_to_all(parts, axis, split_axis=0, concat_axis=0, tiled=True)
    return arrived.astype(jnp.float32).sum(axis=0)


def rms_scale(values):
    return lax.rsqrt(jnp.mean(values * values, axis=-1, keepdims=True) + EPS)


def causal_conv(values, weight, bias_vec, seg_ids):
    conv_sum = bias_vec + weight[0] * values
    for offset in range(1, weight.shape[0]):
        shifted = jnp.pad(values, ((0, 0), (offset, 0), (0, 0)))[:, :-offset]
        shifted_ids = jnp.pad(seg_ids, ((0, 0), (offset, 0)), constant_values=-1)[:, :-offset]
        keep_mask = (shifted_ids == seg_ids).astype(jnp.float32)[:, :, None]
        conv_sum = conv_sum + weight[offset] * shifted * keep_mask
    return conv_sum


def by_slot(values, slot_count):
    return jnp.swapaxes(values.reshape((slot_count, -1) + values.shape[1:]), 0, 1)


def from_slot(values):
    return jnp.swapaxes(values, 0, 1).reshape((-1,) + values.shape[2:])


def spread_cols(values, slot_index, count):
    width = values.shape[-1]
    full = jnp.zeros(values.shape[:-1] + (width * count,), jnp.float32)
    return lax.dynamic_update_slice_in_dim(full, values, slot_index * width, values.ndim - 1)


def own_cols(values, slot_index, width):
    return lax.dynamic_slice_in_dim(values, slot_index * width, width, values.ndim - 1)


def mixer_forward(x_low, b_low, c_low, step_size, log_decay, skip_d, seg_ids):
    slot_count, slot_len = seg_ids.shape
    group_count = slot_len // GROUP
    count_all = slot_count * group_count
    head_count = step_size.shape[-1]
    head_dim = x_low.shape[-1] // head_count
    x_heads = x_low.reshape(count_all, GROUP, head_count, head_dim)
    b_group = b_low.reshape(count_all, GROUP, -1)
    c_group = c_low.reshape(count_all, GROUP, -1)
    step_group = step_size.reshape(count_all, GROUP, head_count)
    cum_decay = jnp.cumsum(log_decay.reshape(count_all, GROUP, head_count), axis=1)
    seg_group = seg_ids.reshape(count_all, GROUP)
    places = jnp.arange(GROUP)
    same_seq = (seg_group[:, :, None] == seg_group[:, None, :]) & (
        places[:, None] >= places[None, :]
    )
    cum_heads = jnp.transpose(cum_decay, (0, 2, 1))
    log_gaps = cum_heads[:, :, :, None] - cum_heads[:, :, None, :]
    inside = same_seq[:, None]
    kernel = jnp.where(inside, jnp.exp(jnp.where(inside, log_gaps, 0.0)), 0.0)
    scores = jnp.einsum("cqn,ckn->cqk", c_group, b_group, preferred_element_type=jnp.float32)
    step_heads = jnp.transpose(step_group, (0, 2, 1))
    weights = (scores[:, None] * kernel * step_heads[:, :, None, :]).astype(jnp.bfloat16)
    within = jnp.einsum("chqk,ckhp->cqhp", weights, x_heads, preferred_element_type=jnp.float32)
    last_seg = seg_group[:, -1]
    tail_mask = (seg_group == last_seg[:, None]).astype(jnp.float32)[:, :, None]
    ending = jnp.exp(cum_decay[:, -1:, :] - cum_decay)
    to_end = ending * step_group * tail_mask
    b_weighted = (to_end[:, :, :, None] * b_group[:, :, None, :].astype(jnp.float32)).astype(
        jnp.bfloat16
    )
    states = jnp.einsum("cqhn,cqhp->chnp", b_weighted, x_heads, preferred_element_type=jnp.float32)
    group_decay = jnp.exp(cum_decay[:, -1, :])
    slot_last = last_seg.reshape(slot_count, group_count)
    follows = jnp.concatenate(
        [
            jnp.zeros((slot_count, 1), jnp.float32),
            (slot_last[:, 1:] == slot_last[:, :-1]).astype(jnp.float32),
        ],
        axis=1,
    ).reshape(count_all)
    factors = group_decay * follows[:, None]

    def carry_step(carried, inputs):
        state_now, factor = inputs
        return (factor[:, :, None, None] * carried + state_now, carried)

    start_state = jnp.zeros((slot_count,) + states.shape[1:], jnp.float32)
    _, prev_slots = lax.scan(
        carry_step, start_state, (by_slot(states, slot_count), by_slot(factors, slot_count))
    )
    previous = from_slot(prev_slots)
    prev_low = previous.astype(jnp.bfloat16)
    from_prev = jnp.einsum("cqn,chnp->cqhp", c_group, prev_low, preferred_element_type=jnp.float32)
    prev_seg = jnp.concatenate(
        [jnp.full((slot_count, 1), -1, jnp.int32), slot_last[:, :-1]], axis=1
    ).reshape(count_all)
    enters = (seg_group == prev_seg[:, None]).astype(jnp.float32)
    reach_in = jnp.exp(cum_decay) * enters[:, :, None]
    combined = (
        within + reach_in[..., None] * from_prev + skip_d[:, None] * x_heads.astype(jnp.float32)
    )
    kept_parts = (
        x_heads,
        b_group,
        c_group,
        step_group,
        kernel,
        scores,
        weights,
        ending,
        tail_mask,
        to_end,
        b_weighted,
        previous,
        prev_low,
        from_prev,
        reach_in,
        group_decay,
        follows,
        factors,
    )
    return (combined.reshape(slot_count, slot_len, head_count * head_dim), kept_parts)


def mixer_backward(dy_low, kept_parts, skip_d, slot_count):
    (
        x_heads,
        b_group,
        c_group,
        step_group,
        kernel,
        scores,
        weights,
        ending,
        tail_mask,
        to_end,
        b_weighted,
        previous,
        prev_low,
        from_prev,
        reach_in,
        group_decay,
        follows,
        factors,
    ) = kept_parts
    group_len = x_heads.shape[1]
    dy_heads = dy_low.reshape(x_heads.shape)
    dy_float = dy_heads.astype(jnp.float32)
    skip_grad = jnp.sum(dy_float * x_heads.astype(jnp.float32), axis=(0, 1, 3))
    dx_heads = skip_d[:, None] * dy_float
    dprev = dy_float * reach_in[..., None]
    dprev_low = dprev.astype(jnp.bfloat16)
    cum_grad = jnp.sum(dprev * from_prev, axis=-1)
    dc_group = jnp.einsum("cqhp,chnp->cqn", dprev_low, prev_low, preferred_element_type=jnp.float32)
    dprev_state = jnp.einsum(
        "cqn,cqhp->chnp", c_group, dprev_low, preferred_element_type=jnp.float32
    )
    dweights = jnp.einsum("cqhp,ckhp->chqk", dy_heads, x_heads, preferred_element_type=jnp.float32)
    dx_heads = dx_heads + jnp.einsum(
        "chqk,cqhp->ckhp", weights, dy_heads, preferred_element_type=jnp.float32
    )
    step_heads = jnp.transpose(step_group, (0, 2, 1))
    dscores_low = jnp.sum(dweights * kernel * step_heads[:, :, None, :], axis=1).astype(
        jnp.bfloat16
    )
    through = dweights * scores[:, None]
    log_grad = through * step_heads[:, :, None, :] * kernel
    cum_grad = cum_grad + jnp.transpose(
        jnp.sum(log_grad, axis=3) - jnp.sum(log_grad, axis=2), (0, 2, 1)
    )
    step_grad = jnp.transpose(jnp.sum(through * kernel, axis=2), (0, 2, 1))
    dc_group = dc_group + jnp.einsum(
        "cqk,ckn->cqn", dscores_low, b_group, preferred_element_type=jnp.float32
    )
    db_group = jnp.einsum("cqk,cqn->ckn", dscores_low, c_group, preferred_element_type=jnp.float32)

    def back_step(grad_after, inputs):
        prev_grad, prev_state, factor = inputs
        factor_grad = jnp.sum(grad_after * prev_state, axis=(2, 3))
        return (prev_grad + factor[:, :, None, None] * grad_after, (grad_after, factor_grad))

    zero_grad = jnp.zeros((slot_count,) + previous.shape[1:], jnp.float32)
    _, (dstates_slots, dfactor_slots) = lax.scan(
        back_step,
        zero_grad,
        (
            by_slot(dprev_state, slot_count),
            by_slot(previous, slot_count),
            by_slot(factors, slot_count),
        ),
        reverse=True,
    )
    dstates_low = from_slot(dstates_slots).astype(jnp.bfloat16)
    last_extra = from_slot(dfactor_slots) * follows[:, None] * group_decay
    dbw = jnp.einsum("cqhp,chnp->cqhn", x_heads, dstates_low, preferred_element_type=jnp.float32)
    dx_heads = dx_heads + jnp.einsum(
        "cqhn,chnp->cqhp", b_weighted, dstates_low, preferred_element_type=jnp.float32
    )
    dto_end = jnp.sum(dbw * b_group[:, :, None, :].astype(jnp.float32), axis=-1)
    db_group = db_group + jnp.sum(dbw * to_end[..., None], axis=2)
    end_terms = dto_end * to_end
    last_extra = last_extra + jnp.sum(end_terms, axis=1)
    cum_grad = cum_grad - end_terms
    step_grad = step_grad + dto_end * ending * tail_mask
    is_last = (jnp.arange(group_len) == group_len - 1).astype(jnp.float32)[None, :, None]
    cum_grad = cum_grad + is_last * last_extra[:, None, :]
    dlog_decay = jnp.flip(jnp.cumsum(jnp.flip(cum_grad, 1), axis=1), 1)
    return (dx_heads, db_group, dc_group, step_grad, dlog_decay, skip_grad)


def per_device(
    tokens,
    lengths,
    cotangent,
    norm_gain,
    w_z,
    w_x,
    w_bc,
    w_dt,
    conv_x,
    bias_x,
    conv_bc,
    bias_bc,
    dt_bias,
    a_log,
    skip_d,
    out_gain,
    w_out,
):
    tensor_count = lax.axis_size("tensor")
    tensor_slot = lax.axis_index("tensor")
    slot_count, own_len, model_dim = tokens.shape
    slot_len = own_len * tensor_count
    all_rows = slot_count * slot_len
    inner_local = w_z.shape[1]
    head_local = w_dt.shape[1]
    state_dim = conv_bc.shape[1] // 2
    first_row = tensor_slot * own_len
    places = jnp.arange(slot_len)
    first_end = lengths[:, 0:1]
    second_end = first_end + lengths[:, 1:2]
    seg_ids = (places[None, :] >= first_end).astype(jnp.int32) + (
        places[None, :] >= second_end
    ).astype(jnp.int32)
    own_places = first_row + jnp.arange(own_len)
    valid_rows = (own_places[None, :] < second_end).astype(jnp.float32)[:, :, None]
    residual = tokens.astype(jnp.float32)

    def norm_apply(values, gain_vec):
        return values * rms_scale(values) * gain_vec

    normed_float, norm_pull = jax.vjp(norm_apply, residual, norm_gain)
    normed = normed_float.astype(jnp.bfloat16)
    normed_all = lax.all_gather(normed, "tensor", axis=1, tiled=True)
    flat_normed = normed_all.reshape(all_rows, model_dim)
    gathered = (
        lax.all_gather(w_z, "dp", axis=0, tiled=True),
        lax.all_gather(w_x, "dp", axis=0, tiled=True),
        lax.all_gather(w_bc, "dp", axis=0, tiled=True),
        lax.all_gather(w_dt, "dp", axis=0, tiled=True),
        lax.all_gather(w_out, "dp", axis=0, tiled=True),
    )
    in_weight = jnp.concatenate([gathered[0], gathered[1], gathered[3], gathered[2]], axis=1)
    in_part = jnp.concatenate([gathered[0], gathered[1], gathered[3]], axis=1)
    projected = jnp.dot(flat_normed, in_weight, preferred_element_type=jnp.float32).reshape(
        slot_count, slot_len, -1
    )
    gate_in = projected[:, :, :inner_local]
    inner_x = projected[:, :, inner_local : 2 * inner_local]
    dt_raw = projected[:, :, 2 * inner_local : 2 * inner_local + head_local]
    state_in = projected[:, :, 2 * inner_local + head_local :]

    def conv_silu(values, weight, bias_vec):
        return jax.nn.silu(causal_conv(values, weight, bias_vec, seg_ids))

    x_act, x_pull = jax.vjp(conv_silu, inner_x, conv_x, bias_x)
    bc_act, bc_pull = jax.vjp(conv_silu, state_in, conv_bc, bias_bc)
    x_low = x_act.astype(jnp.bfloat16)
    b_low = bc_act[:, :, :state_dim].astype(jnp.bfloat16)
    c_low = bc_act[:, :, state_dim:].astype(jnp.bfloat16)

    def step_apply(raw_rates, bias_vec, rate_logs):
        step_size = jax.nn.softplus(raw_rates + bias_vec)
        return (step_size, step_size * -jnp.exp(rate_logs))

    (step_size, log_decay), step_pull = jax.vjp(step_apply, dt_raw, dt_bias, a_log)
    mixer_out, kept_parts = mixer_forward(
        x_low, b_low, c_low, step_size, log_decay, skip_d, seg_ids
    )
    silu_gate, silu_pull = jax.vjp(jax.nn.silu, gate_in)
    gated_out = mixer_out * silu_gate
    total_sq = lax.psum(jnp.sum(gated_out * gated_out, axis=-1), "tensor")
    gate_scale = lax.rsqrt(total_sq / INNER + EPS)[:, :, None]
    gnormed = (gated_out * gate_scale * out_gain).astype(jnp.bfloat16)
    flat_gnormed = gnormed.reshape(all_rows, inner_local)
    branch_part = lax.dot_general(
        flat_gnormed, gathered[4], (((1,), (1,)), ((), ())), preferred_element_type=jnp.float32
    )
    branch = lax.psum_scatter(
        branch_part.reshape(slot_count, slot_len, model_dim).astype(jnp.bfloat16),
        "tensor",
        scatter_dimension=1,
        tiled=True,
    ).astype(jnp.float32)
    output = (residual + branch).astype(jnp.bfloat16)
    dbranch = cotangent.astype(jnp.float32) * valid_rows
    dbranch_all = lax.all_gather(dbranch.astype(jnp.bfloat16), "tensor", axis=1, tiled=True)
    flat_dbranch = dbranch_all.reshape(all_rows, model_dim)
    dgnormed = jnp.dot(flat_dbranch, gathered[4], preferred_element_type=jnp.float32).reshape(
        slot_count, slot_len, inner_local
    )
    gain_out_grad = jnp.sum(dgnormed * (gated_out * gate_scale), axis=(0, 1))
    scaled = dgnormed * out_gain
    total_dot = lax.psum(jnp.sum(scaled * gated_out, axis=-1), "tensor")
    scale_cube = gate_scale * gate_scale * gate_scale
    dgated = gate_scale * scaled - gated_out * scale_cube * (total_dot / INNER)[:, :, None]
    dy_low = (dgated * silu_gate).astype(jnp.bfloat16)
    (gate_in_grad,) = silu_pull(dgated * mixer_out)
    dx_heads, db_group, dc_group, step_grad, dlog_decay, skip_grad = mixer_backward(
        dy_low, kept_parts, skip_d, slot_count
    )
    dbc_part = jnp.concatenate([db_group, dc_group], axis=-1).reshape(
        slot_count, slot_len, 2 * state_dim
    )
    dbc_total = lax.psum(dbc_part.astype(jnp.bfloat16), "tensor").astype(jnp.float32)
    dstate_in, conv_bc_grad, bias_bc_grad = bc_pull(dbc_total)
    dinner_x, conv_x_grad, bias_x_grad = x_pull(dx_heads.reshape(slot_count, slot_len, inner_local))
    ddt_raw, dt_bias_grad, a_log_grad = step_pull(
        (
            step_grad.reshape(slot_count, slot_len, head_local),
            dlog_decay.reshape(slot_count, slot_len, head_local),
        )
    )
    in_grad = (
        jnp.concatenate([gate_in_grad, dinner_x, ddt_raw], axis=-1)
        .astype(jnp.bfloat16)
        .reshape(all_rows, -1)
    )
    dnormed_part = lax.dot_general(
        in_grad, in_part, (((1,), (1,)), ((), ())), preferred_element_type=jnp.float32
    )
    dnormed = lax.psum_scatter(
        dnormed_part.reshape(slot_count, slot_len, model_dim).astype(jnp.bfloat16),
        "tensor",
        scatter_dimension=1,
        tiled=True,
    ).astype(jnp.float32)
    own_state = (
        lax.dynamic_slice_in_dim(dstate_in, first_row, own_len, axis=1)
        .astype(jnp.bfloat16)
        .reshape(slot_count * own_len, 2 * state_dim)
    )
    state_back = lax.dot_general(
        own_state, gathered[2], (((1,), (1,)), ((), ())), preferred_element_type=jnp.float32
    )
    dnormed = dnormed + state_back.reshape(slot_count, own_len, model_dim)
    dresidual, norm_gain_part = norm_pull(dnormed)
    input_grad = (dbranch + dresidual).astype(jnp.bfloat16)
    inner_cols = 2 * inner_local + head_local
    columns = flat_normed
    front_part = lax.dot_general(
        columns, in_grad, (((0,), (0,)), ((), ())), preferred_element_type=jnp.float32
    )
    back_part = lax.dot_general(
        flat_dbranch, flat_gnormed, (((0,), (0,)), ((), ())), preferred_element_type=jnp.float32
    )
    wide_grads = sent_and_summed(
        jnp.concatenate([front_part, back_part], axis=1).astype(jnp.bfloat16), "dp", 0
    )
    own_normed = normed.reshape(slot_count * own_len, model_dim)
    columns = own_normed
    w_bc_grad = lax.psum_scatter(
        lax.dot_general(
            columns, own_state, (((0,), (0,)), ((), ())), preferred_element_type=jnp.float32
        ),
        ("dp", "tensor"),
        scatter_dimension=0,
        tiled=True,
    )
    first_flag = (tensor_slot == 0).astype(jnp.float32)
    small_sums = lax.psum(
        (
            spread_cols(conv_x_grad, tensor_slot, tensor_count),
            spread_cols(bias_x_grad, tensor_slot, tensor_count),
            spread_cols(dt_bias_grad, tensor_slot, tensor_count),
            spread_cols(a_log_grad, tensor_slot, tensor_count),
            spread_cols(skip_grad, tensor_slot, tensor_count),
            spread_cols(gain_out_grad, tensor_slot, tensor_count),
            conv_bc_grad * first_flag,
            bias_bc_grad * first_flag,
            norm_gain_part,
        ),
        ("dp", "tensor"),
    )
    conv_x_total = own_cols(small_sums[0], tensor_slot, inner_local)
    bias_x_total = own_cols(small_sums[1], tensor_slot, inner_local)
    dt_bias_total = own_cols(small_sums[2], tensor_slot, head_local)
    a_log_total = own_cols(small_sums[3], tensor_slot, head_local)
    skip_total = own_cols(small_sums[4], tensor_slot, head_local)
    out_gain_total = own_cols(small_sums[5], tensor_slot, inner_local)
    return (
        output,
        input_grad,
        small_sums[8],
        wide_grads[:, :inner_local],
        wide_grads[:, inner_local : 2 * inner_local],
        w_bc_grad,
        wide_grads[:, 2 * inner_local : inner_cols],
        conv_x_total,
        bias_x_total,
        small_sums[6],
        small_sums[7],
        dt_bias_total,
        a_log_total,
        skip_total,
        out_gain_total,
        wide_grads[:, inner_cols:],
    )


def solution(mesh):
    return jax.shard_map(
        per_device,
        mesh=mesh,
        in_specs=(
            P("dp", "tensor", None),
            P("dp", None),
            P("dp", "tensor", None),
            P(),
            P("dp", "tensor"),
            P("dp", "tensor"),
            P("dp", None),
            P("dp", "tensor"),
            P(None, "tensor"),
            P("tensor"),
            P(),
            P(),
            P("tensor"),
            P("tensor"),
            P("tensor"),
            P("tensor"),
            P("dp", "tensor"),
        ),
        out_specs=(
            P("dp", "tensor", None),
            P("dp", "tensor", None),
            P(),
            P("dp", "tensor"),
            P("dp", "tensor"),
            P(("dp", "tensor"), None),
            P("dp", "tensor"),
            P(None, "tensor"),
            P("tensor"),
            P(),
            P(),
            P("tensor"),
            P("tensor"),
            P("tensor"),
            P("tensor"),
            P("dp", "tensor"),
        ),
        check_vma=False,
    )
```

profile of v0, /device:TPU:0, one launch (start us, length us, event | category | flops | bytes accessed | tf_op | source)
XLA Modules:
  0.0 802.3 jit_solution(17598874591518586094)
XLA Ops:
  10.3 3.0 fusion.33
  20.0 27.8 %all-gather = bf16[8,96,6]{1,2,0:T(8,128)(2,1)S(1)} all-gather(bf16[1,96,6]{1,2,0:T(8,128)(2,1)S(1)} %bitcast.253), channel_id=1, replica_groups=mesh['dp'=8,'tensor'=4] {'dp'}, dimensions={0}, use_global_device_ids=true | all-gather | bytes 10368 | tf_op jit(solution)/shard_map/all_gather | solution.py:277
  48.9 31.0 %all_gather.25 = bf16[768,256]{1,0:T(8,128)(2,1)S(1)} all-gather(bf16[96,256]{1,0:T(8,128)(2,1)S(1)} %copy-done.64), channel_id=1, replica_groups=mesh['dp'=8,'tensor'=4] {'dp'}, dimensions={0}, use_global_device_ids=true | all-gather | bytes 442368 | tf_op jit(solution)/shard_map/all_gather | solution.py:276
  80.7 33.8 %all_gather.26 = bf16[768,384]{1,0:T(8,128)(2,1)} all-gather(bf16[96,384]{1,0:T(8,128)(2,1)S(1)} %copy-done.59), channel_id=1, replica_groups=mesh['dp'=8,'tensor'=4] {'dp'}, dimensions={0}, use_global_device_ids=true | all-gather | bytes 663552 | tf_op jit(solution)/shard_map/all_gather | solution.py:278
  114.6 31.5 %all_gather.22 = bf16[768,384]{1,0:T(8,128)(2,1)S(1)} all-gather(bf16[96,384]{1,0:T(8,128)(2,1)S(1)} %copy-done.60), channel_id=1, replica_groups=mesh['dp'=8,'tensor'=4] {'dp'}, dimensions={0}, use_global_device_ids=true | all-gather | bytes 663552 | tf_op jit(solution)/shard_map/all_gather | solution.py:274
  146.4 31.5 %all_gather.23 = bf16[768,384]{1,0:T(8,128)(2,1)S(1)} all-gather(bf16[96,384]{1,0:T(8,128)(2,1)S(1)} %copy-done.61), channel_id=1, replica_groups=mesh['dp'=8,'tensor'=4] {'dp'}, dimensions={0}, use_global_device_ids=true | all-gather | bytes 663552 | tf_op jit(solution)/shard_map/all_gather | solution.py:275
  178.1 3.0 compare_and_fusion
  181.1 7.9 concatenate.33
  189.1 9.4 %fusion.55 = f32[4,1024,1030]{1,2,0:T(8,128)S(1)} fusion(bf16[4,1024,768]{2,1,0:T(8,128)(2,1)} %all-gather.4.cloned.1.call-done, bf16[768,1030]{0,1:T(8,128)(2,1)} %concatenate.33), kind=kOutput, calls=%fused_computation.135 | convolution fusion | flops 6480199680 | bytes 24749056 | tf_op jit(solution)/shard_map/dot_general | solution.py:282
  198.5 5.8 copy-done.1
  204.6 3.4 reduce-window.14
  209.5 5.5 slice.165
  214.9 6.5 slice.164
  228.0 9.6 %multiply_convert_fusion.9 = (bf16[4,1024,256]{1,2,0:T(8,128)(2,1)S(1)}, f32[4,1024,256]{1,2,0:T(8,128)}) fusion(f32[4,1024]{1,0:T(4,128)S(1)} %get-tuple-element.554, f32[4,1024,256]{1,2,0:T(8,128)} %slice.165, f32[256]{0:T(256)} %bitcast.245, f32[4,1024]{1,0:T(4,128)S(1)} %get-tuple-element.553, f32[256]{0:T(256)} %bitcast.247, ...), kind=kLoop, calls=%fused_computation.98 | loop fusion | flops 16777216 | bytes 10540032 | tf_op jit(solution)/shard_map/convert.12
  240.9 2.7 copy.493
  245.2 14.2 %multiply_convert_fusion.8 = (bf16[4,1024,384]{1,2,0:T(8,128)(2,1)S(1)}, f32[4,1024,384]{1,2,0:T(8,128)}) fusion(f32[4,1024]{1,0:T(4,128)S(1)} %get-tuple-element.554, f32[4,1024,384]{1,2,0:T(8,128)} %slice.164, f32[384]{0:T(512)S(1)} %copy-done.81, f32[4,1024]{1,0:T(4,128)S(1)} %get-tuple-element.553, f32[384]{0:T(512)S(1)} %copy-done.83, ...), kind=kLoop, calls=%fused_computation.71 | loop fusion | flops 25165824 | bytes 15785472 | tf_op jit(solution)/shard_map/convert_element_type | solution.py:295
  261.2 4.1 copy.492
  265.3 6.0 reshape.576
  271.3 6.4 fusion.6
  277.7 5.8 copy.515
  283.5 12.0 %while.32 = (s32[]{:T(128)}, f32[4,6,128,64]{3,2,1,0:T(8,128)S(1)}, f32[4,4,6,128,64]{4,3,2,1,0:T(8,128)}, f32[4,4,6]{2,1,0:T(4,128)S(1)}, f32[4,4,6,128,64]{4,3,2,1,0:T(8,128)}, /*index=5*/s32[]{:T(128)}, s32[]{:T(128)}) while((s32[]{:T(128)}, f32[4,6,128,64]{3,2,1,0:T(8,128)S(1)}, f32[4,4,6,128,64]{4,3,2,1,0:T(8,128)}, ...), condition=%wide.region_4.5_spmd.clone, body=%wide.region_3.4_spmd.clone.sunk | while | flops 786435 | bytes 4718988 | solution.py:105
  295.5 5.2 copy.517
  303.5 2.8 copy-done.27
  307.2 10.5 %fusion.23 = f32[16,256,6,64]{1,3,2,0:T(8,128)S(1)} fusion(f32[16,256,6,64]{1,3,2,0:T(8,128)S(1)} %bitcast.209, f32[6]{0:T(128)S(1)} %copy-done.108, f32[16,256,6]{1,2,0:T(8,128)S(1)} %copy.507, f32[16,6,256]{2,1,0:T(8,128)S(1)} %copy-done.55, f32[16,6,256]{2,1,0:T(8,128)S(1)} %copy-done.53, f32[16,256,256]{2,1,0:T(8,128)S(1)} %fusion.101, ...), kind=kOutput, calls=%fused_computation.52 | convolution fusion | flops 850919424 | bytes 21266456 | tf_op jit(solution)/shard_map/chqk,ckhp->cqhp/dot_general | solution.py:80
  317.8 6.3 copy.519
  324.0 8.1 %reshape.584 = f32[4,1024,384]{1,0,2:T(4,128)} reshape(f32[16,256,6,64]{1,0,3,2:T(8,128)} %copy.519) | data formatting | bytes 12582912 | tf_op jit(solution)/shard_map/reshape | solution.py:139
  332.1 8.0 multiply_reduce_fusion.9
  340.1 10.1 %psum.84 = f32[4,1024]{1,0:T(4,128)S(1)} all-reduce(f32[4,1024]{1,0:T(4,128)S(1)} %get-tuple-element.517), channel_id=1, replica_groups=mesh['dp'=8,'tensor'=4] {'tensor'}, use_global_device_ids=true, to_apply=%region_6.7 | all-reduce | flops 4096 | bytes 32768 | tf_op jit(solution)/shard_map/psum | solution.py:309
  350.3 11.5 %multiply_reduce_fusion.2 = (f32[384]{0:T(512)}, f32[4,1024]{1,0:T(4,128)S(1)}, f32[4,1024,384]{1,2,0:T(8,128)}) fusion(f32[4,1024,384]{1,2,0:T(8,128)} %get-tuple-element.518, f32[4,1024]{1,0:T(4,128)S(1)} %get-tuple-element.549, f32[384]{0:T(512)S(1)} %copy-done.94, bf16[4,1024,768]{2,1,0:T(8,128)(2,1)} %all-gather.6.cloned.1.call-done, ...), kind=kOutput, calls=%fused_computation.53 | convolution fusion | flops 2425351680 | bytes 19500032 | tf_op jit(solution)/shard_map/dot_general | solution.py:326
  361.9 10.5 %psum.85 = f32[4,1024]{1,0:T(4,128)S(1)} all-reduce(f32[4,1024]{1,0:T(4,128)S(1)} %get-tuple-element.459), channel_id=1, replica_groups=mesh['dp'=8,'tensor'=4] {'tensor'}, use_global_device_ids=true, to_apply=%region_9.10 | all-reduce | flops 4096 | bytes 32768 | tf_op jit(solution)/shard_map/psum | solution.py:331
  372.4 14.9 %multiply_reduce_fusion.3 = (f32[384]{0:T(512)}, bf16[4,1024,384]{1,2,0:T(8,128)(2,1)S(1)}, bf16[4,1024,384]{1,2,0:T(8,128)(2,1)}) fusion(bf16[4,1024,384]{1,2,0:T(8,128)(2,1)S(1)} %copy-done.3, f32[4,1024,1030]{1,2,0:T(8,128)} %copy-done.1, f32[4,1024]{1,0:T(4,128)S(1)} %broadcast_multiply_fusion.1, f32[4,1024,384]{1,2,0:T(8,128)} %get-tuple-element.518, ...), kind=kLoop, calls=%fused_computation.54 | loop fusion | flops 36175488 | bytes 34655232 | tf_op jit(solution)/shard_map/reduce_sum | solution.py:166
  387.3 4.2 copy.523
  391.5 4.6 reshape.585
  396.1 6.0 fusion.15
  402.4 24.0 %fusion.1 = (f32[16,6,256]{2,1,0:T(8,128)}, f32[16,6,256]{2,1,0:T(8,128)}, f32[16,6,256]{2,1,0:T(8,128)}, bf16[16,256,256]{2,1,0:T(8,128)(2,1)}) fusion(f32[16,6,256]{2,1,0:T(8,128)S(1)} %copy-done.56, f32[16,6,256]{2,1,0:T(8,128)S(1)} %copy-done.54, f32[16,256,256]{2,1,0:T(8,128)S(1)} %copy-done.25, pred[16,256,256]{2,1,0:T(8,128)(4,1)S(1)} %copy-done.41, ...), kind=kOutput, calls=%fused_computation.15 | convolution fusion | flops 885972992 | bytes 14123008 | tf_op jit(solution)/shard_map/cqhp,ckhp->chqk/dot_general | solution.py:175
  426.4 11.0 %fusion.7 = f32[16,6,64,256]{3,2,1,0:T(8,128)} fusion(f32[16,6,256]{2,1,0:T(8,128)S(1)} %copy-done.56, f32[16,6,256]{2,1,0:T(8,128)S(1)} %copy-done.54, f32[16,256,256]{2,1,0:T(8,128)S(1)} %copy-done.25, pred[16,256,256]{2,1,0:T(8,128)(4,1)S(1)} %copy-done.41, bf16[16,256,6,64]{1,0,3,2:T(8,128)(2,1)S(1)} %reshape.585), kind=kOutput, calls=%fused_computation.26 | convolution fusion | flops 843055104 | bytes 14876672 | tf_op jit(solution)/shard_map/chqk,cqhp->ckhp/dot_general | solution.py:176
  444.8 4.2 fusion.103
  449.0 2.9 fusion.43
  451.9 5.9 copy.526
  459.4 14.9 %while.33 = (s32[]{:T(128)}, f32[4,6,128,64]{3,2,1,0:T(8,128)S(1)}, bf16[4,4,6,128,64]{3,4,2,0,1:T(8,128)(2,1)}, f32[4,4,6]{2,1,0:T(4,128)S(1)}, f32[4,4,6,128,6...) while((s32[]{:T(128)}, f32[4,6,128,64]{3,2,1,0:T(8,128)S(1)}, ...), condition=%wide.region_12.13_spmd.clone, body=%wide.region_10.12_spmd.clone.sunk | while | flops 1179628 | bytes 5902868 | solution.py:200
  474.3 7.3 fusion.4
  481.6 9.0 %fusion.17 = f32[16,256,6,64]{1,3,2,0:T(8,128)} fusion(f32[16,6,64,256]{3,2,1,0:T(8,128)} %fusion.7, f32[6]{0:T(128)S(1)} %copy-done.109, bf16[16,6,128,64]{2,3,1,0:T(8,128)(2,1)S(1)} %bitcast.222, f32[16,256,128]{1,2,0:T(8,128)S(1)} %copy-done.15, f32[16,256,6]{1,2,0:T(8,128)S(1)} %copy.511, bf16[16,256,6,64]{1,0,3,2:T(8,128)(2,1)S(1)} %copy-done.5), kind=kOutput, calls=%fused_computation.45 | convolution fusion | flops 415236096 | bytes 19496984 | tf_op jit(solution)/shard_map/cqhn,chnp->cqhp/dot_general | solution.py:213
  495.2 2.4 copy.559
  497.6 4.4 copy.560
  502.0 9.0 %copy.530 = f32[16,256,6,64]{1,0,3,2:T(8,128)} copy(f32[16,256,6,64]{1,3,2,0:T(8,128)} %fusion.17) | data formatting | bytes 12582912 | tf_op jit(solution)/shard_map/add | solution.py:213
  511.0 8.2 %reshape.587 = f32[4,1024,384]{1,0,2:T(4,128)} reshape(f32[16,256,6,64]{1,0,3,2:T(8,128)} %copy.530) | data formatting | bytes 12582912 | tf_op jit(solution)/shard_map/reshape | solution.py:344
  526.2 3.4 reduce-window.16
  530.3 15.8 %multiply_reduce_fusion.7 = (f32[384]{0:T(512)S(1)}, f32[384]{0:T(512)S(1)}, f32[384]{0:T(512)S(1)}, f32[384]{0:T(512)}, f32[384]{0:T(512)S(1)}, /*index=5*/f32[4,1024,384]{1,2,0:T(8,128)S(1)}) fusion(f32[4,1024,384]{1,2,0:T(8,128)} %slice.164, f32[4,1024]{1,0:T(4,128)S(1)} %copy-done.48, f32[4,1024]{1,0:T(4,128)S(1)} %copy-done.45, ...), kind=kLoop, calls=%fused_computation.58 | loop fusion | flops 33028224 | bytes 31514112 | tf_op jit(solution)/shard_map/transpose(jvp())/reduce_sum | solution.py:35
  546.1 4.3 multiply_multiply_fusion.1
  552.2 8.9 %fusion.14 = bf16[4,1024,384]{1,2,0:T(8,128)(2,1)} fusion(f32[4,1024,384]{1,2,0:T(8,128)} %get-tuple-element.530, f32[4,1024,384]{1,2,0:T(8,128)S(1)} %get-tuple-element.529, f32[4,1024,384]{1,2,0:T(8,128)S(1)} %get-tuple-element.528, f32[4,1024,384]{1,2,0:T(8,128)S(1)} %get-tuple-element.516, f32[384]{0:T(512)S(1)} %copy-done.78), kind=kLoop, calls=%fused_computation.42 | loop fusion | flops 7864320 | bytes 28313088 | tf_op jit(solution)/shard_map/convert.9
  561.1 10.4 %convolution_convert_fusion = bf16[4,1024,768]{2,1,0:T(8,128)(2,1)} fusion(bf16[4,1024,6]{1,2,0:T(8,128)(2,1)S(1)} %get-tuple-element.514, bf16[4,1024,384]{1,2,0:T(8,128)(2,1)} %fusion.14, bf16[4,1024,384]{1,2,0:T(8,128)(2,1)S(1)} %copy-done.26, bf16[768,6]{0,1:T(8,128)(2,1)S(1)} %copy-done.63, bf16[768,384]{0,1:T(8,128)(2,1)S(1)} %copy-done.33, ...), kind=kOutput, calls=%fused_computation.108 | convolution fusion | flops 4895321088 | bytes 13820928 | tf_op jit(solution)/shard_map/dot_general | solution.py:356
  572.2 9.2 %convolution_convert_fusion.1 = bf16[4,1024,768]{2,1,0:T(8,128)(2,1)} fusion(bf16[768,384]{1,0:T(8,128)(2,1)} %all_gather.26, f32[4,1024,384]{1,2,0:T(8,128)} %get-tuple-element.518, f32[384]{0:T(512)S(1)} %copy-done.95, f32[4,1024]{1,0:T(4,128)S(1)} %copy-done.52), kind=kOutput, calls=%fused_computation.109 | convolution fusion | flops 2423783424 | bytes 13190656 | tf_op jit(solution)/shard_map/dot_general | solution.py:313
  585.0 10.2 %bitcast_convert_fusion = bf16[768,774]{0,1:T(8,128)(2,1)} fusion(bf16[4,1024,768]{2,1,0:T(8,128)(2,1)} %all-gather.4.cloned.1.call-done, bf16[4,1024,6]{1,2,0:T(8,128)(2,1)S(1)} %get-tuple-element.514, bf16[4,1024,384]{1,2,0:T(8,128)(2,1)} %fusion.14, bf16[4,1024,384]{1,2,0:T(8,128)(2,1)S(1)} %copy-done.26), kind=kOutput, calls=%fused_computation.123 | convolution fusion | flops 4889203200 | bytes 13820928 | tf_op jit(solution)/shard_map/dot_general | solution.py:378
  597.0 8.1 %fusion.57 = bf16[768,384]{1,0:T(8,128)(2,1)S(1)} fusion(bf16[4,1024,768]{2,1,0:T(8,128)(2,1)} %all-gather.6.cloned.1.call-done, f32[4,1024,384]{1,2,0:T(8,128)} %get-tuple-element.518, f32[384]{0:T(512)S(1)} %copy-done.95, f32[4,1024]{1,0:T(4,128)S(1)} %copy-done.52), kind=kOutput, calls=%fused_computation.138 | convolution fusion | flops 2420932608 | bytes 13190656 | tf_op jit(solution)/shard_map/dot_general | solution.py:381
  606.9 4.7 all-to-all-start
  618.4 11.1 %multiply_reduce_fusion.13 = (f32[256]{0:T(256)}, f32[256]{0:T(256)}, f32[256]{0:T(256)}, f32[256]{0:T(256)}, f32[256]{0:T(256)}, /*index=5*/f32[4,1024,256]{1,2,0:T(8,128)S(1)}) fusion(f32[4,1024,256]{1,2,0:T(8,128)} %slice.165, f32[4,1024]{1,0:T(4,128)S(1)} %copy-done.49, f32[4,1024]{1,0:T(4,128)S(1)} %copy-done.46, f32[4,1024]{1,0:T(4,128)S(1)} %copy-done.43, ...), kind=kLoop, calls=%fused_computation.97 | loop fusion | flops 23067392 | bytes 18928640 | tf_op jit(solution)/shard_map/transpose(jvp())/reduce_sum | solution.py:35
  631.7 3.2 pad_slice_fusion.8
  634.9 4.2 pad_slice_fusion.6
  639.0 2.4 fusion.67
  645.3 11.4 %all-to-all-done = bf16[8,96,1158]{2,1,0:T(8,128)(2,1)S(1)} async-done(((bf16[8,96,1158]{2,1,0:T(8,128)(2,1)}), bf16[8,96,1158]{2,1,0:T(8,128)(2,1)S(1)}, u32[]{:S(2)}, u32[]{:S(2)}) %all-to-all-start) | async-done | bytes 1778720 | tf_op jit(solution)/shard_map/all_to_all | solution.py:21
  658.5 4.7 fusion.34
  663.3 39.5 %all-reduce.25 = (f32[768]{0:T(1024)}, f32[4,1536]{1,0:T(4,128)S(1)}, f32[1536]{0:T(1024)S(1)}, f32[4,256]{1,0:T(4,128)}, f32[256]{0:T(256)}, /*index=5*/f32[24]...) all-reduce(f32[768]{0:T(1024)S(1)} %get-tuple-element.470, ...), channel_id=1, replica_groups=mesh['dp'=8,'tensor'=4] {'dp','tensor'}, use_global_device_ids=true, to_apply=%region_27.28 | all-reduce | flops 11336 | bytes 90688 | tf_op jit(solution)/shard_map/psum | solution.py:398
  706.5 4.2 fusion.36
  710.7 84.4 %reduce-scatter.8.cloned.1.call-done = f32[24,256]{1,0:T(8,128)} async-done(((f32[768,256]{1,0:T(8,128)}), f32[24,256]{1,0:T(8,128)}) %reduce-scatter.8.cloned.1.call-update) | async-done | bytes 24592 | tf_op jit(solution)/shard_map/reduce_scatter | solution.py:389
  (417 shorter events, 106.4 us)
Async XLA Ops:
  7.2 181.9 %all-gather.4.cloned.1.call-start = ((), (), s32[]{:S(2)}) async-start(), calls=%async_computation.4 | async-start | bytes 7864320 | tf_op jit(solution)/shard_map/all_gather | solution.py:271
  10.3 7.6 copy-start.96
  10.3 9.6 %copy-start.100 = (bf16[96,6]{0,1:T(8,128)(2,1)S(1)}, bf16[96,6]{0,1:T(8,128)(2,1)}, u32[]{:S(2)}) copy-start(bf16[96,6]{0,1:T(8,128)(2,1)} %param.28) | copy-start | bytes 3460
  13.4 35.5 %copy-start.64 = (bf16[96,256]{1,0:T(8,128)(2,1)S(1)}, bf16[96,256]{1,0:T(8,128)(2,1)}, u32[]{:S(2)}) copy-start(bf16[96,256]{1,0:T(8,128)(2,1)} %param.27) | copy-start | bytes 147460
  13.4 67.4 %copy-start.59 = (bf16[96,384]{1,0:T(8,128)(2,1)S(1)}, bf16[96,384]{1,0:T(8,128)(2,1)}, u32[]{:S(2)}) copy-start(bf16[96,384]{1,0:T(8,128)(2,1)} %param.37) | copy-start | bytes 221188
  13.4 101.2 %copy-start.60 = (bf16[96,384]{1,0:T(8,128)(2,1)S(1)}, bf16[96,384]{1,0:T(8,128)(2,1)}, u32[]{:S(2)}) copy-start(bf16[96,384]{1,0:T(8,128)(2,1)} %param.25) | copy-start | bytes 221188
  13.4 336.9 %all-gather.6.cloned.1.call-start = ((), (), s32[]{:S(2)}) async-start(), calls=%async_computation.6 | async-start | bytes 7864320 | tf_op jit(solution)/shard_map/all_gather | solution.py:324
  13.6 67.2 %copy-start.67 = (f32[4,256]{1,0:T(4,128)}, f32[4,256]{1,0:T(4,128)S(1)}, u32[]{:S(2)}) copy-start(f32[4,256]{1,0:T(4,128)S(1)} %compare_convert_fusion.2) | copy-start | bytes 12292
  13.6 132.8 %copy-start.61 = (bf16[96,384]{1,0:T(8,128)(2,1)S(1)}, bf16[96,384]{1,0:T(8,128)(2,1)}, u32[]{:S(2)}) copy-start(bf16[96,384]{1,0:T(8,128)(2,1)} %param.26) | copy-start | bytes 221188
  15.1 602.8 %all-reduce.28.cloned.1.call-start = ((), (), s32[]{:S(2)}) async-start(), calls=%async_computation.8 | async-start | bytes 4194304 | tf_op jit(solution)/shard_map/psum | solution.py:342
  18.5 226.6 %copy-start.77 = (f32[384]{0:T(512)}, f32[384]{0:T(512)S(1)}, u32[]{:S(2)}) copy-start(f32[384]{0:T(512)S(1)} %get-tuple-element.474) | copy-start | bytes 4612
  19.0 28.7 %copy-start.85 = (f32[4,4]{1,0:T(4,128)}, f32[4,4]{1,0:T(4,128)S(1)}, u32[]{:S(2)}) copy-start(f32[4,4]{1,0:T(4,128)S(1)} %pad_convert_fusion) | copy-start | bytes 196
  47.8 141.2 %copy-start.62 = (bf16[768,6]{0,1:T(8,128)(2,1)}, bf16[768,6]{0,1:T(8,128)(2,1)S(1)}, u32[]{:S(2)}) copy-start(bf16[768,6]{0,1:T(8,128)(2,1)S(1)} %reshape.594) | copy-start | bytes 27652
  48.0 197.2 %copy-start.42 = (f32[4,1024]{1,0:T(4,128)}, f32[4,1024]{1,0:T(4,128)S(1)}, u32[]{:S(2)}) copy-start(f32[4,1024]{1,0:T(4,128)S(1)} %get-tuple-element.552) | copy-start | bytes 49156
  48.0 197.2 %copy-start.44 = (f32[4,1024]{1,0:T(4,128)}, f32[4,1024]{1,0:T(4,128)S(1)}, u32[]{:S(2)}) copy-start(f32[4,1024]{1,0:T(4,128)S(1)} %get-tuple-element.553) | copy-start | bytes 49156
  48.0 197.2 %copy-start.47 = (f32[4,1024]{1,0:T(4,128)}, f32[4,1024]{1,0:T(4,128)S(1)}, u32[]{:S(2)}) copy-start(f32[4,1024]{1,0:T(4,128)S(1)} %get-tuple-element.554) | copy-start | bytes 49156
  48.8 174.8 %copy-start.38 = (f32[16,256]{0,1:T(8,128)}, f32[16,256]{0,1:T(8,128)S(1)}, u32[]{:S(2)}) copy-start(f32[16,256]{0,1:T(8,128)S(1)} %copy.510) | copy-start | bytes 49156
  146.4 52.1 %copy-start.30 = (bf16[768,384]{0,1:T(8,128)(2,1)}, bf16[768,384]{0,1:T(8,128)(2,1)S(1)}, u32[]{:S(2)}) copy-start(bf16[768,384]{0,1:T(8,128)(2,1)S(1)} %copy.489) | copy-start | bytes 1769476
  178.1 20.4 %copy-start.32 = (bf16[768,384]{0,1:T(8,128)(2,1)}, bf16[768,384]{0,1:T(8,128)(2,1)S(1)}, u32[]{:S(2)}) copy-start(bf16[768,384]{0,1:T(8,128)(2,1)S(1)} %copy.490) | copy-start | bytes 1769476
  189.0 15.3 %copy-start.102 = (f32[6]{0:T(128)S(1)}, f32[6]{0:T(128)}, u32[]{:S(2)}) copy-start(f32[6]{0:T(128)} %param.33) | copy-start | bytes 76
  189.0 15.3 %copy-start.104 = (f32[6]{0:T(128)S(1)}, f32[6]{0:T(128)}, u32[]{:S(2)}) copy-start(f32[6]{0:T(128)} %exponential_negate_fusion) | copy-start | bytes 76
  204.5 17.0 %copy-start.36 = (f32[4,1024,6]{1,2,0:T(8,128)}, f32[4,1024,6]{1,2,0:T(8,128)S(1)}, u32[]{:S(2)}) copy-start(f32[4,1024,6]{1,2,0:T(8,128)S(1)} %get-tuple-element.522) | copy-start | bytes 294916
  209.4 14.2 %copy-start.16 = (f32[16,6,256]{0,2,1:T(8,128)}, f32[16,6,256]{0,2,1:T(8,128)S(1)}, u32[]{:S(2)}) copy-start(f32[16,6,256]{0,2,1:T(8,128)S(1)} %copy.505) | copy-start | bytes 294916
  214.9 8.7 %copy-start.86 = (f32[4,4]{1,0:T(4,128)S(1)}, f32[4,4]{1,0:T(4,128)}, u32[]{:S(2)}) copy-start(f32[4,4]{1,0:T(4,128)} %copy-done.85) | copy-start | bytes 196
  223.5 14.1 %copy-start.71 = (f32[16,1,6]{0,2,1:T(8,128)}, f32[16,1,6]{0,2,1:T(8,128)S(1)}, u32[]{:S(2)}) copy-start(f32[16,1,6]{0,2,1:T(8,128)S(1)} %copy.696) | copy-start | bytes 1156
  226.0 11.6 %copy-start.12 = (f32[16,256,6]{0,1,2:T(8,128)}, f32[16,256,6]{0,1,2:T(8,128)S(1)}, u32[]{:S(2)}) copy-start(f32[16,256,6]{0,1,2:T(8,128)S(1)} %get-tuple-element.541) | copy-start | bytes 294916
  240.8 59.9 %copy-start.7 = (bf16[4,1024,128]{2,1,0:T(8,128)(2,1)}, bf16[4,1024,128]{2,1,0:T(8,128)(2,1)S(1)}, u32[]{:S(2)}) copy-start(bf16[4,1024,128]{2,1,0:T(8,128)(2,1)S(1)} %copy.494) | copy-start | bytes 3145732
  303.1 14.6 %copy-start.6 = (f32[16,256,384]{1,2,0}, f32[16,256,384]{1,2,0:S(1)}, u32[]{:S(2)}) copy-start(f32[16,256,384]{1,2,0:S(1)} %fusion.102) | copy-start | bytes 18874372
  332.1 18.2 %copy-start.94 = (f32[384]{0:T(512)S(1)}, f32[384]{0:T(512)}, u32[]{:S(2)}) copy-start(f32[384]{0:T(512)} %param.36) | copy-start | bytes 4612
  350.3 22.1 %copy-start.51 = (f32[4,1024]{1,0:T(4,128)}, f32[4,1024]{1,0:T(4,128)S(1)}, u32[]{:S(2)}) copy-start(f32[4,1024]{1,0:T(4,128)S(1)} %get-tuple-element.549) | copy-start | bytes 49156
  350.3 22.1 %copy-start.3 = (bf16[4,1024,384]{1,2,0:T(8,128)(2,1)S(1)}, bf16[4,1024,384]{1,2,0:T(8,128)(2,1)}, u32[]{:S(2)}) copy-start(bf16[4,1024,384]{1,2,0:T(8,128)(2,1)} %copy-done.2) | copy-start | bytes 9437188
  396.1 52.9 %copy-start.4 = (bf16[16,256,6,64]{1,0,3,2:T(8,128)(2,1)}, bf16[16,256,6,64]{1,0,3,2:T(8,128)(2,1)S(1)}, u32[]{:S(2)}) copy-start(bf16[16,256,6,64]{1,0,3,2:T(8,128)(2,1)S(1)} %reshape.585) | copy-start | bytes 9437188
  451.9 7.5 copy-start
  474.3 7.3 copy-start.5
  474.3 7.3 copy-start.15
  481.6 9.0 %copy-start.10 = (bf16[4,1024,128]{2,1,0:T(8,128)(2,1)S(1)}, bf16[4,1024,128]{2,1,0:T(8,128)(2,1)}, u32[]{:S(2)}) copy-start(bf16[4,1024,128]{2,1,0:T(8,128)(2,1)} %copy.493) | copy-start | bytes 3145732
  481.6 9.0 %copy-start.14 = (bf16[16,256,256]{2,1,0:T(8,128)(2,1)S(1)}, bf16[16,256,256]{2,1,0:T(8,128)(2,1)}, u32[]{:S(2)}) copy-start(bf16[16,256,256]{2,1,0:T(8,128)(2,1)} %get-tuple-element.457) | copy-start | bytes 6291460
  511.0 8.7 %copy-start.13 = (f32[16,256,6]{0,1,2:T(8,128)S(1)}, f32[16,256,6]{0,1,2:T(8,128)}, u32[]{:S(2)}) copy-start(f32[16,256,6]{0,1,2:T(8,128)} %copy-done.12) | copy-start | bytes 294916
  511.0 8.7 %copy-start.17 = (f32[16,6,256]{0,2,1:T(8,128)S(1)}, f32[16,6,256]{0,2,1:T(8,128)}, u32[]{:S(2)}) copy-start(f32[16,6,256]{0,2,1:T(8,128)} %copy-done.16) | copy-start | bytes 294916
  511.0 8.7 %copy-start.39 = (f32[16,256]{0,1:T(8,128)S(1)}, f32[16,256]{0,1:T(8,128)}, u32[]{:S(2)}) copy-start(f32[16,256]{0,1:T(8,128)} %copy-done.38) | copy-start | bytes 49156
  511.0 8.7 %copy-start.72 = (f32[16,1,6]{0,2,1:T(8,128)S(1)}, f32[16,1,6]{0,2,1:T(8,128)}, u32[]{:S(2)}) copy-start(f32[16,1,6]{0,2,1:T(8,128)} %copy-done.71) | copy-start | bytes 1156
  519.3 139.2 %reduce-scatter.6.cloned.1.call-start = ((), (), s32[]{:S(2)}) async-start(), calls=%async_computation.7 | async-start | bytes 7864320 | tf_op jit(solution)/shard_map/reduce_scatter | solution.py:359
  530.3 15.8 %copy-start.80 = (f32[384]{0:T(512)S(1)}, f32[384]{0:T(512)}, u32[]{:S(2)}) copy-start(f32[384]{0:T(512)} %get-tuple-element.475) | copy-start | bytes 4612
  530.3 15.8 %copy-start.82 = (f32[384]{0:T(512)S(1)}, f32[384]{0:T(512)}, u32[]{:S(2)}) copy-start(f32[384]{0:T(512)} %get-tuple-element.476) | copy-start | bytes 4612
  530.3 15.8 %copy-start.84 = (f32[384]{0:T(512)S(1)}, f32[384]{0:T(512)}, u32[]{:S(2)}) copy-start(f32[384]{0:T(512)} %get-tuple-element.477) | copy-start | bytes 4612
  552.2 8.9 %copy-start.26 = (bf16[4,1024,384]{1,2,0:T(8,128)(2,1)S(1)}, bf16[4,1024,384]{1,2,0:T(8,128)(2,1)}, u32[]{:S(2)}) copy-start(bf16[4,1024,384]{1,2,0:T(8,128)(2,1)} %get-tuple-element.527) | copy-start | bytes 9437188
  552.2 8.9 %copy-start.31 = (bf16[768,384]{0,1:T(8,128)(2,1)S(1)}, bf16[768,384]{0,1:T(8,128)(2,1)}, u32[]{:S(2)}) copy-start(bf16[768,384]{0,1:T(8,128)(2,1)} %copy-done.30) | copy-start | bytes 1769476
  552.2 8.9 %copy-start.33 = (bf16[768,384]{0,1:T(8,128)(2,1)S(1)}, bf16[768,384]{0,1:T(8,128)(2,1)}, u32[]{:S(2)}) copy-start(bf16[768,384]{0,1:T(8,128)(2,1)} %copy-done.32) | copy-start | bytes 1769476
  552.2 8.9 %copy-start.63 = (bf16[768,6]{0,1:T(8,128)(2,1)S(1)}, bf16[768,6]{0,1:T(8,128)(2,1)}, u32[]{:S(2)}) copy-start(bf16[768,6]{0,1:T(8,128)(2,1)} %copy-done.62) | copy-start | bytes 27652
  571.5 134.9 %reduce-scatter.4.cloned.1.call-start = ((), (), s32[]{:S(2)}) async-start(), calls=%async_computation.5 | async-start | bytes 7864320 | tf_op jit(solution)/shard_map/reduce_scatter | solution.py:316
  605.2 13.2 %copy-start.46 = (f32[4,1024]{1,0:T(4,128)S(1)}, f32[4,1024]{1,0:T(4,128)}, u32[]{:S(2)}) copy-start(f32[4,1024]{1,0:T(4,128)} %copy-done.44) | copy-start | bytes 49156
  605.2 13.2 %copy-start.49 = (f32[4,1024]{1,0:T(4,128)S(1)}, f32[4,1024]{1,0:T(4,128)}, u32[]{:S(2)}) copy-start(f32[4,1024]{1,0:T(4,128)} %copy-done.47) | copy-start | bytes 49156
  606.9 49.8 %all-to-all-start = ((bf16[8,96,1158]{2,1,0:T(8,128)(2,1)}), bf16[8,96,1158]{2,1,0:T(8,128)(2,1)S(1)}, u32[]{:S(2)}, u32[]{:S(2)}) async-start(bf16[8,96,1158]{2,1,0:T(8,128)(2,1)} %pad_maximum_fusion.4), calls=%async_computation.2 | async-start | bytes 3932160 | tf_op jit(solution)/shard_map/all_to_all | solution.py:21
  611.6 183.6 %reduce-scatter.8.cloned.1.call-start = ((), (), s32[]{:S(2)}) async-start(), calls=%async_computation.9 | async-start | bytes 811008 | tf_op jit(solution)/shard_map/reduce_scatter | solution.py:389
  617.1 12.4 %copy-start.57 = (f32[4,1536]{1,0:T(4,128)}, f32[4,1536]{1,0:T(4,128)S(1)}, u32[]{:S(2)}) copy-start(f32[4,1536]{1,0:T(4,128)S(1)} %add_dynamic-update-slice_fusion) | copy-start | bytes 73732
  618.4 11.1 %copy-start.90 = (f32[1,256]{1,0:T(1,128)S(1)}, f32[1,256]{1,0:T(1,128)}, u32[]{:S(2)}) copy-start(f32[1,256]{1,0:T(1,128)} %get-tuple-element.556) | copy-start | bytes 3076
  618.4 11.1 %copy-start.91 = (f32[1,256]{1,0:T(1,128)S(1)}, f32[1,256]{1,0:T(1,128)}, u32[]{:S(2)}) copy-start(f32[1,256]{1,0:T(1,128)} %get-tuple-element.557) | copy-start | bytes 3076
  618.4 11.1 %copy-start.92 = (f32[1,256]{1,0:T(1,128)S(1)}, f32[1,256]{1,0:T(1,128)}, u32[]{:S(2)}) copy-start(f32[1,256]{1,0:T(1,128)} %get-tuple-element.558) | copy-start | bytes 3076
  642.3 16.2 %copy-start.11 = (bf16[4,256,768]{2,1,0:T(8,128)(2,1)S(1)}, bf16[4,256,768]{2,1,0:T(8,128)(2,1)}, u32[]{:S(2)}) copy-start(bf16[4,256,768]{2,1,0:T(8,128)(2,1)} %param.21) | copy-start | bytes 4718596
  642.3 16.2 %copy-start.66 = (f32[4,256]{1,0:T(4,128)S(1)}, f32[4,256]{1,0:T(4,128)}, u32[]{:S(2)}) copy-start(f32[4,256]{1,0:T(4,128)} %copy-done.65) | copy-start | bytes 12292
  642.3 16.2 %copy-start.87 = (f32[768]{0:T(1024)S(1)}, f32[768]{0:T(1024)}, u32[]{:S(2)}) copy-start(f32[768]{0:T(1024)} %param.24) | copy-start | bytes 9220
  657.8 48.6 %copy-start.70 = (f32[4,256]{1,0:T(4,128)S(1)}, f32[4,256]{1,0:T(4,128)}, u32[]{:S(2)}) copy-start(f32[4,256]{1,0:T(4,128)} %copy-done.69) | copy-start | bytes 12292
  657.8 48.7 %copy-start.21 = (bf16[4,256,768]{2,1,0:T(8,128)(2,1)S(1)}, bf16[4,256,768]{2,1,0:T(8,128)(2,1)}, u32[]{:S(2)}) copy-start(bf16[4,256,768]{2,1,0:T(8,128)(2,1)} %param.23) | copy-start | bytes 4718596
  657.8 48.7 %copy-start.68 = (f32[4,256]{1,0:T(4,128)S(1)}, f32[4,256]{1,0:T(4,128)}, u32[]{:S(2)}) copy-start(f32[4,256]{1,0:T(4,128)} %copy-done.67) | copy-start | bytes 12292
  (58 other events, 250.9 us)
Sparse Core Ops, SparseCore 0:
  13.5 49.0 all-gather.3
  64.2 46.3 all-gather.5
  519.5 51.1 all-reduce.27
  573.2 58.4 reduce-scatter.5
  634.0 59.1 reduce-scatter.3
  699.6 95.5 reduce-scatter.7
where the time goes:
time: 807 us; the launch traced here: 802 us
  blocking collectives  216 us (27%)
  local copies, waits for them, and re-layouts  168 us (21%)
  other arithmetic  157 us (19%)
  matrix products  145 us (18%)
  waiting for transfers between devices  96 us (12%)
  between operations  15.7 us (2%)
    reduce_scatter x1, waiting for transfers between devices, per_device(): lax.psum_scatter(lax.dot_general(columns, own_state, (((0,), (0,)), ((),...  84.4 us
    psum x1, blocking collectives, per_device(): lax.psum((spread_cols(conv_x_grad, tensor_slot, tensor_count), spread_col...  39.5 us
    all_gather x1, blocking collectives, per_device(): lax.all_gather(w_out, 'dp', axis=0, tiled=True)  33.8 us
    all_gather x1, blocking collectives, per_device(): lax.all_gather(w_z, 'dp', axis=0, tiled=True)  31.5 us
    all_gather x1, blocking collectives, per_device(): lax.all_gather(w_x, 'dp', axis=0, tiled=True)  31.5 us
    all_gather x1, blocking collectives, per_device(): lax.all_gather(w_bc, 'dp', axis=0, tiled=True)  31 us
    all_gather x1, blocking collectives, per_device(): lax.all_gather(w_dt, 'dp', axis=0, tiled=True)  27.8 us
    reduce_sum x2, other arithmetic, causal_conv(): conv_sum = conv_sum + weight[offset] * shifted * keep_mask  26.9 us
  transfers between devices with their start and end apart: 7, of which 2 were waited for; matrix products, arithmetic and copies ran while one was open for 36% of the time, Pallas kernels for 0%

commit v1 on v0

v1 whole, which is shorter than its diff:
```python
import functools

import jax
import jax.numpy as jnp
from jax import lax
from jax.experimental import pallas as pl
from jax.experimental.pallas import tpu as pltpu
from jax.sharding import PartitionSpec as P

INNER = 1536
L = 256
HD = 64
SPAN = 32
EPS = 1e-05
LOG2E = 1.4426950408889634
F32 = jnp.float32
BF = jnp.bfloat16
VMEM_LIMIT = 56 * 1024 * 1024


def dot(a, b):
    return jnp.dot(a, b, preferred_element_type=F32)


def dot_nt(a, b):
    return lax.dot_general(a, b, (((1,), (1,)), ((), ())), preferred_element_type=F32)


def dot_high(a, b):
    return jnp.dot(a, b, preferred_element_type=F32, precision=lax.Precision.HIGHEST)


def sigmoid(v):
    return 0.5 * jnp.tanh(0.5 * v) + 0.5


def lane_iota(rows):
    return lax.broadcasted_iota(jnp.int32, (rows, 128), 1)


def row_iota(rows, lanes):
    return lax.broadcasted_iota(jnp.int32, (rows, lanes), 0)


def seg_of(idx, fe, se):
    return (idx >= fe).astype(jnp.int32) + (idx >= se).astype(jnp.int32)


def ends(sc, s):
    return sc[2 * s], sc[2 * s + 1]


def cross_mask(rows, k, fe, se):
    idx = row_iota(rows, 1)
    cut = ((idx >= fe) & (idx - k < fe)) | ((idx >= se) & (idx - k < se))
    return jnp.where(cut, 0.0, 1.0).astype(F32)


def pair_cols(cols, first):
    lane = lane_iota(cols.shape[0])
    left = jnp.broadcast_to(cols[:, first : first + 1], cols.shape)
    right = jnp.broadcast_to(cols[:, first + 1 : first + 2], cols.shape)
    return jnp.where(lane < HD, left, right)


def group_cols(cols):
    return jnp.concatenate([pair_cols(cols, 2 * p) for p in range(3)], axis=1)


def head_sum_matrix(offset, rows=384):
    r = lax.broadcasted_iota(jnp.int32, (rows, 128), 0)
    c = lax.broadcasted_iota(jnp.int32, (rows, 128), 1)
    return jnp.where(c == offset + r // HD, 1.0, 0.0)


def to_lane0(packed, s, i):
    return pltpu.roll(packed, (256 - s * SPAN - i * 6) % 128, 1)


def rows_of(s, length=L):
    return pl.ds(pl.multiple_of(s * length, length), length)


def conv_forward(v, h, taps, bias, fe, se):
    ext = jnp.concatenate([h, v], axis=0)
    acc = bias + taps[0] * v
    for k in range(1, 4):
        acc = acc + (taps[k] * pltpu.roll(ext, k, 0)[8:]) * cross_mask(L, k, fe, se)
    return acc


def conv_backward(dconv, v_ext, taps, fe, se):
    zeros = jnp.zeros((8, dconv.shape[1]), F32)
    out, tap_grads = None, []
    for k in range(4):
        part = dconv if k == 0 else dconv * cross_mask(L, k, fe, se)
        ext = jnp.concatenate([zeros, part], axis=0)
        if k:
            ext = pltpu.roll(ext, ext.shape[0] - k, 0)
        tap_grads.append(jnp.sum(ext * v_ext, axis=0, keepdims=True))
        out = taps[k] * ext if out is None else out + taps[k] * ext
    return out, tap_grads


def assemble(dst, blocks, me, at):
    count, rows, width = blocks.shape[1:]
    for n in range(count):
        start = pl.multiple_of((n ^ me) * rows, rows) if count > 1 else 0
        dst[pl.ds(start, rows), at : at + width] = blocks[0, n]


def assemble_either(dst, i, me, mine, other):
    @pl.when(i % 2 == 0)
    def _():
        for blocks, at in mine:
            assemble(dst, blocks, me, at)

    @pl.when(i % 2 == 1)
    def _():
        for blocks, at in other:
            assemble(dst, blocks, me, at)


def k1_body(
    sc, tok, halo, gain, wam, war, wbm, wbr, par, cbc, bbc,
    nrm, xo, dslo, inno, sto, blow, clow, sin, dbc, pk, ct,
    wbuf, innx, dtacc, bt,
):
    ph = pl.program_id(0)
    i = pl.program_id(1)
    me_t, me_dp = sc[8], sc[9]
    t = i ^ me_t

    @pl.when((ph == 0) & (i == 0))
    def _():
        def norm(v):
            v = v.astype(F32)
            r = lax.rsqrt(jnp.mean(v * v, axis=-1, keepdims=True) + EPS)
            return (v * r * gain[...]).astype(BF)

        @pl.loop(0, 4)
        def _(s):
            nrm[rows_of(s)] = norm(tok[rows_of(s)])

        nrm[4 * L :] = norm(halo[...])
        dtacc[...] = jnp.zeros_like(dtacc)
        sin[...] = jnp.zeros_like(sin)

    @pl.when(ph == 0)
    def _():
        assemble_either(wbuf, i, me_dp, [(wam, 0), (wbm, 256)], [(war, 0), (wbr, 256)])
        turn = 64 * (t % 2)

        @pl.loop(0, 4)
        def _(s):
            p = dot(nrm[rows_of(s)], wbuf[...])
            innx[i, rows_of(s)] = p[:, :384]
            last = p[:, 384:]
            lane = lane_iota(L)
            sin[t // 2, rows_of(s)] += pltpu.roll(jnp.where(lane < 64, last, 0.0), turn, 1)
            dtacc[...] += pltpu.roll(
                jnp.where(lane >= 64, last, 0.0), (s * SPAN + i * 6 + 64) % 128, 1
            )

        p = dot(nrm[4 * L :], wbuf[...])
        innx[i, 4 * L :] = p[:, :384]
        sin[t // 2, 4 * L :] += pltpu.roll(jnp.where(lane_iota(64) < 64, p[:, 384:], 0.0), turn, 1)

    @pl.when((ph == 0) & (i == 3))
    def _():
        for q, low_out in ((0, blow), (1, clow)):
            cols = slice(128 * q, 128 * q + 128)
            taps = [cbc[k : k + 1, cols] for k in range(4)]

            @pl.loop(0, 4)
            def _(s):
                fe, se = sc[2 * s], sc[2 * s + 1]
                h = sin[q, pl.ds(pl.multiple_of(4 * L + 16 * s + 8, 8), 8)]
                acc = conv_forward(sin[q, rows_of(s)], h, taps, bbc[:, cols], fe, se)
                sg = sigmoid(acc)
                low = (acc * sg).astype(BF)
                low_out[rows_of(s)] = low
                dbc[q, rows_of(s)] = sg * (1.0 + acc * (1.0 - sg))
                if q == 0:
                    bt[s] = (acc * sg).T.astype(BF)

        dtb = jnp.zeros((1, 128), F32)
        alog = jnp.zeros((1, 128), F32)
        for g in range(4):
            for s in range(4):
                dtb += pltpu.roll(par[g, 6:7, :128], s * SPAN + g * 6, 1)
                alog += pltpu.roll(par[g, 7:8, :128], s * SPAN + g * 6, 1)
        raw = dtacc[...] + dtb
        step = jnp.maximum(raw, 0.0) + jnp.log1p(jnp.exp(-jnp.abs(raw)))
        sig = 1.0 / (1.0 + jnp.exp(-raw))
        decay = step * -jnp.exp(alog)
        lower = jnp.where(
            lax.broadcasted_iota(jnp.int32, (L, L), 0) >= lax.broadcasted_iota(jnp.int32, (L, L), 1),
            1.0,
            0.0,
        )
        cum = dot_high(lower, decay)
        row = row_iota(L, 128)
        slot = lane_iota(L) // SPAN
        tail = jnp.zeros((L, 128), F32)
        enters = jnp.zeros((L, 128), F32)
        follows = jnp.zeros((8, 128), F32)
        slot8 = lane_iota(8) // SPAN
        inner_block = jnp.where(me_t > 0, 1.0, 0.0)
        for s in range(4):
            fe, se = ends(sc, s)
            seg = seg_of(row, fe, se)
            last = seg_of(L - 1, fe, se)
            before = seg_of(-1, fe, se)
            here = slot == s
            tail = jnp.where(here & (seg == last), 1.0, tail)
            enters = jnp.where(here & (seg == before), inner_block, enters)
            follows = jnp.where(
                (slot8 == s), jnp.where(last == before, inner_block, 0.0), follows
            )
        cum_last = cum[L - 1 : L]
        cum2 = cum * LOG2E
        pk[0] = cum2
        pk[1] = step
        pk[2] = sig
        pk[3] = jnp.exp(cum_last - cum) * step * tail
        pk[4] = jnp.exp(cum) * enters
        pk[5] = decay
        pk[6] = jnp.broadcast_to(jnp.exp(cum_last) * follows[0:1], (L, 128))
        ct[...] = cum2.T

    @pl.when(ph == 1)
    def _():
        taps = [par[i, k : k + 1] for k in range(4)]
        bias = par[i, 4:5]

        @pl.loop(0, 4)
        def _(s):
            fe, se = sc[2 * s], sc[2 * s + 1]
            v = innx[i, rows_of(s)]
            h = innx[i, pl.ds(pl.multiple_of(4 * L + 16 * s + 8, 8), 8)]
            acc = conv_forward(v, h, taps, bias, fe, se)
            sg = sigmoid(acc)
            low = (acc * sg).astype(BF)
            xo[0, rows_of(s)] = low
            dslo[0, rows_of(s)] = (sg * (1.0 + acc * (1.0 - sg))).astype(BF)
            inno[0, rows_of(s)] = v.astype(BF)
            te = group_cols(to_lane0(pk[3], s, i))
            xs = (low.astype(F32) * te).astype(BF)
            sto[rows_of(s, 128)] = dot(bt[s], xs).astype(BF)

        inno[0, 4 * L :] = innx[i, 4 * L :].astype(BF)
        high, rest = [], []
        for s in range(4):
            f = group_cols(to_lane0(pk[6, 0:8], s, i))[0:1]
            high.append(f)
        f = jnp.concatenate(high, axis=0)
        fh = f.astype(BF).astype(F32)
        sto[512:528] = jnp.concatenate([fh, f - fh, jnp.zeros((8, 384), F32)], axis=0).astype(BF)


def k2_body(sc, nrm, wm, wr, x, blow, clow, pk, ct, gate, within, wbuf, scores):
    i = pl.program_id(0)
    me_dp = sc[9]
    assemble_either(wbuf, i, me_dp, [(wm, 0)], [(wr, 0)])

    @pl.when(i == 0)
    def _():
        @pl.loop(0, 4)
        def _(s):
            fe, se = sc[2 * s], sc[2 * s + 1]
            q = lax.broadcasted_iota(jnp.int32, (L, L), 0)
            k = lax.broadcasted_iota(jnp.int32, (L, L), 1)
            same = (q >= k) & (seg_of(q, fe, se) == seg_of(k, fe, se))
            scores[s] = jnp.where(same, dot_nt(clow[rows_of(s)], blow[rows_of(s)]), 0.0)

    @pl.loop(0, 4)
    def _(s):
        gate[0, rows_of(s)] = dot(nrm[rows_of(s)], wbuf[...])
        cum = to_lane0(pk[0], s, i)
        step = to_lane0(pk[1], s, i)
        lane = lane_iota(L)
        for p in range(3):
            xs = x[0, rows_of(s), 128 * p : 128 * p + 128].astype(F32) * pair_cols(step, 2 * p)
            top = jnp.zeros((128, 128), F32)
            low = jnp.zeros((128, 128), F32)
            for b in range(2):
                h = 2 * p + b
                half = jnp.where((lane < HD) == (b == 0), xs, 0.0).astype(BF)
                cq = cum[:, h : h + 1]
                ck = ct[pl.ds(s * SPAN + i * 6 + h, 1), :]
                g0 = jnp.minimum(cq[:128] - ck[:, :128], 0.0)
                w0 = (jnp.exp2(g0) * scores[s, :128, :128]).astype(BF)
                g1 = jnp.minimum(cq[128:] - ck, 0.0)
                w1 = (jnp.exp2(g1) * scores[s, 128:, :]).astype(BF)
                top = top + dot(w0, half[:128])
                low = low + dot(w1, half)
            within[0, pl.ds(pl.multiple_of(s * L, L), 128), 128 * p : 128 * p + 128] = top
            within[0, pl.ds(pl.multiple_of(s * L + 128, 128), 128), 128 * p : 128 * p + 128] = low


def k3_body(
    sc, within, gate_in, x, r1, r2, r3, pk, clow, par, wm, wr, tok, cot,
    out, gno, dgo, dyo, dpo, dpk, dco, small,
    mo, gt, scaled, prev, sums, branch, dbr, wbuf, frow,
):
    ph = pl.program_id(0)
    i = pl.program_id(1)
    me_t, me_dp = sc[8], sc[9]

    @pl.when((ph == 0) & (i == 0))
    def _():
        sums[...] = jnp.zeros_like(sums)
        branch[...] = jnp.zeros_like(branch)
        dpk[...] = jnp.zeros_like(dpk)
        dco[...] = jnp.zeros_like(dco)
        small[...] = jnp.zeros_like(small)

        @pl.loop(0, 4)
        def _(s):
            se = sc[2 * s + 1]
            keep = row_iota(L, 1) < se
            dbr[rows_of(s)] = jnp.where(keep, cot[rows_of(s)].astype(F32), 0.0).astype(BF)

    def reach_of(s):
        return group_cols(to_lane0(pk[4], s, i))

    @pl.when(ph == 0)
    def _():
        frow[...] = r1[512:528].astype(F32)

        @pl.loop(0, 4)
        def _(s):
            srow = rows_of(s, 128)
            f = frow[pl.ds(s, 1)] + frow[pl.ds(s + 4, 1)]
            pv = r1[srow].astype(F32) + r2[srow].astype(F32) + f * r3[srow].astype(F32)
            pv = pv.astype(BF)
            prev[i, srow] = pv
            from_prev = dot(clow[rows_of(s)], pv)
            xf = x[0, rows_of(s)].astype(F32)
            mixed = within[0, rows_of(s)] + reach_of(s) * from_prev + par[i, 8:9] * xf
            gv = gate_in[0, rows_of(s)]
            gated = mixed * (gv * sigmoid(gv))
            mo[i, rows_of(s)] = mixed
            gt[i, rows_of(s)] = gv
            sums[0, rows_of(s)] += jnp.sum(gated * gated, axis=1, keepdims=True)

    @pl.when(ph == 1)
    def _():
        assemble_either(wbuf, i, me_dp, [(wm, 0)], [(wr, 0)])
        gain = par[i, 5:6]

        @pl.loop(0, 4)
        def _(s):
            r = rows_of(s)
            gscale = lax.rsqrt(sums[0, r, 0:1] * (1.0 / INNER) + EPS)
            gv = gt[i, r]
            gated = mo[i, r] * (gv * sigmoid(gv))
            gs = gated * gscale
            gn = (gs * gain).astype(BF)
            gno[0, r] = gn
            branch[r] += dot_nt(gn, wbuf[...])
            dgn = dot(dbr[r], wbuf[...])
            small[i, 0:1] += jnp.sum(dgn * gs, axis=0, keepdims=True)
            sv = dgn * gain
            scaled[i, r] = sv
            sums[1, r] += jnp.sum(sv * gated, axis=1, keepdims=True)

    @pl.when((ph == 1) & (i == 3))
    def _():
        @pl.loop(0, 4)
        def _(s):
            r = rows_of(s)
            out[r] = (tok[r].astype(F32) + branch[r]).astype(BF)

    @pl.when(ph == 2)
    def _():
        @pl.loop(0, 4)
        def _(s):
            r = rows_of(s)
            srow = rows_of(s, 128)
            gscale = lax.rsqrt(sums[0, r, 0:1] * (1.0 / INNER) + EPS)
            coef = gscale * gscale * gscale * (sums[1, r, 0:1] * (1.0 / INNER))
            gv = gt[i, r]
            mixed = mo[i, r]
            sg = sigmoid(gv)
            silu = gv * sg
            dgated = gscale * scaled[i, r] - (mixed * silu) * coef
            dgo[0, r] = (dgated * mixed * (sg * (1.0 + gv * (1.0 - sg)))).astype(BF)
            dy = (dgated * silu).astype(BF)
            dyo[0, r] = dy
            dyf = dy.astype(F32)
            dprev = dyf * reach_of(s)
            dlow = dprev.astype(BF)
            pv = prev[i, srow]
            cs = clow[r]
            from_prev = dot(cs, pv)
            dco[r] += dot_nt(dlow, pv)
            dpo[srow] = lax.dot_general(
                cs, dlow, (((0,), (0,)), ((), ())), preferred_element_type=F32
            ).astype(BF)
            pick = head_sum_matrix(s * SPAN + i * 6).astype(BF)
            dpk[...] += dot((dprev * from_prev).astype(BF), pick)
            small[i, 1:2] += jnp.sum(dyf * x[0, r].astype(F32), axis=0, keepdims=True)

        high = []
        for s in range(4):
            high.append(group_cols(to_lane0(pk[6, 0:8], s, i))[0:1])
        f = jnp.concatenate(high, axis=0)
        fh = f.astype(BF).astype(F32)
        dpo[512:528] = jnp.concatenate([fh, f - fh, jnp.zeros((8, 384), F32)], axis=0).astype(BF)


def put_grad(i, me_dp, keep, send, value, at):
    count, rows = keep.shape[1], keep.shape[2]
    width = value.shape[1]

    def store(ref):
        for n in range(count):
            part = value[n * rows : (n + 1) * rows].astype(BF)
            if count > 1:
                ref[i // 2, n ^ me_dp, :, at : at + width] = part
            else:
                ref[i // 2, 0, :, at : at + width] = part

    @pl.when(i % 2 == 0)
    def _():
        store(keep)

    @pl.when(i % 2 == 1)
    def _():
        store(send)


def k4_body(
    sc, nrm, cot, gn, dg, wm, wr, ok, os, zk, zs, dn, nt, dt, wbuf,
):
    i = pl.program_id(0)
    me_dp = sc[9]

    @pl.when(i == 0)
    def _():
        @pl.loop(0, 4)
        def _(s):
            r = rows_of(s)
            nt[:, r] = nrm[r].T
            keep = row_iota(L, 1) < sc[2 * s + 1]
            dt[:, r] = jnp.where(keep, cot[r].astype(F32), 0.0).T.astype(BF)

        dn[...] = jnp.zeros_like(dn)

    assemble_either(wbuf, i, me_dp, [(wm, 0)], [(wr, 0)])
    put_grad(i, me_dp, ok, os, dot(dt[...], gn[0]), 0)
    put_grad(i, me_dp, zk, zs, dot(nt[...], dg[0]), 0)

    @pl.loop(0, 4)
    def _(s):
        dn[rows_of(s)] += dot_nt(dg[0, rows_of(s)], wbuf[...])


def k5_body(sc, x, dy, blow, clow, pk, ct, par, dxo, bco, pko, scores, dsc, rowl):
    i = pl.program_id(0)

    @pl.when(i == 0)
    def _():
        pko[...] = jnp.zeros_like(pko)
        dsc[...] = jnp.zeros_like(dsc)
        rowl[...] = jnp.zeros_like(rowl)

        @pl.loop(0, 4)
        def _(s):
            fe, se = sc[2 * s], sc[2 * s + 1]
            k = lax.broadcasted_iota(jnp.int32, (L, L), 0)
            q = lax.broadcasted_iota(jnp.int32, (L, L), 1)
            same = (q >= k) & (seg_of(q, fe, se) == seg_of(k, fe, se))
            scores[s] = jnp.where(same, dot_nt(blow[rows_of(s)], clow[rows_of(s)]), 0.0)

    @pl.loop(0, 4)
    def _(s):
        cum = to_lane0(pk[0], s, i)
        step = to_lane0(pk[1], s, i)
        lane = lane_iota(L)
        lane_half = lane_iota(128)
        col_top = jnp.zeros((128, 128), F32)
        col_low = jnp.zeros((128, 128), F32)
        for p in range(3):
            cols = slice(128 * p, 128 * p + 128)
            dyp = dy[0, rows_of(s), cols]
            dyf = dyp.astype(F32)
            steps = pair_cols(step, 2 * p)
            xs = x[0, rows_of(s), cols].astype(F32) * steps
            top = jnp.zeros((128, 128), F32)
            low = jnp.zeros((128, 128), F32)
            for b in range(2):
                h = 2 * p + b
                mine = (lane < HD) == (b == 0)
                xh = jnp.where(mine, xs, 0.0).astype(BF)
                dyh = jnp.where(mine, dyf, 0.0).astype(BF)
                ck = cum[:, h : h + 1]
                row = s * SPAN + i * 6 + h
                cq = ct[pl.ds(row, 1), :]
                kern = jnp.exp2(jnp.minimum(cq - ck[:128], 0.0))
                grad = dot_nt(xh[:128], dyp) * kern
                sc0 = scores[s, :128, :]
                wt = (kern * sc0).astype(BF)
                dsc[s, :128, :] += grad
                lg = grad * sc0
                col_top = jnp.where(lane_half == h, jnp.sum(lg, axis=1, keepdims=True), col_top)
                over_k = jnp.sum(lg, axis=0, keepdims=True)
                top = top + dot(wt, dyh)
                kern = jnp.exp2(jnp.minimum(cq[:, 128:] - ck[128:], 0.0))
                grad = dot_nt(xh[128:], dyp[128:]) * kern
                sc1 = scores[s, 128:, 128:]
                wt = (kern * sc1).astype(BF)
                dsc[s, 128:, 128:] += grad
                lg = grad * sc1
                col_low = jnp.where(lane_half == h, jnp.sum(lg, axis=1, keepdims=True), col_low)
                over_low = jnp.sum(lg, axis=0, keepdims=True)
                low = low + dot(wt, dyh[128:])
                rowl[pl.ds(row, 1), :] = over_k + jnp.concatenate(
                    [jnp.zeros((1, 128), F32), over_low], axis=1
                )
            skip = par[i, 8:9, cols]
            dxo[0, rows_of(s), cols] = (
                jnp.concatenate([top, low], axis=0) * steps + skip * dyf
            )
        col = jnp.concatenate([col_top, col_low], axis=0)
        pko[0] += pltpu.roll(col, s * SPAN + i * 6, 1)

    @pl.when(i == 3)
    def _():
        pko[1] = rowl[...].T - pko[0]

        @pl.loop(0, 4)
        def _(s):
            fe, se = sc[2 * s], sc[2 * s + 1]
            k = lax.broadcasted_iota(jnp.int32, (L, L), 0)
            q = lax.broadcasted_iota(jnp.int32, (L, L), 1)
            same = (q >= k) & (seg_of(q, fe, se) == seg_of(k, fe, se))
            ds = jnp.where(same, dsc[s], 0.0)
            bco[0, rows_of(s)] = dot(ds.astype(BF), clow[rows_of(s)])
            bco[1, rows_of(s)] = dot(ds.T.astype(BF), blow[rows_of(s)])


def k6_body(
    sc, nrm, x, dsl, inn, dxl, q1, q2, q3, r1, r2, r3, blow, pk, par, cbc,
    bc5, dc3, dpk3, pk5, sin, dbc, wam, war, wbm, wbr, dnz,
    gk, gs, dn, small, sbc, sdt,
    nt, wbuf, wbc, din, dbacc, dte, dfac, gbuf, fqrow, frow,
):
    i = pl.program_id(0)
    me_t, me_dp = sc[8], sc[9]

    @pl.when(i == 0)
    def _():
        @pl.loop(0, 4)
        def _(s):
            r = rows_of(s)
            nt[:, r] = nrm[r].T

        nt[:, 4 * L :] = nrm[4 * L :].T
        dn[0 : 4 * L] = dnz[...]
        dn[4 * L :] = jnp.zeros((64, dn.shape[1]), F32)
        dbacc[...] = jnp.zeros_like(dbacc)
        dte[...] = jnp.zeros_like(dte)
        dfac[...] = jnp.zeros_like(dfac)
        small[...] = jnp.zeros_like(small)

    @pl.when(i < 4)
    def _():
        assemble_either(wbuf, i, me_dp, [(wam, 0), (wbm, 256)], [(war, 0), (wbr, 256)])
        wbc[i] = wbuf[:, 384:]
        taps = [par[i, k : k + 1] for k in range(4)]
        fqrow[...] = q1[512:528].astype(F32)
        frow[...] = r1[512:528].astype(F32)

        @pl.loop(0, 4)
        def _(s):
            fe, se = sc[2 * s], sc[2 * s + 1]
            r = rows_of(s)
            srow = rows_of(s, 128)
            fq = fqrow[pl.ds(s, 1)] + fqrow[pl.ds(s + 4, 1)]
            g = q1[srow].astype(F32) + q2[srow].astype(F32) + fq * q3[srow].astype(F32)
            fr = frow[pl.ds(s, 1)] + frow[pl.ds(s + 4, 1)]
            pv = r1[srow].astype(F32) + r2[srow].astype(F32) + fr * r3[srow].astype(F32)
            pick = head_sum_matrix(s * SPAN + i * 6)
            gp = jnp.broadcast_to(jnp.sum(g * pv, axis=0, keepdims=True), (8, 384))
            dfac[...] += dot_high(gp, pick)
            glow = g.astype(BF)
            u = dot(blow[r], glow)
            te = group_cols(to_lane0(pk[3], s, i))
            xf = x[0, r].astype(F32)
            dte[...] += dot((xf * u).astype(BF), pick.astype(BF))
            dbacc[r] += dot_nt((te * xf).astype(BF), glow)
            dconv = (dxl[0, r] + te * u) * dsl[0, r].astype(F32)
            small[i, 4:5] += jnp.sum(dconv, axis=0, keepdims=True)
            hrow = pl.ds(pl.multiple_of(4 * L + 16 * s, 16), 16)
            v_ext = jnp.concatenate(
                [inn[0, hrow].astype(F32)[8:], inn[0, r].astype(F32)], axis=0
            )
            dv, tap_grads = conv_backward(dconv, v_ext, taps, fe, se)
            for k in range(4):
                small[i, k : k + 1] += tap_grads[k]
            din[r] = dv[8:].astype(BF)
            din[hrow] = jnp.concatenate([jnp.zeros((8, 384), F32), dv[:8]], axis=0).astype(BF)
            dn[r] += dot_nt(din[r], wbuf[:, :384])

        dn[4 * L :] += dot_nt(din[4 * L :], wbuf[:, :384])
        put_grad(i, me_dp, gk, gs, dot(nt[...], din[...]), 0)

    @pl.when(i == 4)
    def _():
        for q in range(2):
            taps = [cbc[k : k + 1, 128 * q : 128 * q + 128] for k in range(4)]
            sbc[q] = jnp.zeros((8, 128), F32)

            @pl.loop(0, 4)
            def _(s):
                fe, se = sc[2 * s], sc[2 * s + 1]
                r = rows_of(s)
                grad = bc5[q, r] + (dbacc[r] if q == 0 else dc3[r])
                dconv = grad * dbc[q, r]
                hrow = pl.ds(pl.multiple_of(4 * L + 16 * s, 16), 16)
                v_ext = jnp.concatenate([sin[q, hrow][8:], sin[q, r]], axis=0)
                dv, tap_grads = conv_backward(dconv, v_ext, taps, fe, se)
                sbc[q, 4:5] += jnp.sum(dconv, axis=0, keepdims=True)
                for k in range(4):
                    sbc[q, k : k + 1] += tap_grads[k]
                gbuf[q, r] = dv[8:]
                gbuf[q, hrow] = jnp.concatenate([jnp.zeros((8, 128), F32), dv[:8]], axis=0)

        end_terms = dte[...] * pk[3]
        row = row_iota(L, 128)
        last = jnp.sum(end_terms, axis=0, keepdims=True) + dfac[0:1] * pk[6, 0:1]
        dcum = dpk3[...] + pk5[1] - end_terms + jnp.where(row == L - 1, last, 0.0)
        upper = jnp.where(
            lax.broadcasted_iota(jnp.int32, (L, L), 0) <= lax.broadcasted_iota(jnp.int32, (L, L), 1),
            1.0,
            0.0,
        )
        dlog = dot_high(upper, dcum)
        alog = jnp.zeros((1, 128), F32)
        for g in range(4):
            for s in range(4):
                alog += pltpu.roll(par[g, 7:8, :128], s * SPAN + g * 6, 1)
        step, sig = pk[1], pk[2]
        ratio = jnp.where(step > 1e-30, sig / jnp.maximum(step, 1e-30), 1.0)
        ddt = ratio * (pk5[0] + end_terms) - sig * jnp.exp(alog) * dlog
        sdt[...] = jnp.concatenate(
            [
                jnp.sum(ddt, axis=0, keepdims=True),
                jnp.sum(dlog * pk[5], axis=0, keepdims=True),
                jnp.zeros((6, 128), F32),
            ],
            axis=0,
        )
        for n in range(4):
            t = n ^ me_t
            turn = (64 * (t % 2)) % 128
            lane = lane_iota(L)

            @pl.loop(0, 4)
            def _(s):
                r = rows_of(s)
                a = pltpu.roll(gbuf[t // 2, r], turn, 1)
                d = pltpu.roll(ddt, (320 - s * SPAN - n * 6) % 128, 1)
                piece = jnp.where(lane < 64, a, jnp.where(lane < 70, d, 0.0)).astype(BF)
                din[r, 0:128] = piece
                dn[r] += dot_nt(piece, wbc[n])

            a = pltpu.roll(gbuf[t // 2, 4 * L :], turn, 1)
            piece = jnp.where(lane_iota(64) < 64, a, 0.0).astype(BF)
            din[4 * L :, 0:128] = piece
            dn[4 * L :] += dot_nt(piece, wbc[n])
            put_grad_static(n, me_dp, gk, gs, dot(nt[...], din[:, 0:128]), 384)


def put_grad_static(n, me_dp, keep, send, value, at):
    ref = keep if n % 2 == 0 else send
    count, rows = ref.shape[1], ref.shape[2]
    width = value.shape[1]
    for m in range(count):
        part = value[m * rows : (m + 1) * rows].astype(BF)
        place = m ^ me_dp if count > 1 else 0
        ref[n // 2, place, :, at : at + width] = part


def k7_body(sc, dn, hr, tok, cot, gain, ig, ng):
    s = pl.program_id(0)

    @pl.when(s == 0)
    def _():
        ng[...] = jnp.zeros_like(ng)

    d = dn[...]
    extra = hr[...].astype(F32)
    width = d.shape[1]
    d = jnp.concatenate([d[: L - 16], d[L - 16 :] + extra], axis=0)
    tv = tok[...].astype(F32)
    r = lax.rsqrt(jnp.mean(tv * tv, axis=-1, keepdims=True) + EPS)
    tr = tv * r
    ng[0:1] += jnp.sum(d * tr, axis=0, keepdims=True)
    gd = gain[...] * d
    inner = jnp.sum(gd * tr, axis=-1, keepdims=True) * (1.0 / width)
    keep = row_iota(L, 1) < sc[2 * s + 1]
    res = jnp.where(keep, cot[...].astype(F32), 0.0)
    ig[...] = (res + r * (gd - tr * inner)).astype(BF)


def full(shape):
    return pl.BlockSpec(shape, lambda *a: (0,) * len(shape))


def call(body, grid, in_specs, out_specs, out_shapes, scratch, cost, name):
    flops, moved = cost
    return pl.pallas_call(
        body,
        grid_spec=pltpu.PrefetchScalarGridSpec(
            num_scalar_prefetch=1,
            grid=grid,
            in_specs=in_specs,
            out_specs=out_specs,
            scratch_shapes=scratch,
        ),
        out_shape=out_shapes,
        compiler_params=pltpu.CompilerParams(vmem_limit_bytes=VMEM_LIMIT),
        cost_estimate=pl.CostEstimate(flops=flops, bytes_accessed=moved, transcendentals=0),
        name=name,
    )


def sds(shape, dtype):
    return jax.ShapeDtypeStruct(shape, dtype)


def flip(value, axis, bit):
    count = lax.axis_size(axis)
    return lax.ppermute(value, axis, [(a, a ^ bit) for a in range(count)])


def stack2(a, b, at):
    return jnp.stack([a, b], axis=at)


def per_device(
    tokens, lengths, cotangent, norm_gain, w_z, w_x, w_bc, w_dt, conv_x, bias_x, conv_bc, bias_bc,
    dt_bias, a_log, skip_d, out_gain, w_out,
):
    tcount = lax.axis_size("tensor")
    dpcount = lax.axis_size("dp")
    me_t = lax.axis_index("tensor")
    me_dp = lax.axis_index("dp")
    slots, own_len, dim = tokens.shape
    rows = slots * own_len
    shard = w_z.shape[0]
    cols = w_z.shape[1]
    heads = w_dt.shape[1]
    fast = shard % 16 == 0 and dpcount & (dpcount - 1) == 0 and dpcount >= 2
    count = dpcount if fast else 1
    brow = shard if fast else dim

    first = lengths[:, 0] - me_t * own_len
    second = first + lengths[:, 1]
    sc = jnp.concatenate(
        [
            jnp.stack([first, second], axis=1).reshape(-1),
            jnp.stack([me_t, me_dp]),
            jnp.zeros((6,), jnp.int32),
        ]
    ).astype(jnp.int32)
    tok = tokens.reshape(rows, dim)
    cot = cotangent.reshape(rows, dim)
    gain = norm_gain.reshape(1, dim)

    bq = w_bc.shape[1] // tcount
    state = w_bc.shape[1] // 2
    own_bc = lax.dynamic_slice_in_dim(w_bc, me_t * bq, bq, 1)
    p1 = jnp.concatenate(
        [w_x, own_bc, w_dt, jnp.zeros((shard, 128 - bq - heads), BF)], axis=1
    )
    tail = tokens[:, own_len - 16 :, :].reshape(slots * 16, dim)
    halo = lax.ppermute(tail, "tensor", [(a, a + 1) for a in range(tcount - 1)])

    def gather_z(v):
        v = v[None]
        bit = dpcount // 2
        while bit > 1:
            v = stack2(v, flip(v, "dp", bit), 1)
            v = v.reshape((-1,) + v.shape[2:])
            bit //= 2
        return v

    def add_y(v, at):
        return stack2(v, flip(v, "dp", 1), at)

    def add_x(v):
        return stack2(v, flip(v, "tensor", 2), 0)

    def order_xy(v):
        v = add_y(add_x(v), 2)
        return v.reshape(2, count, brow, v.shape[-1])

    def order_yx(v):
        v = add_x(add_y(v, 1))
        return v.reshape(2, count, brow, v.shape[-1])

    def core(v):
        return flip(v, "tensor", 1)

    if fast:
        z1 = gather_z(p1)
        wam = order_xy(z1[..., :256])
        wbm = order_yx(z1[..., 256:])
    else:
        z1 = lax.all_gather(p1, "dp", axis=0, tiled=True)[None]
        wam = add_x(z1[..., :256])
        wbm = add_x(z1[..., 256:])
    war, wbr = core(wam), core(wbm)
    if fast:
        z2 = gather_z(jnp.stack([w_z, w_out]))
        wzm = order_xy(z2[:, 0])
        wom = order_yx(z2[:, 1])
    else:
        wzm = add_x(lax.all_gather(w_z, "dp", axis=0, tiled=True)[None])
        wom = add_x(lax.all_gather(w_out, "dp", axis=0, tiled=True)[None])
    wzr, wor = core(wzm), core(wom)

    def lanes(v):
        return jnp.pad(v, (0, cols - v.shape[0]))[None]

    par = jnp.concatenate(
        [
            conv_x,
            bias_x[None],
            out_gain[None],
            lanes(dt_bias),
            lanes(a_log),
            jnp.repeat(skip_d, cols // heads)[None],
            jnp.zeros((7, cols), F32),
        ],
        axis=0,
    )
    par = add_x(par)
    par = stack2(par, core(par), 1).reshape(4, 16, cols)
    bbc = bias_bc.reshape(1, -1)

    srows = slots * state
    wblock = (1, count, brow, 256)
    wide = (1, count, brow, cols)
    group = (1, rows, cols)
    erows = rows + 64

    def by_phase(phase, rank):
        def index(p, i, sc):
            return (jnp.where(p == phase, i, jnp.where(p < phase, 0, 3)),) + (0,) * (rank - 1)

        return index

    def w_phase(phase):
        def index(p, i, sc):
            return (jnp.where(p == phase, i // 2, jnp.where(p < phase, 0, 1)), 0, 0, 0)

        return index

    def abs_phase(phase):
        def index(p, i, sc):
            return (0, jnp.where(p == phase, i, jnp.where(p < phase, 0, 3)) ^ sc[8])

        return index

    nrm, xl, dsl, inn, st, blow, clow, sin, dbc, pk, ct = call(
        k1_body,
        (2, 4),
        [full((rows, dim)), full((64, dim)), full((1, dim))]
        + [pl.BlockSpec(wblock, w_phase(0))] * 4
        + [full((4, 16, cols)), full((4, 2 * state)), full((1, 2 * state))],
        [
            full((erows, dim)),
            pl.BlockSpec(group, by_phase(1, 3)),
            pl.BlockSpec(group, by_phase(1, 3)),
            pl.BlockSpec((1, erows, cols), by_phase(1, 3)),
            pl.BlockSpec((srows + 16, cols), abs_phase(1)),
            full((rows, state)),
            full((rows, state)),
            full((2, erows, state)),
            full((2, rows, state)),
            full((7, L, 128)),
            full((128, L)),
        ],
        [
            sds((erows, dim), BF),
            sds((4, rows, cols), BF),
            sds((4, rows, cols), BF),
            sds((4, erows, cols), BF),
            sds((srows + 16, 4 * cols), BF),
            sds((rows, state), BF),
            sds((rows, state), BF),
            sds((2, erows, state), F32),
            sds((2, rows, state), F32),
            sds((7, L, 128), F32),
            sds((128, L), F32),
        ],
        [
            pltpu.VMEM((dim, 512), BF),
            pltpu.VMEM((4, erows, cols), F32),
            pltpu.VMEM((L, 128), F32),
            pltpu.VMEM((4, state, L), BF),
        ],
        (int(8e9), int(4e7)),
        "project_and_states",
    )(sc, tok, halo, gain, wam, war, wbm, wbr, par, conv_bc, bbc)

    def carry(mine, hops):
        one = lax.ppermute(mine, "tensor", hops[0])
        f = mine[srows : srows + 4].astype(F32) + mine[srows + 4 : srows + 8].astype(F32)
        width = mine.shape[1]
        end = mine[:srows].astype(F32).reshape(slots, state, width) + f[:, None] * one[
            :srows
        ].astype(F32).reshape(slots, state, width)
        end = end.astype(BF).reshape(srows, width)
        two = lax.ppermute(end, "tensor", hops[1])
        three = lax.ppermute(two, "tensor", hops[2])
        return one, two, three

    r1, r2, r3 = carry(st, ([(0, 1), (2, 3)], [(1, 2)], [(2, 3)]))

    def by_i(rank):
        return lambda i, sc: (jnp.minimum(i, 3),) + (0,) * (rank - 1)

    def w_i(i, sc):
        return (jnp.minimum(i, 3) // 2, 0, 0, 0)

    def abs_i(i, sc):
        return (0, jnp.minimum(i, 3) ^ sc[8])

    gate, within = call(
        k2_body,
        (4,),
        [
            full((erows, dim)),
            pl.BlockSpec(wide, w_i),
            pl.BlockSpec(wide, w_i),
            pl.BlockSpec(group, by_i(3)),
            full((rows, state)),
            full((rows, state)),
            full((7, L, 128)),
            full((128, L)),
        ],
        [pl.BlockSpec(group, by_i(3))] * 2,
        [sds((4, rows, cols), F32)] * 2,
        [pltpu.VMEM((dim, cols), BF), pltpu.VMEM((slots, L, L), F32)],
        (int(1.5e10), int(4e7)),
        "gate_and_within",
    )(sc, nrm, wzm, wzr, xl, blow, clow, pk, ct)

    out, gn, dg, dy, dp, dpk3, dc3, small3 = call(
        k3_body,
        (3, 4),
        [
            pl.BlockSpec(group, by_phase(0, 3)),
            pl.BlockSpec(group, by_phase(0, 3)),
            pl.BlockSpec(group, lambda p, i, sc: (jnp.where(p == 1, 3, i), 0, 0)),
            pl.BlockSpec((srows + 16, cols), abs_phase(0)),
            pl.BlockSpec((srows, cols), abs_phase(0)),
            pl.BlockSpec((srows, cols), abs_phase(0)),
            full((7, L, 128)),
            full((rows, state)),
            full((4, 16, cols)),
            pl.BlockSpec(wide, w_phase(1)),
            pl.BlockSpec(wide, w_phase(1)),
            full((rows, dim)),
            full((rows, dim)),
        ],
        [
            full((rows, dim)),
            pl.BlockSpec(group, by_phase(1, 3)),
            pl.BlockSpec(group, by_phase(2, 3)),
            pl.BlockSpec(group, by_phase(2, 3)),
            pl.BlockSpec((srows + 16, cols), abs_phase(2)),
            full((L, 128)),
            full((rows, state)),
            full((4, 8, cols)),
        ],
        [
            sds((rows, dim), BF),
            sds((4, rows, cols), BF),
            sds((4, rows, cols), BF),
            sds((4, rows, cols), BF),
            sds((srows + 16, 4 * cols), BF),
            sds((L, 128), F32),
            sds((rows, state), F32),
            sds((4, 8, cols), F32),
        ],
        [
            pltpu.VMEM((4, rows, cols), F32),
            pltpu.VMEM((4, rows, cols), F32),
            pltpu.VMEM((4, rows, cols), F32),
            pltpu.VMEM((4, srows, cols), BF),
            pltpu.VMEM((2, rows, 128), F32),
            pltpu.VMEM((rows, dim), F32),
            pltpu.VMEM((rows, dim), BF),
            pltpu.VMEM((dim, cols), BF),
            pltpu.VMEM((16, cols), F32),
        ],
        (int(1.2e10), int(4e7)),
        "gated_norm",
    )(sc, within, gate, xl, r1, r2, r3, pk, clow, par, wom, wor, tok, cot)

    q1, q2, q3 = carry(dp, ([(1, 0), (3, 2)], [(2, 1)], [(1, 0)]))

    gshape = (2, count, brow, cols)
    ok, osend, zk, zsend, dnz = call(
        k4_body,
        (4,),
        [
            full((erows, dim)),
            full((rows, dim)),
            pl.BlockSpec(group, by_i(3)),
            pl.BlockSpec(group, by_i(3)),
            pl.BlockSpec(wide, w_i),
            pl.BlockSpec(wide, w_i),
        ],
        [full(gshape)] * 4 + [full((rows, dim))],
        [sds(gshape, BF)] * 4 + [sds((rows, dim), F32)],
        [
            pltpu.VMEM((dim, rows), BF),
            pltpu.VMEM((dim, rows), BF),
            pltpu.VMEM((dim, cols), BF),
        ],
        (int(7.2e9), int(2e7)),
        "outer_weight_grads",
    )(sc, nrm, cot, gn, dg, wzm, wzr)

    def summed(a, b):
        return (a.astype(F32) + b.astype(F32)).astype(BF)

    def halve(v, axis):
        return lax.index_in_dim(v, 0, axis, False), lax.index_in_dim(v, 1, axis, False)

    def reduce_step(v, axis, mesh_axis, bit):
        keep, send = halve(v, axis)
        return summed(keep, flip(send, mesh_axis, bit))

    def reduce_xy(v):
        v = reduce_step(v, 0, "tensor", 2)
        v = v.reshape((count // 2, 2) + v.shape[1:])
        return reduce_step(v, 1, "dp", 1)

    def reduce_yx(v):
        v = v.reshape((2, count // 2, 2) + v.shape[2:])
        v = reduce_step(v, 2, "dp", 1)
        return reduce_step(v, 0, "tensor", 2)

    def reduce_z(v):
        bit = 2
        while bit < dpcount:
            v = v.reshape((v.shape[0] // 2, 2) + v.shape[1:])
            v = reduce_step(v, 1, "dp", bit)
            bit *= 2
        return v[0].astype(F32)

    def reduce_slow(v):
        v = reduce_step(v, 0, "tensor", 2)[0]
        v = v.reshape(dpcount, shard, v.shape[-1])
        got = lax.all_to_all(v, "dp", split_axis=0, concat_axis=0, tiled=True)
        return got.astype(F32).sum(axis=0)

    def reduce_core(keep, send):
        return summed(keep, flip(send, "tensor", 1))

    vo = reduce_core(ok, osend)
    vz = reduce_core(zk, zsend)
    if fast:
        grad_w_out = reduce_z(reduce_xy(vo))
        grad_w_z = reduce_z(reduce_yx(vz))
    else:
        grad_w_out = reduce_slow(vo)
        grad_w_z = reduce_slow(vz)

    dxl, bc5, pk5 = call(
        k5_body,
        (4,),
        [
            pl.BlockSpec(group, by_i(3)),
            pl.BlockSpec(group, by_i(3)),
            full((rows, state)),
            full((rows, state)),
            full((7, L, 128)),
            full((128, L)),
            full((4, 16, cols)),
        ],
        [pl.BlockSpec(group, by_i(3)), full((2, rows, state)), full((2, L, 128))],
        [
            sds((4, rows, cols), F32),
            sds((2, rows, state), F32),
            sds((2, L, 128), F32),
        ],
        [
            pltpu.VMEM((slots, L, L), F32),
            pltpu.VMEM((slots, L, L), F32),
            pltpu.VMEM((128, L), F32),
        ],
        (int(2e10), int(4e7)),
        "within_backward",
    )(sc, xl, dy, blow, clow, pk, ct, par)

    g1 = (2, count, brow, 512)
    gk, gsend, dn, small6, sbc, sdt = call(
        k6_body,
        (5,),
        [
            full((erows, dim)),
            pl.BlockSpec(group, by_i(3)),
            pl.BlockSpec(group, by_i(3)),
            pl.BlockSpec((1, erows, cols), by_i(3)),
            pl.BlockSpec(group, by_i(3)),
            pl.BlockSpec((srows + 16, cols), abs_i),
            pl.BlockSpec((srows, cols), abs_i),
            pl.BlockSpec((srows, cols), abs_i),
            pl.BlockSpec((srows + 16, cols), abs_i),
            pl.BlockSpec((srows, cols), abs_i),
            pl.BlockSpec((srows, cols), abs_i),
            full((rows, state)),
            full((7, L, 128)),
            full((4, 16, cols)),
            full((4, 2 * state)),
            full((2, rows, state)),
            full((rows, state)),
            full((L, 128)),
            full((2, L, 128)),
            full((2, erows, state)),
            full((2, rows, state)),
        ]
        + [pl.BlockSpec(wblock, w_i)] * 4
        + [full((rows, dim))],
        [
            full(g1),
            full(g1),
            full((erows, dim)),
            full((4, 8, cols)),
            full((2, 8, state)),
            full((8, 128)),
        ],
        [
            sds(g1, BF),
            sds(g1, BF),
            sds((erows, dim), F32),
            sds((4, 8, cols), F32),
            sds((2, 8, state), F32),
            sds((8, 128), F32),
        ],
        [
            pltpu.VMEM((dim, erows), BF),
            pltpu.VMEM((dim, 512), BF),
            pltpu.VMEM((4, dim, 128), BF),
            pltpu.VMEM((erows, cols), BF),
            pltpu.VMEM((rows, state), F32),
            pltpu.VMEM((L, 128), F32),
            pltpu.VMEM((8, 128), F32),
            pltpu.VMEM((2, erows, state), F32),
            pltpu.VMEM((16, cols), F32),
            pltpu.VMEM((16, cols), F32),
        ],
        (int(1e10), int(4e7)),
        "states_backward",
    )(
        sc, nrm, xl, dsl, inn, dxl, q1, q2, q3, r1, r2, r3, blow, pk, par, conv_bc,
        bc5, dc3, dpk3, pk5, sin, dbc, wam, war, wbm, wbr, dnz,
    )

    hr = lax.ppermute(dn[rows:].astype(BF), "tensor", [(a + 1, a) for a in range(tcount - 1)])
    v1 = reduce_core(gk, gsend)
    if fast:
        ga = reduce_xy(v1[..., :256])
        gb = reduce_yx(v1[..., 256:])
        grad1 = reduce_z(jnp.concatenate([ga, gb], axis=-1))
    else:
        grad1 = reduce_slow(v1)

    ig, ng = call(
        k7_body,
        (slots,),
        [
            pl.BlockSpec((L, dim), lambda s, sc: (s, 0)),
            pl.BlockSpec((16, dim), lambda s, sc: (s, 0)),
            pl.BlockSpec((L, dim), lambda s, sc: (s, 0)),
            pl.BlockSpec((L, dim), lambda s, sc: (s, 0)),
            full((1, dim)),
        ],
        [pl.BlockSpec((L, dim), lambda s, sc: (s, 0)), full((8, dim))],
        [sds((rows, dim), BF), sds((8, dim), F32)],
        [],
        (int(1e8), int(1e7)),
        "input_grad",
    )(sc, dn, hr, tok, cot, gain)

    dts = sdt[:2].reshape(2, slots, SPAN)[:, :, : 4 * heads].sum(axis=1).reshape(2, 4, heads)
    dts = jnp.pad(jnp.swapaxes(dts, 0, 1), ((0, 0), (0, 0), (0, cols - heads)))
    skip_sum = small3[:, 1:2]
    mine = jnp.concatenate(
        [small6[:, :5], small3[:, 0:1], skip_sum, dts, jnp.zeros((4, 7, cols), F32)], axis=1
    )
    flat = jnp.concatenate(
        [
            jnp.concatenate([sbc[0, :5], sbc[1, :5]], axis=1).reshape(-1),
            ng[0],
        ]
    )
    flat = jnp.pad(flat, (0, 8 * cols - flat.shape[0])).reshape(8, cols)
    mine = mine.reshape(2, 2, 16, cols)
    send = jnp.concatenate([mine[:, 1].reshape(32, cols), flat], axis=0)
    got = flip(send, "tensor", 1)
    own = mine[:, 0] + got[:32].reshape(2, 16, cols)
    flat = flat + got[32:]
    got = flip(jnp.concatenate([own[1], flat], axis=0), "tensor", 2)
    both = jnp.concatenate([own[0], flat], axis=0) + got
    bit = 1
    while bit < dpcount:
        both = both + flip(both, "dp", bit)
        bit *= 2
    own, flat = both[:16], both[16:].reshape(-1)
    bcs = flat[: 5 * 2 * state].reshape(5, 2 * state)
    ngain = flat[5 * 2 * state : 5 * 2 * state + dim]
    skip_grad = own[6].reshape(heads, cols // heads).sum(axis=1)

    mine_bc = grad1[:, cols : cols + bq]
    parts = mine_bc.reshape(tcount, shard // tcount, bq)
    got = lax.all_to_all(parts, "tensor", split_axis=0, concat_axis=0, tiled=True)
    grad_w_bc = jnp.swapaxes(got, 0, 1).reshape(shard // tcount, bq * tcount)

    return (
        out.reshape(tokens.shape),
        ig.reshape(tokens.shape),
        ngain,
        grad_w_z,
        grad1[:, :cols],
        grad_w_bc,
        grad1[:, cols + bq : cols + bq + heads],
        own[:4],
        own[4],
        bcs[:4],
        bcs[4],
        own[7, :heads],
        own[8, :heads],
        skip_grad,
        own[5],
        grad_w_out,
    )


def solution(mesh):
    return jax.shard_map(
        per_device,
        mesh=mesh,
        in_specs=(
            P("dp", "tensor", None), P("dp", None), P("dp", "tensor", None), P(),
            P("dp", "tensor"), P("dp", "tensor"), P("dp", None), P("dp", "tensor"),
            P(None, "tensor"), P("tensor"), P(), P(),
            P("tensor"), P("tensor"), P("tensor"), P("tensor"), P("dp", "tensor"),
        ),
        out_specs=(
            P("dp", "tensor", None), P("dp", "tensor", None), P(),
            P("dp", "tensor"), P("dp", "tensor"), P(("dp", "tensor"), None), P("dp", "tensor"),
            P(None, "tensor"), P("tensor"), P(), P(),
            P("tensor"), P("tensor"), P("tensor"), P("tensor"), P("dp", "tensor"),
        ),
        check_vma=False,
    )
```

time: 807 us -> 419 us (0.52)
  Pallas kernels: 0 us -> 219 us
  blocking collectives: 216 us -> 0 us
  matrix products: 145 us -> 0 us
  local copies, waits for them, and re-layouts: 168 us -> 25.8 us
  other arithmetic: 157 us -> 15.3 us
  starting transfers between devices: 5.09 us -> 60.5 us
  between operations: 15.7 us -> 1.57 us
    pallas_call x0 -> x7, Pallas kernels: none -> 219 us  [the longest x1 50.4 us: per_device(): call(k6_body, (5,), [full((erows, dim)), pl.BlockSpec(group, by_i(3)), pl...]
    all_gather x5 -> x0, blocking collectives: 156 us -> none  [the longest x1 33.8 us: per_device(): lax.all_gather(w_out, 'dp', axis=0, tiled=True)]
    dot_general x19 -> x0, matrix products: 144 us -> none  [the longest x1 24 us: mixer_backward(): jnp.einsum('cqhp,ckhp->chqk', dy_heads, x_heads, preferred_element_type=j...]
    ppermute x0 -> x48, waiting for transfers between devices: none -> 96 us  [the longest x40 94.1 us: flip(): return lax.ppermute(value, axis, [(a, a ^ bit) for a in range(count)])]
    reduce_scatter x3 -> x0, waiting for transfers between devices: 84.5 us -> none  [the longest x1 84.4 us: per_device(): lax.psum_scatter(lax.dot_general(columns, own_state, (((0,), (0,)), ((),...]
    reduce_sum x13 -> x2, other arithmetic: 69.7 us -> 0.65 us  [the longest x1 0.63 us: per_device(): skip_grad = own[6].reshape(heads, cols // heads).sum(axis=1)]
    psum x3 -> x0, blocking collectives: 60.1 us -> none  [the longest x1 39.5 us: per_device(): lax.psum((spread_cols(conv_x_grad, tensor_slot, tensor_count), spread_col...]
    ppermute x0 -> x48, starting transfers between devices: none -> 57.3 us  [the longest x40 46.4 us: flip(): return lax.ppermute(value, axis, [(a, a ^ bit) for a in range(count)])]
  transfers between devices with their start and end apart: 7 -> 49, of which waited for: 2 -> 24; matrix products, arithmetic and copies ran while one was open for 36% -> 7% of each run, Pallas kernels for 0% -> 36%
where the time goes in v1:
time: 419 us; the launch traced here: 418 us
  Pallas kernels  219 us (52%)
  waiting for transfers between devices  96 us (23%)
  starting transfers between devices  60.5 us (14%)
  local copies, waits for them, and re-layouts  25.8 us (6%)
  other arithmetic  15.3 us (4%)
    ppermute x40, waiting for transfers between devices, flip(): return lax.ppermute(value, axis, [(a, a ^ bit) for a in range(count)])  94.1 us
    pallas_call x1, Pallas kernels, per_device(): call(k6_body, (5,), [full((erows, dim)), pl.BlockSpec(group, by_i(3)), pl...  50.4 us
    ppermute x40, starting transfers between devices, flip(): return lax.ppermute(value, axis, [(a, a ^ bit) for a in range(count)])  46.4 us
    pallas_call x1, Pallas kernels, per_device(): call(k3_body, (3, 4), [pl.BlockSpec(group, by_phase(0, 3)), pl.BlockSpec(...  46 us
    pallas_call x1, Pallas kernels, per_device(): call(k5_body, (4,), [pl.BlockSpec(group, by_i(3)), pl.BlockSpec(group, by...  42.3 us
    pallas_call x1, Pallas kernels, per_device(): call(k1_body, (2, 4), [full((rows, dim)), full((64, dim)), full((1, dim))...  32 us
    pallas_call x1, Pallas kernels, per_device(): call(k4_body, (4,), [full((erows, dim)), full((rows, dim)), pl.BlockSpec(...  23.4 us
    pallas_call x1, Pallas kernels, per_device(): call(k2_body, (4,), [full((erows, dim)), pl.BlockSpec(wide, w_i), pl.Bloc...  19.1 us
  transfers between devices with their start and end apart: 49, of which 24 were waited for; matrix products, arithmetic and copies ran while one was open for 7% of the time, Pallas kernels for 36%

profile of v1, /device:TPU:0, one launch (start us, length us, event | category | flops | bytes accessed | tf_op | source)
XLA Modules:
  0.0 418.3 jit_solution(14213438161538280709)
XLA Ops:
  2.6 4.1 collective-permute-start.1
  6.7 4.9 %collective-permute-done.1 = bf16[1,96,512]{2,1,0:T(8,128)(2,1)S(1)} collective-permute-done((bf16[1,96,512]{2,1,0:T(8,128)(2,1)S(1)}, bf16[1,96,512]{2,1,0:T(8,128)(2,1)S(1)}, u32[]{:S(2)}, u32[]{:S(2)}) %collective-permute-start.1) | collective-permute-done | bytes 98336 | tf_op jit(solution)/shard_map/ppermute | solution.py:738
  12.4 5.4 %collective-permute-done.2 = bf16[2,96,512]{2,1,0:T(8,128)(2,1)S(1)} collective-permute-done((bf16[2,96,512]{2,1,0:T(8,128)(2,1)S(1)}, bf16[2,96,512]{2,1,0:T(8,128)(2,1)S(1)}, u32[]{:S(2)}, u32[]{:S(2)}) %collective-permute-start.2) | collective-permute-done | bytes 196640 | tf_op jit(solution)/shard_map/ppermute | solution.py:738
  18.0 1.3 collective-permute-start.6
  19.3 1.5 collective-permute-start.3
  20.8 2.9 collective-permute-done.6
  23.8 1.3 collective-permute-start.7
  25.1 1.3 collective-permute-done.3
  27.0 1.6 collective-permute-start.9
  28.6 1.5 slice.237
  30.1 1.9 collective-permute-start
  32.1 1.6 collective-permute-done.7
  35.8 4.3 %collective-permute-start.11 = (bf16[1,2,96,384]{3,2,1,0:T(8,128)(2,1)}, bf16[1,2,96,384]{3,2,1,0:T(8,128)(2,1)S(1)}, u32[]{:S(2)}, u32[]{:S(2)}) collective-permute-start(bf16[1,2,96,384]{3,2,1,0:T(8,128)(2,1)} %get-tuple-element.160), channel_id=1, source_target_pairs={{0,16},{4,20},{8,24},{12,28},{16,0},{20,4},{24,8},{28,12},{1,17},{... | collective-permute-start | bytes 442376 | tf_op jit(solution)/shard_map/ppermute | solution.py:738
  43.4 32.0 %project_and_states.1 = (bf16[1088,768]{1,0:T(8,128)(2,1)}, bf16[4,1024,384]{2,1,0:T(8,128)(2,1)}, bf16[4,1024,384]{2,1,0:T(8,128)(2,1)}, bf16[4,1088,384]{2,1,0...) custom-call(s32[16]{0:T(128)} %pad_add_fusion.1.sc, ...), custom_call_target="tpu_custom_call" | custom-call | flops 8000000000 | bytes 40000000 | tf_op jit(solution)/shard_map/project_and_states/pallas_call | solution.py:871
  75.4 2.4 collective-permute-start.16
  77.9 1.2 collective-permute-start.12
  79.1 7.1 %collective-permute-done.12 = bf16[2,2,96,384]{3,2,1,0:T(8,128)(2,1)S(1)} collective-permute-done((bf16[2,2,96,384]{3,2,1,0:T(8,128)(2,1)S(1)}, bf16[2,2,96,384]{3,2,1,0:T(8,128)(2,1)S(1)}, u32[]{:S(2)}, u32[]{:S(2)}) %collective-permute-start.12) | collective-permute-done | bytes 294944 | tf_op jit(solution)/shard_map/ppermute | solution.py:738
  86.4 1.2 collective-permute-start.13
  87.5 6.1 %collective-permute-done.13 = bf16[4,96,384]{2,1,0:T(8,128)(2,1)S(1)} collective-permute-done((bf16[4,96,384]{2,1,0:T(8,128)(2,1)S(1)}, bf16[4,96,384]{2,1,0:T(8,128)(2,1)S(1)}, u32[]{:S(2)}, u32[]{:S(2)}) %collective-permute-start.13) | collective-permute-done | bytes 294944 | tf_op jit(solution)/shard_map/ppermute | solution.py:738
  93.8 1.6 collective-permute-start.14
  97.3 9.2 %collective-permute-done.14 = bf16[2,4,96,384]{3,2,1,0:T(8,128)(2,1)S(1)} collective-permute-done((bf16[2,4,96,384]{3,2,1,0:T(8,128)(2,1)S(1)}, bf16[2,4,96,384]{3,2,1,0:T(8,128)(2,1)S(1)}, u32[]{:S(2)}, u32[]{:S(2)}) %collective-permute-start.14) | collective-permute-done | bytes 589856 | tf_op jit(solution)/shard_map/ppermute | solution.py:738
  106.9 1.6 collective-permute-start.19
  108.5 7.8 %collective-permute-done.19 = bf16[4,96,384]{2,1,0:T(8,128)(2,1)S(1)} collective-permute-done((bf16[4,96,384]{2,1,0:T(8,128)(2,1)S(1)}, bf16[4,96,384]{2,1,0:T(8,128)(2,1)S(1)}, u32[]{:S(2)}, u32[]{:S(2)}) %collective-permute-start.19) | collective-permute-done | bytes 294944 | tf_op jit(solution)/shard_map/ppermute | solution.py:738
  116.4 1.2 collective-permute-start.20
  118.5 12.8 %collective-permute-done.20 = bf16[4,2,96,384]{3,2,1,0:T(8,128)(2,1)S(1)} collective-permute-done((bf16[4,2,96,384]{3,2,1,0:T(8,128)(2,1)S(1)}, bf16[4,2,96,384]{3,2,1,0:T(8,128)(2,1)S(1)}, u32[]{:S(2)}, u32[]{:S(2)}) %collective-permute-start.20) | collective-permute-done | bytes 589856 | tf_op jit(solution)/shard_map/ppermute | solution.py:738
  131.6 1.1 copy-done.31
  132.7 19.1 %gate_and_within.1 = (f32[4,1024,384]{2,1,0:T(8,128)}, f32[4,1024,384]{2,1,0:T(8,128)}) custom-call(s32[16]{0:T(128)} %pad_add_fusion.1.sc, bf16[1088,768]{1,0:T(8,128)(2,1)} %get-tuple-element.53.nrm, bf16[2,8,96,384]{3,2,1,0:T(8,128)(2,1)} %bitcast.282, bf16[2,8,96,384]{3,2,1,0:T(8,128)(2,1)} %copy-done.31, bf16[4,1024,384]{2,1,0:T(8,128)(2,1)} %get-tuple-element.54.x, ...), custom_call_target="tpu_custom_call" | custom-call | flops 15000000512 | bytes 40000000 | tf_op jit(solution)/shard_map/gate_and_within/pallas_call | solution.py:936
  151.9 1.1 copy-done.32
  153.5 46.0 %gated_norm.1 = (bf16[1024,768]{1,0:T(8,128)(2,1)}, bf16[4,1024,384]{2,1,0:T(8,128)(2,1)}, bf16[4,1024,384]{2,1,0:T(8,128)(2,1)}, bf16[4,1024,384]{2,1,0:T(8,128...) custom-call(s32[16]{0:T(128)} %pad_add_fusion.1.sc, ...), custom_call_target="tpu_custom_call" | custom-call | flops 12000000000 | bytes 40000000 | tf_op jit(solution)/shard_map/gated_norm/pallas_call | solution.py:956
  199.5 23.4 %outer_weight_grads.1 = (bf16[2,8,96,384]{3,2,1,0:T(8,128)(2,1)}, bf16[2,8,96,384]{3,2,1,0:T(8,128)(2,1)}, bf16[2,8,96,384]{3,2,1,0:T(8,128)(2,1)}, bf16[2,8,96,384]{3,2,1,0:T(8,128)(2,1)}, f32[1024,768]{1,0:T(8,128)}) custom-call(s32[16]{0:T(128)} %pad_add_fusion.1.sc, bf16[1088,768]{1,0:T(8,128)(2,1)} %get-tuple-element.53.nrm, ...), custom_call_target="tpu_custom_call" | custom-call | flops 7200000000 | bytes 20000000 | tf_op jit(solution)/shard_map/outer_weight_grads/pallas_call | solution.py:1012
  223.4 1.3 collective-permute-start.22
  224.8 1.2 collective-permute-done.43
  226.0 1.7 add_convert_fusion.1
  227.8 1.1 collective-permute-start.44
  229.3 1.4 collective-permute-start.32
  232.6 42.3 %within_backward.1 = (f32[4,1024,384]{2,1,0:T(8,128)}, f32[2,1024,128]{2,1,0:T(8,128)}, f32[2,256,128]{2,1,0:T(8,128)}) custom-call(s32[16]{0:T(128)} %pad_add_fusion.1.sc, bf16[4,1024,384]{2,1,0:T(8,128)(2,1)} %get-tuple-element.54.x, bf16[4,1024,384]{2,1,0:T(8,128)(2,1)} %get-tuple-element.65.dy, bf16[1024,128]{1,0:T(8,128)(2,1)} %get-tuple-element.55.blow, ...), custom_call_target="tpu_custom_call" | custom-call | flops 20000000000 | bytes 40000000 | tf_op jit(solution)/shard_map/within_backward/pallas_call | solution.py:1080
  275.7 1.2 fusion.4
  277.7 1.5 collective-permute-start.24
  279.4 2.4 collective-permute-start.33
  281.9 4.4 %collective-permute-done.45 = bf16[4,96,384]{2,1,0:T(8,128)(2,1)S(1)} collective-permute-done((bf16[4,96,384]{2,1,0:T(8,128)(2,1)S(1)}, bf16[4,96,384]{2,1,0:T(8,128)(2,1)S(1)}, u32[]{:S(2)}, u32[]{:S(2)}) %collective-permute-start.45) | collective-permute-done | bytes 294944 | tf_op jit(solution)/shard_map/ppermute | solution.py:738
  286.4 1.0 collective-permute-start.46
  287.4 2.3 collective-permute-done.33
  290.4 1.1 collective-permute-start.34
  292.4 1.2 copy-done.11
  293.5 50.4 %states_backward.1 = (bf16[2,8,96,512]{3,2,1,0:T(8,128)(2,1)}, bf16[2,8,96,512]{3,2,1,0:T(8,128)(2,1)}, f32[1088,768]{1,0:T(8,128)}, f32[4,8,384]{2,1,0:T(8,128)...) custom-call(s32[16]{0:T(128)} %pad_add_fusion.1.sc, bf16[1088,768]{1,0:T(8,128)(2,1)} %get-tuple-element.53.nrm, ...), custom_call_target="tpu_custom_call" | custom-call | flops 10000000000 | bytes 40000000 | tf_op jit(solution)/shard_map/states_backward/pallas_call | solution.py:1108
  348.0 1.3 collective-permute-start.25
  349.4 1.9 collective-permute-done.25.hr
  351.9 6.0 %input_grad.1 = (bf16[1024,768]{1,0:T(8,128)(2,1)}, f32[8,768]{1,0:T(8,128)}) custom-call(s32[16]{0:T(128)} %pad_add_fusion.1.sc, f32[1088,768]{1,0:T(8,128)} %get-tuple-element.77.dn, bf16[64,768]{1,0:T(8,128)(2,1)} %copy-done.20, bf16[1024,768]{1,0:T(8,128)(2,1)} %bitcast.266, bf16[1024,768]{1,0:T(8,128)(2,1)} %bitcast.274, f32[1,768]{1,0:T(1,128)} %reshape.234.gain), custom_call_target="tpu_custom_call" | custom-call | flops 100000000 | bytes 10000000 | tf_op jit(solution)/shard_map/input_grad/pallas_call | solution.py:1180
  358.7 3.3 collective-permute-start.26
  365.0 2.9 collective-permute-done.27
  367.9 1.3 collective-permute-start.28
  369.1 3.0 collective-permute-start.35
  372.1 1.1 collective-permute-start.29
  374.8 1.3 collective-permute-done.29
  376.1 2.6 collective-permute-start.30
  378.8 1.3 collective-permute-start.39
  380.1 2.8 collective-permute-done.37
  383.8 4.9 %collective-permute-done.39 = bf16[2,4,96,256]{3,2,1,0:T(8,128)(2,1)S(1)} collective-permute-done((bf16[2,4,96,256]{3,2,1,0:T(8,128)(2,1)S(1)}, bf16[2,4,96,256]{3,2,1,0:T(8,128)(2,1)S(1)}, u32[]{:S(2)}, u32[]{:S(2)}) %collective-permute-start.39) | collective-permute-done | bytes 393248 | tf_op jit(solution)/shard_map/ppermute | solution.py:738
  389.5 1.3 collective-permute-done.38
  390.9 3.7 collective-permute-done.40
  394.7 1.2 collective-permute-start.41
  396.6 3.9 collective-permute-done.41
  401.5 5.7 %collective-permute-done.42 = bf16[1,96,512]{2,1,0:T(8,128)(2,1)S(1)} collective-permute-done((bf16[1,96,512]{2,1,0:T(8,128)(2,1)S(1)}, bf16[1,96,512]{2,1,0:T(8,128)(2,1)S(1)}, u32[]{:S(2)}, u32[]{:S(2)}) %collective-permute-start.42) | collective-permute-done | bytes 98336 | tf_op jit(solution)/shard_map/ppermute | solution.py:738
  407.9 3.3 all-to-all-start
  (236 shorter events, 41.2 us)
Async XLA Ops:
  2.6 9.0 %collective-permute-start.1 = (bf16[1,96,512]{2,1,0:T(8,128)(2,1)S(1)}, bf16[1,96,512]{2,1,0:T(8,128)(2,1)S(1)}, u32[]{:S(2)}, u32[]{:S(2)}) collective-permute-start(bf16[1,96,512]{2,1,0:T(8,128)(2,1)S(1)} %get-tuple-element.162), channel_id=1, source_target_pairs={{0,16},{4,20},{8,24},{12,28},{16,0},{20,4},{24,8},{28,12},{1,17},{... | collective-permute-start | bytes 294920 | tf_op jit(solution)/shard_map/ppermute | solution.py:738
  11.7 6.2 %collective-permute-start.2 = (bf16[2,96,512]{2,1,0:T(8,128)(2,1)S(1)}, bf16[2,96,512]{2,1,0:T(8,128)(2,1)S(1)}, u32[]{:S(2)}, u32[]{:S(2)}) collective-permute-start(bf16[2,96,512]{2,1,0:T(8,128)(2,1)S(1)} %get-tuple-element.158), channel_id=1, source_target_pairs={{0,8},{4,12},{8,0},{12,4},{16,24},{20,28},{24,16},{28,20},{1,9},{5... | collective-permute-start | bytes 589832 | tf_op jit(solution)/shard_map/ppermute | solution.py:738
  17.8 8.8 %copy-start.28 = (f32[6]{0:T(128)S(1)}, f32[6]{0:T(128)}, u32[]{:S(2)}) copy-start(f32[6]{0:T(128)} %param.31) | copy-start | bytes 76
  17.9 9.0 %copy-start.29 = (f32[6]{0:T(128)S(1)}, f32[6]{0:T(128)}, u32[]{:S(2)}) copy-start(f32[6]{0:T(128)} %param.29) | copy-start | bytes 76
  17.9 9.0 %copy-start.30 = (f32[6]{0:T(128)S(1)}, f32[6]{0:T(128)}, u32[]{:S(2)}) copy-start(f32[6]{0:T(128)} %param.30) | copy-start | bytes 76
  17.9 9.0 %copy-start.25 = (f32[384]{0:T(512)S(1)}, f32[384]{0:T(512)}, u32[]{:S(2)}) copy-start(f32[384]{0:T(512)} %param.26) | copy-start | bytes 4612
  17.9 9.0 %copy-start.26 = (f32[384]{0:T(512)S(1)}, f32[384]{0:T(512)}, u32[]{:S(2)}) copy-start(f32[384]{0:T(512)} %param.32) | copy-start | bytes 4612
  17.9 9.0 %copy-start.23 = (f32[4,384]{1,0:T(4,128)S(1)}, f32[4,384]{1,0:T(4,128)}, u32[]{:S(2)}) copy-start(f32[4,384]{1,0:T(4,128)} %param.25) | copy-start | bytes 18436
  18.0 5.7 %collective-permute-start.6 = (bf16[4,96,256]{2,1,0:T(8,128)(2,1)S(1)}, bf16[4,96,256]{2,1,0:T(8,128)(2,1)S(1)}, u32[]{:S(2)}, u32[]{:S(2)}) collective-permute-start(bf16[4,96,256]{2,1,0:T(8,128)(2,1)S(1)} %get-tuple-element.151), channel_id=1, source_target_pairs={{0,4},{4,0},{8,12},{12,8},{16,20},{20,16},{24,28},{28,24},{1,5},{5... | collective-permute-start | bytes 589832 | tf_op jit(solution)/shard_map/ppermute | solution.py:738
  19.3 7.0 %collective-permute-start.3 = (bf16[4,96,256]{2,1,0:T(8,128)(2,1)S(1)}, bf16[4,96,256]{2,1,0:T(8,128)(2,1)S(1)}, u32[]{:S(2)}, u32[]{:S(2)}) collective-permute-start(bf16[4,96,256]{2,1,0:T(8,128)(2,1)S(1)} %get-tuple-element.152), channel_id=1, source_target_pairs={{0,2},{1,3},{2,0},{3,1},{4,6},{5,7},{6,4},{7,5},{8,10},{9,11},{10,... | collective-permute-start | bytes 589832 | tf_op jit(solution)/shard_map/ppermute | solution.py:738
  23.8 9.9 %collective-permute-start.7 = (bf16[4,2,96,256]{3,2,0,1:T(8,128)(2,1)S(1)}, bf16[4,2,96,256]{3,2,0,1:T(8,128)(2,1)S(1)}, u32[]{:S(2)}, u32[]{:S(2)}) collective-permute-start(bf16[4,2,96,256]{3,2,0,1:T(8,128)(2,1)S(1)} %pad_maximum_fusion.9), channel_id=1, source_target_pairs={{0,2},{1,3},{2,0},{3,1},{4,6},{5,7},{6,4},{7,5},{8,10},{9,11},{10,... | collective-permute-start | bytes 1179656 | tf_op jit(solution)/shard_map/ppermute | solution.py:738
  26.4 7.8 %collective-permute-start.4 = (bf16[2,4,96,256]{3,2,1,0:T(8,128)(2,1)S(1)}, bf16[2,4,96,256]{3,2,1,0:T(8,128)(2,1)S(1)}, u32[]{:S(2)}, u32[]{:S(2)}) collective-permute-start(bf16[2,4,96,256]{3,2,1,0:T(8,128)(2,1)S(1)} %get-tuple-element.154), channel_id=1, source_target_pairs={{0,4},{4,0},{8,12},{12,8},{16,20},{20,16},{24,28},{28,24},{1,5},{5... | collective-permute-start | bytes 1179656 | tf_op jit(solution)/shard_map/ppermute | solution.py:738
  27.0 13.3 %collective-permute-start.9 = (f32[16,384]{1,0:T(8,128)S(1)}, f32[16,384]{1,0:T(8,128)S(1)}, u32[]{:S(2)}, u32[]{:S(2)}) collective-permute-start(f32[16,384]{1,0:T(8,128)S(1)} %concatenate.35), channel_id=1, source_target_pairs={{0,2},{1,3},{2,0},{3,1},{4,6},{5,7},{6,4},{7,5},{8,10},{9,11},{10,... | collective-permute-start | bytes 73736 | tf_op jit(solution)/shard_map/ppermute | solution.py:738
  30.1 12.2 %collective-permute-start = (bf16[64,768]{1,0:T(8,128)(2,1)}, bf16[64,768]{1,0:T(8,128)(2,1)}, u32[]{:S(2)}, u32[]{:S(2)}) collective-permute-start(bf16[64,768]{1,0:T(8,128)(2,1)} %bitcast.3), channel_id=1, source_target_pairs={{0,1},{1,2},{2,3},{4,5},{5,6},{6,7},{8,9},{9,10},{10,11},{12,13},{... | collective-permute-start | bytes 294920 | tf_op jit(solution)/shard_map/ppermute | solution.py:782
  33.8 8.5 %collective-permute-start.8 = (bf16[2,8,96,256]{3,2,1,0:T(8,128)(2,1)S(1)}, bf16[2,8,96,256]{3,2,1,0:T(8,128)(2,1)S(1)}, u32[]{:S(2)}, u32[]{:S(2)}) collective-permute-start(bf16[2,8,96,256]{3,2,1,0:T(8,128)(2,1)S(1)} %pad_maximum_fusion.3.wbm), channel_id=1, source_target_pairs={{0,1},{1,0},{2,3},{3,2},{4,5},{5,4},{6,7},{7,6},{8,9},{9,8},{10,11... | collective-permute-start | bytes 2359304 | tf_op jit(solution)/shard_map/ppermute | solution.py:738
  34.7 7.6 %copy-start.5 = (bf16[2,4,2,96,256]{4,3,2,1,0:T(8,128)(2,1)}, bf16[2,4,2,96,256]{4,3,2,1,0:T(8,128)(2,1)S(1)}, u32[]{:S(2)}) copy-start(bf16[2,4,2,96,256]{4,3,2,1,0:T(8,128)(2,1)S(1)} %copy.74) | copy-start | bytes 2359300
  34.7 7.6 %collective-permute-start.5 = (bf16[2,8,96,256]{3,2,1,0:T(8,128)(2,1)S(1)}, bf16[2,8,96,256]{3,2,1,0:T(8,128)(2,1)S(1)}, u32[]{:S(2)}, u32[]{:S(2)}) collective-permute-start(bf16[2,8,96,256]{3,2,1,0:T(8,128)(2,1)S(1)} %bitcast.257), channel_id=1, source_target_pairs={{0,1},{1,0},{2,3},{3,2},{4,5},{5,4},{6,7},{7,6},{8,9},{9,8},{10,11... | collective-permute-start | bytes 2359304 | tf_op jit(solution)/shard_map/ppermute | solution.py:738
  35.8 42.0 %collective-permute-start.11 = (bf16[1,2,96,384]{3,2,1,0:T(8,128)(2,1)}, bf16[1,2,96,384]{3,2,1,0:T(8,128)(2,1)S(1)}, u32[]{:S(2)}, u32[]{:S(2)}) collective-permute-start(bf16[1,2,96,384]{3,2,1,0:T(8,128)(2,1)} %get-tuple-element.160), channel_id=1, source_target_pairs={{0,16},{4,20},{8,24},{12,28},{16,0},{20,4},{24,8},{28,12},{1,17},{... | collective-permute-start | bytes 442376 | tf_op jit(solution)/shard_map/ppermute | solution.py:738
  40.3 1.3 collective-permute-start.10
  75.4 20.0 %collective-permute-start.16 = (bf16[528,1536]{1,0:T(8,128)(2,1)}, bf16[528,1536]{1,0:T(8,128)(2,1)S(1)}, u32[]{:S(2)}, u32[]{:S(2)}) collective-permute-start(bf16[528,1536]{1,0:T(8,128)(2,1)} %get-tuple-element.61), channel_id=1, source_target_pairs={{0,1},{2,3},{4,5},{6,7},{8,9},{10,11},{12,13},{14,15},{16,17},{18,... | collective-permute-start | bytes 4866056 | tf_op jit(solution)/shard_map/ppermute | solution.py:914
  77.9 8.3 %collective-permute-start.12 = (bf16[2,2,96,384]{3,2,1,0:T(8,128)(2,1)S(1)}, bf16[2,2,96,384]{3,2,1,0:T(8,128)(2,1)S(1)}, u32[]{:S(2)}, u32[]{:S(2)}) collective-permute-start(bf16[2,2,96,384]{3,2,1,0:T(8,128)(2,1)S(1)} %get-tuple-element.156), channel_id=1, source_target_pairs={{0,8},{4,12},{8,0},{12,4},{16,24},{20,28},{24,16},{28,20},{1,9},{5... | collective-permute-start | bytes 884744 | tf_op jit(solution)/shard_map/ppermute | solution.py:738
  86.2 9.2 %copy-start.6 = (bf16[528,1536]{1,0:T(8,128)(2,1)S(1)}, bf16[528,1536]{1,0:T(8,128)(2,1)}, u32[]{:S(2)}) copy-start(bf16[528,1536]{1,0:T(8,128)(2,1)} %get-tuple-element.61) | copy-start | bytes 4866052
  86.4 7.3 %collective-permute-start.13 = (bf16[4,96,384]{2,1,0:T(8,128)(2,1)S(1)}, bf16[4,96,384]{2,1,0:T(8,128)(2,1)S(1)}, u32[]{:S(2)}, u32[]{:S(2)}) collective-permute-start(bf16[4,96,384]{2,1,0:T(8,128)(2,1)S(1)} %get-tuple-element.145), channel_id=1, source_target_pairs={{0,2},{1,3},{2,0},{3,1},{4,6},{5,7},{6,4},{7,5},{8,10},{9,11},{10,... | collective-permute-start | bytes 884744 | tf_op jit(solution)/shard_map/ppermute | solution.py:738
  93.8 12.7 %collective-permute-start.14 = (bf16[2,4,96,384]{3,2,1,0:T(8,128)(2,1)S(1)}, bf16[2,4,96,384]{3,2,1,0:T(8,128)(2,1)S(1)}, u32[]{:S(2)}, u32[]{:S(2)}) collective-permute-start(bf16[2,4,96,384]{3,2,1,0:T(8,128)(2,1)S(1)} %get-tuple-element.148), channel_id=1, source_target_pairs={{0,4},{4,0},{8,12},{12,8},{16,20},{20,16},{24,28},{28,24},{1,5},{5... | collective-permute-start | bytes 1769480 | tf_op jit(solution)/shard_map/ppermute | solution.py:738
  96.6 21.0 %collective-permute-start.17 = (bf16[512,1536]{1,0:T(8,128)(2,1)S(1)}, bf16[512,1536]{1,0:T(8,128)(2,1)S(1)}, u32[]{:S(2)}, u32[]{:S(2)}) collective-permute-start(bf16[512,1536]{1,0:T(8,128)(2,1)S(1)} %fusion.3), channel_id=1, source_target_pairs={{1,2},{5,6},{9,10},{13,14},{17,18},{21,22},{25,26},{29,30}} | collective-permute-start | bytes 4718600 | tf_op jit(solution)/shard_map/ppermute | solution.py:921
  106.8 24.7 %copy-start.14 = (bf16[2,4,2,96,384]{4,3,2,1,0:T(8,128)(2,1)}, bf16[2,4,2,96,384]{4,3,2,1,0:T(8,128)(2,1)S(1)}, u32[]{:S(2)}) copy-start(bf16[2,4,2,96,384]{4,3,2,1,0:T(8,128)(2,1)S(1)} %copy.79) | copy-start | bytes 3538948
  106.8 24.8 %collective-permute-start.15 = (bf16[2,8,96,384]{3,2,1,0:T(8,128)(2,1)S(1)}, bf16[2,8,96,384]{3,2,1,0:T(8,128)(2,1)S(1)}, u32[]{:S(2)}, u32[]{:S(2)}) collective-permute-start(bf16[2,8,96,384]{3,2,1,0:T(8,128)(2,1)S(1)} %bitcast.281), channel_id=1, source_target_pairs={{0,1},{1,0},{2,3},{3,2},{4,5},{5,4},{6,7},{7,6},{8,9},{9,8},{10,11... | collective-permute-start | bytes 3538952 | tf_op jit(solution)/shard_map/ppermute | solution.py:738
  106.9 9.4 %collective-permute-start.19 = (bf16[4,96,384]{2,1,0:T(8,128)(2,1)S(1)}, bf16[4,96,384]{2,1,0:T(8,128)(2,1)S(1)}, u32[]{:S(2)}, u32[]{:S(2)}) collective-permute-start(bf16[4,96,384]{2,1,0:T(8,128)(2,1)S(1)} %get-tuple-element.144), channel_id=1, source_target_pairs={{0,4},{4,0},{8,12},{12,8},{16,20},{20,16},{24,28},{28,24},{1,5},{5... | collective-permute-start | bytes 884744 | tf_op jit(solution)/shard_map/ppermute | solution.py:738
  116.4 15.0 %collective-permute-start.20 = (bf16[4,2,96,384]{3,2,1,0:T(8,128)(2,1)S(1)}, bf16[4,2,96,384]{3,2,1,0:T(8,128)(2,1)S(1)}, u32[]{:S(2)}, u32[]{:S(2)}) collective-permute-start(bf16[4,2,96,384]{3,2,1,0:T(8,128)(2,1)S(1)} %pad_maximum_fusion.6), channel_id=1, source_target_pairs={{0,2},{1,3},{2,0},{3,1},{4,6},{5,7},{6,4},{7,5},{8,10},{9,11},{10,... | collective-permute-start | bytes 1769480 | tf_op jit(solution)/shard_map/ppermute | solution.py:738
  117.6 34.3 %copy-start.8 = (bf16[512,1536]{1,0:T(8,128)(2,1)}, bf16[512,1536]{1,0:T(8,128)(2,1)S(1)}, u32[]{:S(2)}) copy-start(bf16[512,1536]{1,0:T(8,128)(2,1)S(1)} %collective-permute-done.17.r2) | copy-start | bytes 4718596
  117.6 34.3 %collective-permute-start.18 = (bf16[512,1536]{1,0:T(8,128)(2,1)S(1)}, bf16[512,1536]{1,0:T(8,128)(2,1)S(1)}, u32[]{:S(2)}, u32[]{:S(2)}) collective-permute-start(bf16[512,1536]{1,0:T(8,128)(2,1)S(1)} %collective-permute-done.17.r2), channel_id=1, source_target_pairs={{2,3},{6,7},{10,11},{14,15},{18,19},{22,23},{26,27},{30,31}} | collective-permute-start | bytes 4718600 | tf_op jit(solution)/shard_map/ppermute | solution.py:922
  131.5 20.3 %copy-start.15 = (bf16[2,8,96,384]{3,2,1,0:T(8,128)(2,1)}, bf16[2,8,96,384]{3,2,1,0:T(8,128)(2,1)S(1)}, u32[]{:S(2)}) copy-start(bf16[2,8,96,384]{3,2,1,0:T(8,128)(2,1)S(1)} %pad_maximum_fusion.1.wm) | copy-start | bytes 3538948
  131.5 20.3 %collective-permute-start.21 = (bf16[2,8,96,384]{3,2,1,0:T(8,128)(2,1)S(1)}, bf16[2,8,96,384]{3,2,1,0:T(8,128)(2,1)S(1)}, u32[]{:S(2)}, u32[]{:S(2)}) collective-permute-start(bf16[2,8,96,384]{3,2,1,0:T(8,128)(2,1)S(1)} %pad_maximum_fusion.1.wm), channel_id=1, source_target_pairs={{0,1},{1,0},{2,3},{3,2},{4,5},{5,4},{6,7},{7,6},{8,9},{9,8},{10,11... | collective-permute-start | bytes 3538952 | tf_op jit(solution)/shard_map/ppermute | solution.py:738
  199.5 23.9 %copy-start.7 = (bf16[528,1536]{1,0:T(8,128)(2,1)S(1)}, bf16[528,1536]{1,0:T(8,128)(2,1)}, u32[]{:S(2)}) copy-start(bf16[528,1536]{1,0:T(8,128)(2,1)} %get-tuple-element.67) | copy-start | bytes 4866052
  222.9 3.1 collective-permute-start.43
  223.4 5.5 %collective-permute-start.31 = (bf16[2,8,96,384]{3,2,1,0:T(8,128)(2,1)}, bf16[2,8,96,384]{3,2,1,0:T(8,128)(2,1)S(1)}, u32[]{:S(2)}, u32[]{:S(2)}) collective-permute-start(bf16[2,8,96,384]{3,2,1,0:T(8,128)(2,1)} %get-tuple-element.85), channel_id=1, source_target_pairs={{0,1},{1,0},{2,3},{3,2},{4,5},{5,4},{6,7},{7,6},{8,9},{9,8},{10,11... | collective-permute-start | bytes 3538952 | tf_op jit(solution)/shard_map/ppermute | solution.py:738
  223.4 7.2 %collective-permute-start.22 = (bf16[528,1536]{1,0:T(8,128)(2,1)S(1)}, bf16[528,1536]{1,0:T(8,128)(2,1)S(1)}, u32[]{:S(2)}, u32[]{:S(2)}) collective-permute-start(bf16[528,1536]{1,0:T(8,128)(2,1)S(1)} %copy-done.7), channel_id=1, source_target_pairs={{1,0},{3,2},{5,4},{7,6},{9,8},{11,10},{13,12},{15,14},{17,16},{19,... | collective-permute-start | bytes 4866056 | tf_op jit(solution)/shard_map/ppermute | solution.py:914
  227.8 47.9 %collective-permute-start.44 = (bf16[8,96,384]{2,1,0:T(8,128)(2,1)S(1)}, bf16[8,96,384]{2,1,0:T(8,128)(2,1)}, u32[]{:S(2)}, u32[]{:S(2)}) collective-permute-start(bf16[8,96,384]{2,1,0:T(8,128)(2,1)S(1)} %slice_bitcast_fusion), channel_id=1, source_target_pairs={{0,2},{1,3},{2,0},{3,1},{4,6},{5,7},{6,4},{7,5},{8,10},{9,11},{10,... | collective-permute-start | bytes 1769480 | tf_op jit(solution)/shard_map/ppermute | solution.py:738
  229.3 50.0 %collective-permute-start.32 = (bf16[2,4,96,384]{3,2,1,0:T(8,128)(2,1)S(1)}, bf16[2,4,96,384]{3,2,1,0:T(8,128)(2,1)S(1)}, u32[]{:S(2)}, u32[]{:S(2)}) collective-permute-start(bf16[2,4,96,384]{3,2,1,0:T(8,128)(2,1)S(1)} %slice_bitcast_fusion.2), channel_id=1, source_target_pairs={{0,4},{4,0},{8,12},{12,8},{16,20},{20,16},{24,28},{28,24},{1,5},{5... | collective-permute-start | bytes 1769480 | tf_op jit(solution)/shard_map/ppermute | solution.py:738
  231.8 45.9 %collective-permute-start.23 = (bf16[512,1536]{1,0:T(8,128)(2,1)S(1)}, bf16[512,1536]{1,0:T(8,128)(2,1)S(1)}, u32[]{:S(2)}, u32[]{:S(2)}) collective-permute-start(bf16[512,1536]{1,0:T(8,128)(2,1)S(1)} %fusion.1), channel_id=1, source_target_pairs={{2,1},{6,5},{10,9},{14,13},{18,17},{22,21},{26,25},{30,29}} | collective-permute-start | bytes 4718600 | tf_op jit(solution)/shard_map/ppermute | solution.py:921
  277.0 9.3 %collective-permute-start.45 = (bf16[4,96,384]{2,1,0:T(8,128)(2,1)S(1)}, bf16[4,96,384]{2,1,0:T(8,128)(2,1)S(1)}, u32[]{:S(2)}, u32[]{:S(2)}) collective-permute-start(bf16[4,96,384]{2,1,0:T(8,128)(2,1)S(1)} %slice_bitcast_fusion.8), channel_id=1, source_target_pairs={{0,4},{4,0},{8,12},{12,8},{16,20},{20,16},{24,28},{28,24},{1,5},{5... | collective-permute-start | bytes 884744 | tf_op jit(solution)/shard_map/ppermute | solution.py:738
  277.7 8.6 %copy-start.10 = (bf16[512,1536]{1,0:T(8,128)(2,1)}, bf16[512,1536]{1,0:T(8,128)(2,1)S(1)}, u32[]{:S(2)}) copy-start(bf16[512,1536]{1,0:T(8,128)(2,1)S(1)} %collective-permute-done.23.q2) | copy-start | bytes 4718596
  277.7 14.7 %collective-permute-start.24 = (bf16[512,1536]{1,0:T(8,128)(2,1)S(1)}, bf16[512,1536]{1,0:T(8,128)(2,1)S(1)}, u32[]{:S(2)}, u32[]{:S(2)}) collective-permute-start(bf16[512,1536]{1,0:T(8,128)(2,1)S(1)} %collective-permute-done.23.q2), channel_id=1, source_target_pairs={{1,0},{5,4},{9,8},{13,12},{17,16},{21,20},{25,24},{29,28}} | collective-permute-start | bytes 4718600 | tf_op jit(solution)/shard_map/ppermute | solution.py:922
  279.4 10.2 %collective-permute-start.33 = (bf16[4,96,384]{2,1,0:T(8,128)(2,1)S(1)}, bf16[4,96,384]{2,1,0:T(8,128)(2,1)S(1)}, u32[]{:S(2)}, u32[]{:S(2)}) collective-permute-start(bf16[4,96,384]{2,1,0:T(8,128)(2,1)S(1)} %slice_bitcast_fusion.10), channel_id=1, source_target_pairs={{0,2},{1,3},{2,0},{3,1},{4,6},{5,7},{6,4},{7,5},{8,10},{9,11},{10,... | collective-permute-start | bytes 884744 | tf_op jit(solution)/shard_map/ppermute | solution.py:738
  286.4 5.3 %collective-permute-start.46 = (bf16[2,96,384]{2,1,0:T(8,128)(2,1)S(1)}, bf16[2,96,384]{2,1,0:T(8,128)(2,1)S(1)}, u32[]{:S(2)}, u32[]{:S(2)}) collective-permute-start(bf16[2,96,384]{2,1,0:T(8,128)(2,1)S(1)} %slice_bitcast_fusion.20), channel_id=1, source_target_pairs={{0,8},{4,12},{8,0},{12,4},{16,24},{20,28},{24,16},{28,20},{1,9},{5... | collective-permute-start | bytes 442376 | tf_op jit(solution)/shard_map/ppermute | solution.py:738
  290.4 73.6 %collective-permute-start.34 = (bf16[2,96,384]{2,1,0:T(8,128)(2,1)}, bf16[2,96,384]{2,1,0:T(8,128)(2,1)}, u32[]{:S(2)}, u32[]{:S(2)}) collective-permute-start(bf16[2,96,384]{2,1,0:T(8,128)(2,1)} %slice_bitcast_fusion.22), channel_id=1, source_target_pairs={{0,8},{4,12},{8,0},{12,4},{16,24},{20,28},{24,16},{28,20},{1,9},{5... | collective-permute-start | bytes 442376 | tf_op jit(solution)/shard_map/ppermute | solution.py:738
  343.9 29.3 %collective-permute-start.36 = (bf16[2,8,96,512]{3,2,1,0:T(8,128)(2,1)}, bf16[2,8,96,512]{3,2,1,0:T(8,128)(2,1)S(1)}, u32[]{:S(2)}, u32[]{:S(2)}) collective-permute-start(bf16[2,8,96,512]{3,2,1,0:T(8,128)(2,1)} %get-tuple-element.87), channel_id=1, source_target_pairs={{0,1},{1,0},{2,3},{3,2},{4,5},{5,4},{6,7},{7,6},{8,9},{9,8},{10,11... | collective-permute-start | bytes 4718600 | tf_op jit(solution)/shard_map/ppermute | solution.py:738
  348.0 3.2 collective-permute-start.25
  357.8 15.4 %copy-start.12 = (bf16[2,8,96,512]{3,2,1,0:T(8,128)(2,1)S(1)}, bf16[2,8,96,512]{3,2,1,0:T(8,128)(2,1)}, u32[]{:S(2)}) copy-start(bf16[2,8,96,512]{3,2,1,0:T(8,128)(2,1)} %get-tuple-element.86) | copy-start | bytes 4718596
  358.7 4.2 %collective-permute-start.26 = (f32[40,384]{1,0:T(8,128)S(1)}, f32[40,384]{1,0:T(8,128)S(1)}, u32[]{:S(2)}, u32[]{:S(2)}) collective-permute-start(f32[40,384]{1,0:T(8,128)S(1)} %pad_maximum_fusion.15), channel_id=1, source_target_pairs={{0,1},{1,0},{2,3},{3,2},{4,5},{5,4},{6,7},{7,6},{8,9},{9,8},{10,11... | collective-permute-start | bytes 184328 | tf_op jit(solution)/shard_map/ppermute | solution.py:738
  362.9 10.9 %collective-permute-start.47 = (bf16[1,96,384]{2,1,0:T(8,128)(2,1)S(1)}, bf16[1,96,384]{2,1,0:T(8,128)(2,1)S(1)}, u32[]{:S(2)}, u32[]{:S(2)}) collective-permute-start(bf16[1,96,384]{2,1,0:T(8,128)(2,1)S(1)} %slice_bitcast_fusion.26), channel_id=1, source_target_pairs={{0,16},{4,20},{8,24},{12,28},{16,0},{20,4},{24,8},{28,12},{1,17},{... | collective-permute-start | bytes 221192 | tf_op jit(solution)/shard_map/ppermute | solution.py:738
  363.8 4.0 collective-permute-start.27
  367.9 4.2 %collective-permute-start.28 = (f32[24,384]{1,0:T(8,128)S(1)}, f32[24,384]{1,0:T(8,128)S(1)}, u32[]{:S(2)}, u32[]{:S(2)}) collective-permute-start(f32[24,384]{1,0:T(8,128)S(1)} %fusion.36), channel_id=1, source_target_pairs={{0,4},{4,0},{8,12},{12,8},{16,20},{20,16},{24,28},{28,24},{1,5},{5... | collective-permute-start | bytes 110600 | tf_op jit(solution)/shard_map/ppermute | solution.py:738
  369.1 26.8 %collective-permute-start.35 = (bf16[1,96,384]{2,1,0:T(8,128)(2,1)S(1)}, bf16[1,96,384]{2,1,0:T(8,128)(2,1)S(1)}, u32[]{:S(2)}, u32[]{:S(2)}) collective-permute-start(bf16[1,96,384]{2,1,0:T(8,128)(2,1)S(1)} %slice_bitcast_fusion.28), channel_id=1, source_target_pairs={{0,16},{4,20},{8,24},{12,28},{16,0},{20,4},{24,8},{28,12},{1,17},{... | collective-permute-start | bytes 221192 | tf_op jit(solution)/shard_map/ppermute | solution.py:738
  372.1 4.0 collective-permute-start.29
  373.8 9.1 %collective-permute-start.37 = (bf16[8,96,256]{2,1,0:T(8,128)(2,1)S(1)}, bf16[8,96,256]{2,1,0:T(8,128)(2,1)S(1)}, u32[]{:S(2)}, u32[]{:S(2)}) collective-permute-start(bf16[8,96,256]{2,1,0:T(8,128)(2,1)S(1)} %slice_bitcast_fusion.6), channel_id=1, source_target_pairs={{0,2},{1,3},{2,0},{3,1},{4,6},{5,7},{6,4},{7,5},{8,10},{9,11},{10,... | collective-permute-start | bytes 1179656 | tf_op jit(solution)/shard_map/ppermute | solution.py:738
  376.1 20.4 %collective-permute-start.30 = (f32[24,384]{1,0:T(8,128)S(1)}, f32[24,384]{1,0:T(8,128)S(1)}, u32[]{:S(2)}, u32[]{:S(2)}) collective-permute-start(f32[24,384]{1,0:T(8,128)S(1)} %add.108), channel_id=1, source_target_pairs={{0,16},{4,20},{8,24},{12,28},{16,0},{20,4},{24,8},{28,12},{1,17},{... | collective-permute-start | bytes 110600 | tf_op jit(solution)/shard_map/ppermute | solution.py:738
  378.8 9.9 %collective-permute-start.39 = (bf16[2,4,96,256]{3,2,1,0:T(8,128)(2,1)S(1)}, bf16[2,4,96,256]{3,2,1,0:T(8,128)(2,1)S(1)}, u32[]{:S(2)}, u32[]{:S(2)}) collective-permute-start(bf16[2,4,96,256]{3,2,1,0:T(8,128)(2,1)S(1)} %slice_bitcast_fusion.4), channel_id=1, source_target_pairs={{0,4},{4,0},{8,12},{12,8},{16,20},{20,16},{24,28},{28,24},{1,5},{5... | collective-permute-start | bytes 1179656 | tf_op jit(solution)/shard_map/ppermute | solution.py:738
  383.1 7.8 %collective-permute-start.38 = (bf16[4,96,256]{2,1,0:T(8,128)(2,1)S(1)}, bf16[4,96,256]{2,1,0:T(8,128)(2,1)S(1)}, u32[]{:S(2)}, u32[]{:S(2)}) collective-permute-start(bf16[4,96,256]{2,1,0:T(8,128)(2,1)S(1)} %slice_bitcast_fusion.18), channel_id=1, source_target_pairs={{0,4},{4,0},{8,12},{12,8},{16,20},{20,16},{24,28},{28,24},{1,5},{5... | collective-permute-start | bytes 589832 | tf_op jit(solution)/shard_map/ppermute | solution.py:738
  388.9 5.7 %collective-permute-start.40 = (bf16[4,96,256]{2,1,0:T(8,128)(2,1)S(1)}, bf16[4,96,256]{2,1,0:T(8,128)(2,1)S(1)}, u32[]{:S(2)}, u32[]{:S(2)}) collective-permute-start(bf16[4,96,256]{2,1,0:T(8,128)(2,1)S(1)} %slice_bitcast_fusion.16), channel_id=1, source_target_pairs={{0,2},{1,3},{2,0},{3,1},{4,6},{5,7},{6,4},{7,5},{8,10},{9,11},{10,... | collective-permute-start | bytes 589832 | tf_op jit(solution)/shard_map/ppermute | solution.py:738
  394.6 23.7 %copy-start.1 = (bf16[96,256]{1,0:T(8,128)(2,1)S(1)}, bf16[96,256]{1,0:T(8,128)(2,1)}, u32[]{:S(2)}) copy-start(bf16[96,256]{1,0:T(8,128)(2,1)} %param.23) | copy-start | bytes 147460
  394.7 5.7 %collective-permute-start.41 = (bf16[2,96,512]{2,1,0:T(8,128)(2,1)S(1)}, bf16[2,96,512]{2,1,0:T(8,128)(2,1)S(1)}, u32[]{:S(2)}, u32[]{:S(2)}) collective-permute-start(bf16[2,96,512]{2,1,0:T(8,128)(2,1)S(1)} %slice_bitcast_fusion.14), channel_id=1, source_target_pairs={{0,8},{4,12},{8,0},{12,4},{16,24},{20,28},{24,16},{28,20},{1,9},{5... | collective-permute-start | bytes 589832 | tf_op jit(solution)/shard_map/ppermute | solution.py:738
  400.5 6.6 %collective-permute-start.42 = (bf16[1,96,512]{2,1,0:T(8,128)(2,1)S(1)}, bf16[1,96,512]{2,1,0:T(8,128)(2,1)S(1)}, u32[]{:S(2)}, u32[]{:S(2)}) collective-permute-start(bf16[1,96,512]{2,1,0:T(8,128)(2,1)S(1)} %slice_bitcast_fusion.24), channel_id=1, source_target_pairs={{0,16},{4,20},{8,24},{12,28},{16,0},{20,4},{24,8},{28,12},{1,17},{... | collective-permute-start | bytes 294920 | tf_op jit(solution)/shard_map/ppermute | solution.py:738
  407.9 8.4 %all-to-all-start = ((f32[4,1,1536]{2,1,0:T(1,128)}), f32[4,1,1536]{2,1,0:T(1,128)S(1)}, u32[]{:S(2)}, u32[]{:S(2)}) async-start(f32[4,1,1536]{2,1,0:T(1,128)} %reshape.286), calls=%async_computation | async-start | bytes 49152 | tf_op jit(solution)/shard_map/all_to_all | solution.py:1228
  (18 other events, 30.5 us)

commit v2 on v0

v2 whole, which is shorter than its diff:
```python
import functools

import jax
import jax.numpy as jnp
from jax import lax
from jax.experimental import pallas as pl
from jax.experimental.pallas import tpu as pltpu
from jax.sharding import PartitionSpec as P

INNER = 1536
L = 256
HD = 64
SPAN = 32
EPS = 1e-05
LOG2E = 1.4426950408889634
F32 = jnp.float32
BF = jnp.bfloat16
CHUNK = 64
WIDE = 768
VMEM_MIB = 40
K5_MIB = 58


def dot(a, b):
    return jnp.dot(a, b, preferred_element_type=F32)


def dot_nt(a, b):
    return lax.dot_general(a, b, (((1,), (1,)), ((), ())), preferred_element_type=F32)


def dot_high(a, b):
    return jnp.dot(a, b, preferred_element_type=F32, precision=lax.Precision.HIGHEST)


def sigmoid(v):
    return 0.5 * jnp.tanh(0.5 * v) + 0.5


def lane_iota(rows):
    return lax.broadcasted_iota(jnp.int32, (rows, 128), 1)


def row_iota(rows, lanes):
    return lax.broadcasted_iota(jnp.int32, (rows, lanes), 0)


def seg_of(idx, fe, se):
    return (idx >= fe).astype(jnp.int32) + (idx >= se).astype(jnp.int32)


def ends(sc, s):
    return sc[2 * s], sc[2 * s + 1]


def pair_cols(cols, first):
    lane = lane_iota(cols.shape[0])
    left = jnp.broadcast_to(cols[:, first : first + 1], cols.shape)
    right = jnp.broadcast_to(cols[:, first + 1 : first + 2], cols.shape)
    return jnp.where(lane < HD, left, right)


def head_pick():
    r = lax.broadcasted_iota(jnp.int32, (WIDE, 128), 0)
    c = lax.broadcasted_iota(jnp.int32, (WIDE, 128), 1)
    return jnp.where(c == r // HD, 1.0, 0.0)


def head_spread():
    r = lax.broadcasted_iota(jnp.int32, (256, WIDE), 0)
    c = lax.broadcasted_iota(jnp.int32, (256, WIDE), 1)
    return jnp.where(r % 128 == c // HD, 1.0, 0.0).astype(BF)


def expand(dst, cols, spread):
    high = cols.astype(BF)
    low = (cols - high.astype(F32)).astype(BF)
    both = jnp.concatenate([high, low], axis=1)
    for n in range(3):
        dst[:, 256 * n : 256 * n + 256] = dot(both, spread[:, 256 * n : 256 * n + 256])


def three_terms(v):
    high = v.astype(BF).astype(F32)
    mid = (v - high).astype(BF).astype(F32)
    return high, mid, v - high - mid


def tile_spread():
    r = lax.broadcasted_iota(jnp.int32, (256, 2 * WIDE), 0)
    h = lax.broadcasted_iota(jnp.int32, (256, 2 * WIDE), 1) // 128
    return jnp.where((r == h) | (r == h + 128) | (r == h + 144), 1.0, 0.0).astype(BF)


def expand_tiles(dst, cols, spread):
    high, mid, low = three_terms(cols)
    lane = lane_iota(L)
    rest = jnp.where(lane < 16, mid, pltpu.roll(low, 16, 1))
    left = jnp.concatenate([high, rest], axis=1).astype(BF)
    for n in range(6):
        dst[:, 256 * n : 256 * n + 256] = dot(left, spread[:, 256 * n : 256 * n + 256])


def to_lane0(packed, s, g):
    return pltpu.roll(packed, (256 - s * SPAN - g * 12) % 128, 1)


def from_lane0(cols, s, g):
    return pltpu.roll(cols, s * SPAN + g * 12, 1)


def rows_of(s, length=L):
    return pl.ds(pl.multiple_of(s * length, length), length)


def tile(j):
    return slice(128 * j, 128 * j + 128)


def conv_forward(ext, taps, bias, masks, first=0, length=L):
    acc = bias + taps[0] * ext[8 + first : 8 + first + length]
    for k in range(1, 4):
        acc = acc + (taps[k] * ext[8 + first - k : 8 + first - k + length]) * masks[k - 1]
    return acc


def conv_backward(ext, v_ext, taps, masks):
    out, tap_grads = None, []
    for k in range(4):
        part = ext[k : 264 + k]
        if k:
            part = part * masks[k - 1]
        tap_grads.append(jnp.sum(part * v_ext, axis=0, keepdims=True))
        out = taps[k] * part if out is None else out + taps[k] * part
    return out, tap_grads


def slot_masks(packed, s):
    cols = pltpu.roll(packed[...], (128 - 4 * s) % 128, 1)
    return [jnp.broadcast_to(cols[:, k : k + 1], cols.shape) for k in (1, 2, 3)]


def place_rows(dst, blocks, me, at, first=0, width=None, lead=0):
    count, rows = blocks.shape[1:3]
    width = blocks.shape[3] - first if width is None else width
    for n in range(count):
        start = pl.multiple_of((n ^ me) * rows, rows) if count > 1 else 0
        dst[pl.ds(start, rows), at : at + width] = blocks[lead, n, :, first : first + width]


def place_pair(dst, mine, other, me):
    place_rows(dst, mine, me, 0)
    place_rows(dst, other, me, 384)


def place_p1(dst, am, bm, ar, br, me, pieces):
    place_rows(dst, am, me, 0)
    place_rows(dst, bm, me, 256, 0, 128)
    place_rows(dst, ar, me, 384)
    place_rows(dst, br, me, 640, 0, 128)
    place_rows(pieces, bm, me, 0, 128, 128)
    place_rows(pieces, br, me, 128, 128, 128)


def half_at(c, me_t):
    return pl.ds(pl.multiple_of(384 * (c ^ (me_t % 2)), 128), 384)


def k1_body(
    sc, tok, halo, gain, am, ar, bm, br, par, cbc, bbc,
    nrm, inx, blow, clow, bto, sin, dbc,
    cumo, stepo, sigo, eto, reacho, decayo, faco, uvo, masko, backo, ct,
    wbuf, wpc, pcs, dtacc, ext,
):
    g = pl.program_id(0)
    me_t, me_dp = sc[8], sc[9]

    @pl.when(g == 0)
    def _():
        def norm(v):
            v = v.astype(F32)
            r = lax.rsqrt(jnp.mean(v * v, axis=-1, keepdims=True) + EPS)
            return (v * r * gain[...]).astype(BF)

        @pl.loop(0, 16)
        def _(s):
            nrm[rows_of(s, 64)] = norm(tok[rows_of(s, 64)])

        nrm[4 * L :] = norm(halo[...])
        dtacc[...] = jnp.zeros_like(dtacc)
        sin[...] = jnp.zeros_like(sin)

    place_p1(wbuf, am, bm, ar, br, me_dp, wpc)
    for n in range(3):
        cols = slice(256 * n, 256 * n + 256)
        inx[0, :, cols] = dot(nrm[...], wbuf[:, cols]).astype(BF)
    pcs[...] = dot(nrm[...], wpc[...])

    for c in range(2):
        i = 2 * g + c
        t = i ^ me_t
        turn = 64 * (t % 2)

        @pl.loop(0, 4)
        def _(s):
            last = pcs[rows_of(s), tile(c)]
            lane = lane_iota(L)
            sin[t // 2, rows_of(s)] += pltpu.roll(jnp.where(lane < 64, last, 0.0), turn, 1)
            dtacc[...] += pltpu.roll(
                jnp.where(lane >= 64, last, 0.0), (s * SPAN + i * 6 + 64) % 128, 1
            )

        last = pcs[4 * L :, tile(c)]
        sin[t // 2, 4 * L :] += pltpu.roll(jnp.where(lane_iota(64) < 64, last, 0.0), turn, 1)

    @pl.when(g == 1)
    def _():
        dtb = jnp.zeros((1, 128), F32)
        alog = jnp.zeros((1, 128), F32)
        for i in range(4):
            for s in range(4):
                at = slice(384 * (i % 2), 384 * (i % 2) + 128)
                dtb += pltpu.roll(par[i // 2, 6:7, at], s * SPAN + i * 6, 1)
                alog += pltpu.roll(par[i // 2, 7:8, at], s * SPAN + i * 6, 1)
        raw = dtacc[...] + dtb
        step = jnp.maximum(raw, 0.0) + jnp.log1p(jnp.exp(-jnp.abs(raw)))
        sig = 1.0 / (1.0 + jnp.exp(-raw))
        decay = step * -jnp.exp(alog)
        lower = jnp.where(
            lax.broadcasted_iota(jnp.int32, (L, L), 0) >= lax.broadcasted_iota(jnp.int32, (L, L), 1),
            1.0,
            0.0,
        )
        cum = dot_high(lower, decay)
        row = row_iota(L, 128)
        lane = lane_iota(L)
        slot = lane // SPAN
        tail = jnp.zeros((L, 128), F32)
        enters = jnp.zeros((L, 128), F32)
        follows = jnp.zeros((8, 128), F32)
        masks = jnp.ones((L, 128), F32)
        row_b = row_iota(L + 8, 128) - 8
        lane_b = lane_iota(L + 8)
        back_masks = jnp.ones((L + 8, 128), F32)
        slot8 = lane_iota(8) // SPAN
        inner_block = jnp.where(me_t > 0, 1.0, 0.0)
        back = lane % 4
        for s in range(4):
            fe, se = ends(sc, s)
            seg = seg_of(row, fe, se)
            last = seg_of(L - 1, fe, se)
            before = seg_of(-1, fe, se)
            here = slot == s
            tail = jnp.where(here & (seg == last), 1.0, tail)
            enters = jnp.where(here & (seg == before), inner_block, enters)
            follows = jnp.where(
                (slot8 == s), jnp.where(last == before, inner_block, 0.0), follows
            )
            masks = jnp.where((lane // 4 == s) & (seg != seg_of(row - back, fe, se)), 0.0, masks)
            cut = seg_of(row_b, fe, se) != seg_of(row_b + lane_b % 4, fe, se)
            back_masks = jnp.where((lane_b // 4 == s) & cut, 0.0, back_masks)
        cum_last = cum[L - 1 : L]
        cum2 = cum * LOG2E
        cumo[...] = cum2
        stepo[...] = step
        sigo[...] = sig
        eto[...] = jnp.exp(cum_last - cum) * tail
        reacho[...] = jnp.exp(cum) * enters
        decayo[...] = decay
        faco[...] = jnp.exp(cum_last) * follows
        uvo[...] = jnp.exp2(-jnp.abs(cum2 - cum2[127:128]))
        masko[...] = masks
        backo[...] = back_masks
        ct[...] = cum2.T
        for q, low_out in ((0, blow), (1, clow)):
            taps = [cbc[k : k + 1, tile(q)] for k in range(4)]

            @pl.loop(0, 4)
            def _(s):
                ext[0:8] = sin[q, pl.ds(pl.multiple_of(4 * L + 16 * s + 8, 8), 8)]
                ext[8:] = sin[q, rows_of(s)]
                acc = conv_forward(ext, taps, bbc[:, tile(q)], slot_masks(masko, s))
                sg = sigmoid(acc)
                low = acc * sg
                low_out[rows_of(s)] = low.astype(BF)
                dbc[q, rows_of(s)] = sg + low * (1.0 - sg)
                if q == 0:
                    bto[rows_of(s, 128)] = low.T.astype(BF)


def factor_rows(fac, g):
    rows = []
    for s in range(4):
        f = to_lane0(fac[...], s, g)
        rows.append(jnp.concatenate([pair_cols(f, 2 * j)[0:1] for j in range(6)], axis=1))
    f = jnp.concatenate(rows, axis=0)
    high = f.astype(BF).astype(F32)
    return jnp.concatenate([high, f - high, jnp.zeros((8, WIDE), F32)], axis=0).astype(BF)


def k2_body(g, sc, inx, halo, par, bt, stepp, etp, fac, mask, *rest):
    xo, xso, dslo, sto, xe, ext, spread, stepx, stepe = rest[-9:]
    s = pl.program_id(0)
    me_t = sc[8]

    @pl.when(s == 0)
    def _():
        spread[...] = head_spread()

    masks = slot_masks(mask, s)
    step = to_lane0(stepp[...], s, g)
    expand(stepx, step, spread)
    expand(stepe, step * to_lane0(etp[...], s, g), spread)
    for j in range(6):
        ext[j, 0:8] = halo[0, :, tile(j)].astype(F32)[8:]
        ext[j, 8:] = inx[0, :, tile(j)].astype(F32)
    for n in range(L // CHUNK):
        r = slice(CHUNK * n, CHUNK * n + CHUNK)
        mr = [m[r] for m in masks]
        for j in range(6):
            taps = [0.5 * par[0, k : k + 1, tile(j)] for k in range(4)]
            half = conv_forward(ext.at[j], taps, 0.5 * par[0, 4:5, tile(j)], mr, CHUNK * n, CHUNK)
            th = jnp.tanh(half)
            up = 1.0 + th
            act = half * up
            xo[0, r, tile(j)] = act.astype(BF)
            dslo[0, r, tile(j)] = ((0.5 * up) * (1.0 + half * (1.0 - th))).astype(BF)
            xso[0, r, tile(j)] = (act * stepx[r, tile(j)]).astype(BF)
            xe[r, tile(j)] = (act * stepe[r, tile(j)]).astype(BF)
    for c in range(2):
        sto[rows_of(s, 128), half_at(c, me_t)] = dot(
            bt[...], xe[:, 384 * c : 384 * c + 384]
        ).astype(BF)

    @pl.when(s == 3)
    def _():
        f = factor_rows(fac, g)
        for c in range(2):
            sto[512:528, half_at(c, me_t)] = f[:, 384 * c : 384 * c + 384]


def by_head(pair):
    lane = lane_iota(128)
    zero = jnp.zeros_like(pair)
    return jnp.concatenate(
        [jnp.where(lane < HD, pair, zero), jnp.where(lane < HD, zero, pair)], axis=0
    )


def diag_mask(d, fe, se, key_rows):
    r = lax.broadcasted_iota(jnp.int32, (128, 128), 0) + 128 * d
    c = lax.broadcasted_iota(jnp.int32, (128, 128), 1) + 128 * d
    order = (c >= r) if key_rows else (r >= c)
    return order & (seg_of(r, fe, se) == seg_of(c, fe, se))


def cross_half(fe, se, key_rows):
    r = lax.broadcasted_iota(jnp.int32, (128, 128), 0) + (0 if key_rows else 128)
    c = lax.broadcasted_iota(jnp.int32, (128, 128), 1) + (128 if key_rows else 0)
    return seg_of(r, fe, se) == seg_of(c, fe, se)


def k3_body(g, sc, xs, blow, clow, cump, uvp, ct, *rest):
    within, scores, cross, spread, uvx, tiles, cumx = rest[-7:]
    s = pl.program_id(0)
    fe, se = sc[2 * s], sc[2 * s + 1]

    @pl.when(s == 0)
    def _():
        spread[...] = head_spread()
        tiles[...] = tile_spread()


    for d in range(2):
        r = slice(128 * d, 128 * d + 128)
        scores[d] = jnp.where(diag_mask(d, fe, se, False), dot_nt(clow[r], blow[r]), 0.0)
    cross[...] = jnp.where(cross_half(fe, se, False), dot_nt(clow[128:], blow[:128]), 0.0).astype(BF)

    expand_tiles(cumx, to_lane0(cump[...], s, g), tiles)
    expand(uvx, to_lane0(uvp[...], s, g), spread)
    for j in range(6):
        for d in range(2):
            r = slice(128 * d, 128 * d + 128)
            pair = xs[0, r, tile(j)]
            parts = []
            for b in range(2):
                h = 2 * j + b
                gap = cumx[r, tile(h)] - ct[pl.ds(s * SPAN + g * 12 + h, 1), :][:, r]
                parts.append((jnp.exp2(jnp.minimum(gap, 0.0)) * scores[d]).astype(BF))
            total = dot(jnp.concatenate(parts, axis=1), by_head(pair))
            if d == 1:
                xv = (xs[0, :128, tile(j)].astype(F32) * uvx[:128, tile(j)]).astype(BF)
                total = total + dot(cross[...], xv) * uvx[128:, tile(j)]
            within[0, r, tile(j)] = total


def k4_body(sc, nrm, cot, wzm, wzr, wom, wor, gate, dgn, dbro, wz, wo):
    g = pl.program_id(0)
    n = pl.program_id(1)
    me_dp = sc[9]

    @pl.when((g == 0) & (n == 0))
    def _():
        @pl.loop(0, 16)
        def _(n):
            s = n // 4
            r = rows_of(n, 64)
            keep = row_iota(64, 1) + 64 * (n % 4) < sc[2 * s + 1]
            dbro[r] = jnp.where(keep, cot[r].astype(F32), 0.0).astype(BF)

    @pl.when(n == 0)
    def _():
        place_pair(wz, wzm, wzr, me_dp)
        place_pair(wo, wom, wor, me_dp)

    cols = pl.ds(pl.multiple_of(n * 256, 256), 256)
    gate[0] = dot(nrm[0 : 4 * L], wz[:, cols]).astype(BF)
    dgn[0] = dot(dbro[...], wo[:, cols]).astype(BF)


def k5_body(
    sc, within, gate, dgn, x, r1, r2, r3, reachp, fac, clow, par, wom, wor, tok,
    out, gno, dgo, dyo, dpo, prevo, rowsum, dco, small,
    mo, sums, branch, wbuf, gnb, frow, dlow, seg_h, seg_l, pick, pv, spread, reachx,
):
    ph = pl.program_id(0)
    g = pl.program_id(1)
    s = pl.program_id(2)
    me_t, me_dp = sc[8], sc[9]
    r = rows_of(s)
    first = (g == 0) & (s == 0)

    @pl.when((ph == 0) & first)
    def _():
        rowsum[...] = jnp.zeros_like(rowsum)
        dco[...] = jnp.zeros_like(dco)
        small[...] = jnp.zeros_like(small)
        pick[...] = head_pick().astype(BF)
        spread[...] = head_spread()

    expand(reachx, to_lane0(reachp[...], s, g), spread)

    @pl.when(ph == 0)
    def _():
        srow = rows_of(s, 128)
        for c in range(2):
            at = half_at(c, me_t)
            frow[...] = r1[512:528, at].astype(F32)
            f = frow[pl.ds(s, 1)] + frow[pl.ds(s + 4, 1)]
            p = r1[srow, at].astype(F32) + r2[srow, at].astype(F32) + f * r3[srow, at].astype(F32)
            pv[:, 384 * c : 384 * c + 384] = p.astype(BF)
        prevo[g, srow] = pv[...]
        sq = jnp.zeros((L, 128), F32)
        dd = jnp.zeros((L, 128), F32)
        for j in range(6):
            from_prev = dot(clow[...], pv[:, tile(j)])
            mixed = (
                within[0, :, tile(j)]
                + reachx[:, tile(j)] * from_prev
                + par[0, 8:9, tile(j)] * x[0, :, tile(j)].astype(F32)
            )
            mo[g, r, tile(j)] = mixed
            gv = gate[0, :, tile(j)].astype(F32)
            gated = mixed * (gv * sigmoid(gv))
            sq = sq + gated * gated
            dd = dd + dgn[0, :, tile(j)].astype(F32) * par[0, 5:6, tile(j)] * gated
        sq = jnp.broadcast_to(jnp.sum(sq, axis=1, keepdims=True), (L, 128))
        dd = jnp.broadcast_to(jnp.sum(dd, axis=1, keepdims=True), (L, 128))

        @pl.when(g == 0)
        def _():
            sums[0, r] = sq
            sums[1, r] = dd

        @pl.when(g == 1)
        def _():
            sq2 = sums[0, r] + sq
            dd2 = sums[1, r] + dd
            gscale = lax.rsqrt(sq2 * (1.0 / INNER) + EPS)
            sums[0, r] = gscale
            sums[1, r] = gscale * gscale * gscale * (dd2 * (1.0 / INNER))

    @pl.when(ph == 1)
    def _():
        gscale = sums[0, r]
        coef = sums[1, r]
        srow = rows_of(s, 128)
        for j in range(6):
            gv = gate[0, :, tile(j)].astype(F32)
            mixed = mo[g, r, tile(j)]
            sg = sigmoid(gv)
            silu = gv * sg
            gated = mixed * silu
            gs = gated * gscale
            gain = par[0, 5:6, tile(j)]
            gn = (gs * gain).astype(BF)
            gno[0, :, tile(j)] = gn
            gnb[r, tile(j)] = gn
            d = dgn[0, :, tile(j)].astype(F32)
            small[g, 0:1, tile(j)] += jnp.sum(d * gs, axis=0, keepdims=True)
            dgated = gscale * (d * gain) - gated * coef
            dgo[0, :, tile(j)] = (dgated * mixed * (sg + silu * (1.0 - sg))).astype(BF)
            dy = (dgated * silu).astype(BF)
            dyo[0, :, tile(j)] = dy
            dyf = dy.astype(F32)
            dlow[:, tile(j)] = (dyf * reachx[:, tile(j)]).astype(BF)
            dx_skip = dyf * x[0, :, tile(j)].astype(F32)
            small[g, 1:2, tile(j)] += jnp.sum(dx_skip, axis=0, keepdims=True)
            v = dyf * mixed - par[0, 8:9, tile(j)] * dx_skip
            high = v.astype(BF)
            seg_h[:, tile(j)] = high
            seg_l[:, tile(j)] = (v - high.astype(F32)).astype(BF)
        seg = dot(seg_h[...], pick[...]) + dot(seg_l[...], pick[...])
        rowsum[...] += from_lane0(seg, s, g)
        dco[r] += dot_nt(dlow[...], prevo[g, srow])
        for c in range(2):
            dpo[srow, half_at(c, me_t)] = lax.dot_general(
                clow[...],
                dlow[:, 384 * c : 384 * c + 384],
                (((0,), (0,)), ((), ())),
                preferred_element_type=F32,
            ).astype(BF)

        @pl.when(s == 3)
        def _():
            f = factor_rows(fac, g)
            for c in range(2):
                dpo[512:528, half_at(c, me_t)] = f[:, 384 * c : 384 * c + 384]
            place_pair(wbuf, wom, wor, me_dp)

        @pl.when((s == 3) & (g == 0))
        def _():
            branch[...] = dot_nt(gnb[...], wbuf[...])

        @pl.when((s == 3) & (g == 1))
        def _():
            branch[...] += dot_nt(gnb[...], wbuf[...])

            @pl.loop(0, 16)
            def _(n):
                q = rows_of(n, 64)
                out[q] = (tok[q].astype(F32) + branch[q]).astype(BF)


def store_grad(ref, lead, me_dp, value_ref, first, width, at=0):
    count, rows = ref.shape[-3], ref.shape[-2]
    for n in range(count):
        place = n ^ me_dp if count > 1 else 0
        part = value_ref[n * rows : (n + 1) * rows, first : first + width].astype(BF)
        ref[lead + (place, slice(None), slice(at, at + width))] = part


def add_weighted(total, val, w, lead=()):
    @pl.loop(0, total.shape[0] // 64)
    def _(n):
        r = rows_of(n, 64)
        part = total[r]
        for j in range(w.shape[1] // 128):
            v = val[j, r] if lead else val[r, tile(j)]
            part = part + v * w[r, tile(j)].astype(F32)
        total[r] = part


def k6_body(sc, nrm, dbr, gn, dg, wzm, wzr, ok, os, zk, zs, nt, ngz, dt, val, wz):
    g = pl.program_id(0)
    me_dp = sc[9]
    place_pair(wz, wzm, wzr, me_dp)

    @pl.when(g == 0)
    def _():
        ngz[...] = jnp.zeros_like(ngz)

        @pl.loop(0, 4)
        def _(s):
            nt[:, rows_of(s)] = nrm[rows_of(s)].T
            dt[:, rows_of(s)] = dbr[rows_of(s)].T

        nt[:, 4 * L :] = nrm[4 * L :].T

    for lhs, rhs, keep, send in ((dt, gn, ok, os), (nt, dg, zk, zs)):
        for n in range(3):
            cols = slice(256 * n, 256 * n + 256)
            val[:, cols] = dot(lhs[:, : 4 * L], rhs[0, :, cols])
        store_grad(keep, (0,), me_dp, val, 0, 384)
        store_grad(send, (0,), me_dp, val, 384, 384)
    add_weighted(ngz, val, wz)


def k7_body(g, sc, xs, dy, blow, clow, cump, uvp, ct, *rest):
    dxo, bco, pko, scores, cross, xvb, udb, spread, uvx, tiles, cumx, pick, corr = rest[-13:]
    s = pl.program_id(0)

    @pl.when(s == 0)
    def _():
        spread[...] = head_spread()
        tiles[...] = tile_spread()
        pick[...] = head_pick().astype(BF)
        pko[...] = jnp.zeros_like(pko)

    fe, se = sc[2 * s], sc[2 * s + 1]

    for d in range(2):
        r = slice(128 * d, 128 * d + 128)
        scores[d] = jnp.where(diag_mask(d, fe, se, True), dot_nt(blow[r], clow[r]), 0.0)
    cross[...] = jnp.where(cross_half(fe, se, True), dot_nt(blow[:128], clow[128:]), 0.0).astype(BF)

    expand_tiles(cumx, to_lane0(cump[...], s, g), tiles)
    expand(uvx, to_lane0(uvp[...], s, g), spread)
    totals = [jnp.zeros((128, 128), F32), jnp.zeros((128, 128), F32)]
    crossq = cross[...].astype(F32).T.astype(BF)
    for j in range(6):
        for d in range(2):
            r = slice(128 * d, 128 * d + 128)
            xp = xs[0, r, tile(j)]
            dyp = dy[0, r, tile(j)]
            grads = dot_nt(by_head(xp), dyp)
            parts = []
            for b in range(2):
                h = 2 * j + b
                gap = ct[pl.ds(s * SPAN + g * 12 + h, 1), :][:, r] - cumx[r, tile(h)]
                kern = jnp.exp2(jnp.minimum(gap, 0.0))
                totals[d] = totals[d] + grads[128 * b : 128 * b + 128] * kern
                parts.append((kern * scores[d]).astype(BF))
            dx = dot(jnp.concatenate(parts, axis=1), by_head(dyp))
            scaled = (xp if d == 0 else dyp).astype(F32) * uvx[r, tile(j)]
            low = scaled.astype(BF)
            diff = low.astype(F32) - scaled
            if d == 0:
                xvb[:, tile(j)] = low
                top, xdiff = dx, diff
            else:
                udb[:, tile(j)] = low
                off = dot(cross[...], low)
                dxo[0, r, tile(j)] = dx
                dxo[0, :128, tile(j)] = top + off * uvx[:128, tile(j)]
                corr[:128, tile(j)] = (xdiff * off).astype(BF)
                corr[128:, tile(j)] = (diff * dot(crossq, xvb[:, tile(j)])).astype(BF)
    dcr = dot_nt(xvb[...], udb[...])
    pko[...] += from_lane0(dot(corr[...], pick[...]), s, g)
    d0 = jnp.where(diag_mask(0, fe, se, True), totals[0], 0.0)
    d1 = jnp.where(diag_mask(1, fe, se, True), totals[1], 0.0)
    dl = jnp.where(cross_half(fe, se, True), dcr, 0.0)
    c0, c1, b0, b1 = clow[:128], clow[128:], blow[:128], blow[128:]
    bco[0, 0:128] = dot(d0.astype(BF), c0) + dot(dl.astype(BF), c1)
    bco[0, 128:] = dot(d1.astype(BF), c1)
    bco[1, 0:128] = dot(d0.T.astype(BF), b0)
    bco[1, 128:] = dot(d1.T.astype(BF), b1) + dot(dl.T.astype(BF), b0)


def k8_body(
    g, last, sc, nt, xs, dy, dsl, inx, halo, dxw, q1, q2, q3, prev, blow, stepp, etp, back, par,
    am, ar, bm, br, *rest,
):
    if last:
        (
            fac, sigp, decay, gain, ngz, nga, cbc, bc7a, bc7b, corr_a, corr_b, dc3, rowsum, sin, dbc, sega, enda, dba,
            keep, send, din, seg, end, dba_o, small, ngx, din5, sbc, sdt, ngo,
            val, hsum, gsc, gf, glow, xe, seg_h, seg_l, pick, wbuf, wpc, gbuf, pcs, pblk, ub, ext, spread, stepx, etx,
        ) = rest
    else:
        (
            keep, send, din, seg, end, dba_o, small, ngx,
            val, hsum, gsc, gf, glow, xe, seg_h, seg_l, pick, wbuf, ub, ext, spread, stepx, etx,
        ) = rest
    s = pl.program_id(0)
    me_t, me_dp = sc[8], sc[9]
    r = rows_of(s)
    hrow = pl.ds(pl.multiple_of(4 * L + 16 * s, 16), 16)

    @pl.when(s == 0)
    def _():
        seg[...] = jnp.zeros_like(seg)
        end[...] = jnp.zeros_like(end)
        small[...] = jnp.zeros_like(small)
        pick[...] = head_pick().astype(BF)
        ext[:, 0:8] = jnp.zeros((6, 8, 128), F32)
        ext[:, 264:] = jnp.zeros((6, 8, 128), F32)
        spread[...] = head_spread()

    srow = rows_of(s, 128)
    for c in range(2):
        at = half_at(c, me_t)
        gf[...] = q1[512:528, at].astype(F32)
        f = gf[pl.ds(s, 1)] + gf[pl.ds(s + 4, 1)]
        v = q1[srow, at].astype(F32) + q2[srow, at].astype(F32) + f * q3[srow, at].astype(F32)
        gsc[:, 384 * c : 384 * c + 384] = v
        glow[:, 384 * c : 384 * c + 384] = v.astype(BF)
    for n in range(3):
        cols = slice(256 * n, 256 * n + 256)
        ub[:, cols] = dot(blow[...], glow[:, cols])
    masks = slot_masks(back, s)
    expand(stepx, to_lane0(stepp[...], s, g), spread)
    expand(etx, to_lane0(etp[...], s, g), spread)
    ends_row, gp_row = [], []
    for j in range(6):
        taps = [par[0, k : k + 1, tile(j)] for k in range(4)]
        xf = xs[0, :, tile(j)].astype(F32)
        ec = etx[:, tile(j)]
        eu = ub[:, tile(j)] * ec
        xe[:, tile(j)] = (xf * ec).astype(BF)
        ends_row.append(jnp.sum(xf * eu, axis=0, keepdims=True))
        gp_row.append(
            jnp.sum(gsc[:, tile(j)] * prev[0, srow, tile(j)].astype(F32), axis=0, keepdims=True)
        )
        dxi = dxw[0, :, tile(j)] + eu
        v = xf * dxi
        high = v.astype(BF)
        seg_h[:, tile(j)] = high
        seg_l[:, tile(j)] = (v - high.astype(F32)).astype(BF)
        dx = dxi * stepx[:, tile(j)] + par[0, 8:9, tile(j)] * dy[0, :, tile(j)].astype(F32)
        dconv = dx * dsl[0, :, tile(j)].astype(F32)
        small[4:5, tile(j)] += jnp.sum(dconv, axis=0, keepdims=True)
        v_ext = jnp.concatenate(
            [halo[0, :, tile(j)].astype(F32)[8:], inx[0, :, tile(j)].astype(F32)], axis=0
        )
        ext[j, 8:264] = dconv
        dv, tap_grads = conv_backward(ext.at[j], v_ext, taps, masks)
        for k in range(4):
            small[k : k + 1, tile(j)] += tap_grads[k]
        din[r, tile(j)] = dv[8:].astype(BF)
        din[hrow, tile(j)] = jnp.concatenate([jnp.zeros((8, 128), F32), dv[:8]], axis=0).astype(BF)
    seg[...] += from_lane0(dot(seg_h[...], pick[...]) + dot(seg_l[...], pick[...]), s, g)
    dba_o[r] = dot_nt(xe[...], glow[...])
    rows = jnp.concatenate(
        [
            jnp.concatenate(ends_row, axis=1),
            jnp.concatenate(gp_row, axis=1),
            jnp.zeros((6, WIDE), F32),
        ],
        axis=0,
    )
    end[...] += from_lane0(dot_high(rows, pick[...].astype(F32)), s, g)

    @pl.when(s == 3)
    def _():
        for n in range(3):
            cols = slice(256 * n, 256 * n + 256)
            hsum[...] = dot(nt[:, 4 * L :], din[4 * L :, cols])
            val[:, cols] = dot(nt[:, : 4 * L], din[: 4 * L, cols]) + hsum[...]
        store_grad(keep, (), me_dp, val, 0, 384)
        store_grad(send, (), me_dp, val, 384, 384)
        place_rows(wbuf, am, me_dp, 0)
        place_rows(wbuf, ar, me_dp, 384)
        place_rows(wbuf, bm, me_dp, 256, 0, 128, g if last else 0)
        place_rows(wbuf, br, me_dp, 640, 0, 128, g if last else 0)
        ngx[...] = ngz[...] + nga[...] if last else jnp.zeros_like(ngx)
        add_weighted(ngx, val, wbuf)

    if not last:
        return

    @pl.when(s == 3)
    def _():
        for q in range(2):
            taps = [cbc[k : k + 1, tile(q)] for k in range(4)]
            sbc[q] = jnp.zeros((8, 128), F32)

            @pl.loop(0, 4)
            def _(n):
                rn = rows_of(n)
                if q == 0:
                    grad = bc7a[0, rn] + bc7b[0, rn] + dba_o[rn] + dba[rn]
                else:
                    grad = bc7a[1, rn] + bc7b[1, rn] + dc3[rn]
                dconv = grad * dbc[q, rn]
                hn = pl.ds(pl.multiple_of(4 * L + 16 * n, 16), 16)
                v_ext = jnp.concatenate([sin[q, hn][8:], sin[q, rn]], axis=0)
                ext[q, 8:264] = dconv
                dv, tap_grads = conv_backward(ext.at[q], v_ext, taps, slot_masks(back, n))
                sbc[q, 4:5] += jnp.sum(dconv, axis=0, keepdims=True)
                for k in range(4):
                    sbc[q, k : k + 1] += tap_grads[k]
                gbuf[q, rn] = dv[8:]
                gbuf[q, hn] = jnp.concatenate([jnp.zeros((8, 128), F32), dv[:8]], axis=0)

        row = row_iota(L, 128)
        corr = corr_a[...] + corr_b[...]
        col = seg[...] + sega[...] + jnp.where(row < 128, corr, 0.0)
        ends_all = end[...] + enda[...]
        at_last = ends_all[0:1] + ends_all[1:2] * fac[0:1]
        dcum = rowsum[...] + jnp.where(row < 128, 0.0, corr) - col + jnp.where(row == L - 1, at_last, 0.0)
        upper = jnp.where(
            lax.broadcasted_iota(jnp.int32, (L, L), 0) <= lax.broadcasted_iota(jnp.int32, (L, L), 1),
            1.0,
            0.0,
        )
        dlog = dot_high(upper, dcum)
        alog = jnp.zeros((1, 128), F32)
        for i in range(4):
            at = slice(384 * (i % 2), 384 * (i % 2) + 128)
            for n in range(4):
                alog += pltpu.roll(par[i // 2, 7:8, at], n * SPAN + i * 6, 1)
        step_all, sig = stepp[...], sigp[...]
        ratio = jnp.where(step_all > 1e-30, sig / jnp.maximum(step_all, 1e-30), 1.0)
        ddt = ratio * col - sig * jnp.exp(alog) * dlog
        sdt[...] = jnp.concatenate(
            [
                jnp.sum(ddt, axis=0, keepdims=True),
                jnp.sum(dlog * decay[...], axis=0, keepdims=True),
                jnp.zeros((6, 128), F32),
            ],
            axis=0,
        )
        for n in range(4):
            t = n ^ me_t
            turn = (64 * (t % 2)) % 128

            @pl.loop(0, 4)
            def _(m):
                rm = rows_of(m)
                lane = lane_iota(L)
                a = pltpu.roll(gbuf[t // 2, rm], turn, 1)
                d = pltpu.roll(ddt, (320 - m * SPAN - n * 6) % 128, 1)
                piece = jnp.where(lane < 64, a, jnp.where(lane < 70, d, 0.0))
                din5[rm, tile(n)] = piece.astype(BF)

            a = pltpu.roll(gbuf[t // 2, 4 * L :], turn, 1)
            din5[4 * L :, tile(n)] = jnp.where(lane_iota(64) < 64, a, 0.0).astype(BF)
        for n in range(2):
            cols = slice(256 * n, 256 * n + 256)
            hsum[...] = dot(nt[:, 4 * L :], din5[4 * L :, cols])
            v = dot(nt[:, : 4 * L], din5[: 4 * L, cols]) + hsum[...]
            pcs[2 * n] = v[:, :128]
            pcs[2 * n + 1] = v[:, 128:]
            place_rows(wpc, bm, me_dp, 256 * n, 128, 128, n)
            place_rows(wpc, br, me_dp, 256 * n + 128, 128, 128, n)
        add_weighted(ngx, pcs, wpc, (0,))
        ngo[...] = (
            lax.dot_general(
                jnp.ones((8, 128), F32),
                ngx[...],
                (((1,), (1,)), ((), ())),
                preferred_element_type=F32,
                precision=lax.Precision.HIGHEST,
            )
            / gain[...]
        )
        count, brow = keep.shape[0], keep.shape[1]
        for n in range(4):
            ref = keep if n % 2 == 0 else send
            at = slice(384 + 128 * (n // 2), 512 + 128 * (n // 2))
            if count == 1:
                ref[0, :, at] = pcs[n].astype(BF)
                continue
            t = n ^ me_t
            quarter = brow // 4
            for m in range(count):
                for c in range(4):
                    pblk[quarter * c : quarter * c + quarter] = pcs[
                        c ^ me_t, pl.ds(pl.multiple_of(brow * m + quarter * t, 8), quarter)
                    ]
                both = jnp.where(
                    lane_iota(brow) < 64, pblk[...], pcs[n, brow * m : brow * m + brow]
                )
                ref[m ^ me_dp, :, at] = both.astype(BF)


def k9z_body(sc, dg, wzm, wzr, dn, wz):
    place_pair(wz, wzm, wzr, sc[9])
    dn[...] = dot_nt(dg[0], wz[...])


def k9_body(sc, din0, din1, din5, dna, dnb, am, ar, bm, br, dn, wx, wpc):
    g = pl.program_id(0)
    place_p1(wx, am, bm, ar, br, sc[9], wpc)

    @pl.when(g == 0)
    def _():
        dn[...] = dot_nt(din0[...], wx[...])

    @pl.when(g == 1)
    def _():
        dn[...] += dot_nt(din1[...], wx[...])
        dn[: 4 * L] += dna[...] + dnb[...]

    dn[...] += dot_nt(din5[...], wpc[...])


def k10_body(sc, dn, hr, tok, cot, gain, ig):
    s = pl.program_id(0)
    d = dn[...]
    extra = hr[...].astype(F32)
    width = d.shape[1]
    d = jnp.concatenate([d[: L - 16], d[L - 16 :] + extra], axis=0)
    tv = tok[...].astype(F32)
    r = lax.rsqrt(jnp.mean(tv * tv, axis=-1, keepdims=True) + EPS)
    tr = tv * r
    gd = gain[...] * d
    inner = jnp.sum(gd * tr, axis=-1, keepdims=True) * (1.0 / width)
    keep = row_iota(L, 1) < sc[2 * s + 1]
    res = jnp.where(keep, cot[...].astype(F32), 0.0)
    ig[...] = (res + r * (gd - tr * inner)).astype(BF)


def full(shape):
    return pl.BlockSpec(shape, lambda *a: (0,) * len(shape))


def call(body, grid, in_specs, out_specs, out_shapes, scratch, cost, name, aliases=None, vmem_mib=VMEM_MIB):
    flops, moved = cost
    return pl.pallas_call(
        body,
        grid_spec=pltpu.PrefetchScalarGridSpec(
            num_scalar_prefetch=1,
            grid=grid,
            in_specs=in_specs,
            out_specs=out_specs,
            scratch_shapes=scratch,
        ),
        out_shape=out_shapes,
        compiler_params=pltpu.CompilerParams(vmem_limit_bytes=vmem_mib * 2**20),
        cost_estimate=pl.CostEstimate(flops=flops, bytes_accessed=moved, transcendentals=0),
        input_output_aliases=aliases or {},
        name=name,
    )


def sds(shape, dtype):
    return pltpu.HBM(shape, dtype)


def anywhere(count):
    return [pl.BlockSpec(memory_space=pl.ANY)] * count


def flip(value, axis, bit):
    count = lax.axis_size(axis)
    return lax.ppermute(value, axis, [(a, a ^ bit) for a in range(count)])


def meet(*values):
    return lax.optimization_barrier(values)


def per_device(
    tokens, lengths, cotangent, norm_gain, w_z, w_x, w_bc, w_dt, conv_x, bias_x, conv_bc, bias_bc,
    dt_bias, a_log, skip_d, out_gain, w_out,
):
    tcount = lax.axis_size("tensor")
    dpcount = lax.axis_size("dp")
    me_t = lax.axis_index("tensor")
    me_dp = lax.axis_index("dp")
    slots, own_len, dim = tokens.shape
    rows = slots * own_len
    shard = w_z.shape[0]
    cols = w_z.shape[1]
    heads = w_dt.shape[1]
    fast = shard % 32 == 0 and dpcount & (dpcount - 1) == 0 and dpcount >= 8
    count = dpcount if fast else 1
    brow = shard if fast else dim

    first = lengths[:, 0] - me_t * own_len
    second = first + lengths[:, 1]
    sc = jnp.concatenate(
        [
            jnp.stack([first, second], axis=1).reshape(-1),
            jnp.stack([me_t, me_dp]),
            jnp.zeros((6,), jnp.int32),
        ]
    ).astype(jnp.int32)
    tok = tokens.reshape(rows, dim)
    cot = cotangent.reshape(rows, dim)
    gain = norm_gain.reshape(1, dim)

    bq = w_bc.shape[1] // tcount
    state = w_bc.shape[1] // 2
    own_bc = lax.dynamic_slice_in_dim(w_bc, me_t * bq, bq, 1)
    p1 = jnp.concatenate(
        [w_x, own_bc, w_dt, jnp.zeros((shard, 128 - bq - heads), BF)], axis=1
    )
    tail = tokens[:, own_len - 16 :, :].reshape(slots * 16, dim)
    def add_y(v, at):
        return jnp.stack([v, flip(v, "dp", 1)], axis=at)

    def add_x(v):
        return jnp.stack([v, flip(v, "tensor", 2)], axis=0)

    def blocks(v):
        return v.reshape(2, count, brow, v.shape[-1])

    def core(v):
        return flip(v, "tensor", 1)

    par = jnp.concatenate(
        [
            conv_x,
            bias_x[None],
            out_gain[None],
            jnp.pad(dt_bias, (0, cols - heads))[None],
            jnp.pad(a_log, (0, cols - heads))[None],
            jnp.repeat(skip_d, cols // heads)[None],
            jnp.zeros((7, cols), F32),
        ],
        axis=0,
    )
    bbc = bias_bc.reshape(1, -1)

    def grown(v, got, at):
        v = jnp.stack([v, got], axis=at)
        return v.reshape(v.shape[: at - 1] + (-1,) + v.shape[at + 1 :])

    if fast:
        v = p1[None]
        w2 = jnp.stack([w_z, w_out])[None]
        bit = dpcount // 2
        got = flip(v, "dp", bit)
        got, w2, sc, par, tail, gain = meet(got, w2, sc, par, tail, gain)
        v = grown(v, got, 1)
        while bit > 4:
            bit //= 2
            v = grown(v, flip(v, "dp", bit), 1)
            w2 = grown(w2, flip(w2, "dp", 2 * bit), 1)
        halo = lax.ppermute(tail, "tensor", [(a, a + 1) for a in range(tcount - 1)])
        got, w2, parx, halo = meet(flip(v, "dp", 2), w2, flip(par, "tensor", 2), halo)
        par = jnp.stack([par, parx], axis=0)
        v = grown(v, got, 1)
        az, bz = v[..., :256], v[..., 256:]
        ax, by, parc, w2z = meet(
            flip(az, "tensor", 2), flip(bz, "dp", 1), core(par), flip(w2, "dp", 4)
        )
        w2 = grown(w2, w2z, 1)
        par = jnp.concatenate([par, parc], axis=-1)
        ax = jnp.stack([az, ax], axis=0)
        by = jnp.stack([bz, by], axis=1)
        ay, bx, w2z, par = meet(flip(ax, "dp", 1), flip(by, "tensor", 2), flip(w2, "dp", 2), par)
        w2 = grown(w2, w2z, 1)
        wam = blocks(jnp.stack([ax, ay], axis=2))
        wbm = blocks(jnp.stack([by, bx], axis=0))
        zz, oz = w2[:, 0], w2[:, 1]
        zx, oy = flip(zz, "tensor", 2), flip(oz, "dp", 1)
        war, wbr = core(wam), core(wbm)
    else:
        halo = lax.ppermute(tail, "tensor", [(a, a + 1) for a in range(tcount - 1)])
        par = add_x(par)
        par = jnp.concatenate([par, core(par)], axis=-1)
        z1 = lax.all_gather(p1, "dp", axis=0, tiled=True)[None]
        wam = add_x(z1[..., :256])
        wbm = add_x(z1[..., 256:])
        war, wbr = core(wam), core(wbm)

    srows = slots * state
    wide = 2 * cols
    erows = rows + 64
    p1block = (1, count, brow, 256)
    wblock = (1, count, brow, cols)
    vmem = pltpu.VMEM

    def w_g(g, *a):
        return (g, 0, 0, 0)

    nrm, inx, blow, clow, bt, sin, dbc, cump, stepp, sigp, etp, reachp, decay, fac, uvp, mask, back, ct = call(
        k1_body,
        (2,),
        [full((rows, dim)), full((64, dim)), full((1, dim))]
        + [pl.BlockSpec(p1block, w_g)] * 4
        + [full((2, 16, wide)), full((4, 2 * state)), full((1, 2 * state))],
        [
            full((erows, dim)),
            pl.BlockSpec((1, erows, wide), lambda g, sc: (g, 0, 0)),
            full((rows, state)),
            full((rows, state)),
            full((srows, L)),
            full((2, erows, state)),
            full((2, rows, state)),
        ]
        + [full((L, 128))] * 6
        + [full((8, 128)), full((L, 128)), full((L, 128)), full((L + 8, 128)), full((128, L))],
        [
            sds((erows, dim), BF),
            sds((2, erows, wide), BF),
            sds((rows, state), BF),
            sds((rows, state), BF),
            sds((srows, L), BF),
            sds((2, erows, state), F32),
            sds((2, rows, state), F32),
        ]
        + [sds((L, 128), F32)] * 6
        + [sds((8, 128), F32), sds((L, 128), F32), sds((L, 128), F32), sds((L + 8, 128), F32)]
        + [sds((128, L), F32)],
        [
            vmem((dim, wide), BF),
            vmem((dim, 256), BF),
            vmem((erows, 256), F32),
            vmem((L, 128), F32),
            vmem((L + 8, 128), F32),
        ],
        (int(7e9), int(2e7)),
        "projections",
    )(sc, tok, halo, gain, wam, war, wbm, wbr, par, conv_bc, bbc)

    def gs(g, s, sc):
        return (g, s, 0)

    def halo_gs(g, s, sc):
        return (g, rows // 16 + s, 0)

    def by_s(g, s, sc):
        return (s, 0)

    def mirror(g, sc):
        return (0, g ^ (sc[8] // 2))

    group = (1, L, wide)

    def gsel(g):
        return lambda s, sc: (g, s, 0)

    def conv_and_states(g, inx, kept):
        return call(
            functools.partial(k2_body, g),
            (slots,),
            [
                pl.BlockSpec(group, gsel(g)),
                pl.BlockSpec((1, 16, wide), lambda s, sc: (g, rows // 16 + s, 0)),
                pl.BlockSpec((1, 16, wide), lambda s, sc: (g, 0, 0)),
                pl.BlockSpec((state, L), lambda s, sc: (s, 0)),
                full((L, 128)),
                full((L, 128)),
                full((8, 128)),
                full((L, 128)),
            ]
            + anywhere(len(kept)),
            [pl.BlockSpec(group, gsel(g))] * 3
            + [pl.BlockSpec((srows + 16, wide), lambda s, sc: mirror(g, sc))],
            [sds((2, rows, wide), BF)] * 3 + [sds((srows + 16, 2 * wide), BF)],
            [
                vmem((L, wide), BF),
                vmem((6, L + 8, 128), F32),
                vmem((256, wide), BF),
                vmem((L, wide), F32),
                vmem((L, wide), F32),
            ],
            (int(5e9) if g else 1, int(2e7) if g else 1),
            "conv_and_states_%d" % g,
            {9 + n: n for n in range(len(kept))},
        )(sc, inx, inx, par, bt, stepp, etp, fac, mask, *kept)

    if fast:
        inx0, zx, oy = meet(inx, zx, oy)
        zx = jnp.stack([zz, zx], axis=0)
        oy = jnp.stack([oz, oy], axis=1)
        zy, ox = flip(zx, "dp", 1), flip(oy, "tensor", 2)
        xl, xs, dsl, st = conv_and_states(1, inx, conv_and_states(0, inx0, []))
        st, zy, ox = meet(st, zy, ox)
        wzm = blocks(jnp.stack([zx, zy], axis=2))
        wom = blocks(jnp.stack([oy, ox], axis=0))
        wzr, wor = core(wzm), core(wom)
    else:
        xl, xs, dsl, st = conv_and_states(1, inx, conv_and_states(0, inx, []))
        wzm = add_x(lax.all_gather(w_z, "dp", axis=0, tiled=True)[None])
        wom = add_x(lax.all_gather(w_out, "dp", axis=0, tiled=True)[None])
        wzr, wor = core(wzm), core(wom)

    def end_state(mine, one):
        f = mine[srows : srows + 4].astype(F32) + mine[srows + 4 : srows + 8].astype(F32)
        width = mine.shape[1]
        end = mine[:srows].astype(F32).reshape(slots, state, width) + f[:, None] * one[
            :srows
        ].astype(F32).reshape(slots, state, width)
        return end.astype(BF).reshape(srows, width)

    r1 = lax.ppermute(st, "tensor", [(0, 1), (2, 3)])
    end = end_state(st, r1)
    r2 = lax.ppermute(end, "tensor", [(1, 2)])
    xs3, _ = meet(xs, end)

    def within_of(g, kept):
        return call(
            functools.partial(k3_body, g),
            (slots,),
            [
                pl.BlockSpec(group, gsel(g)),
                pl.BlockSpec((L, state), lambda s, sc: (s, 0)),
                pl.BlockSpec((L, state), lambda s, sc: (s, 0)),
                full((L, 128)),
                full((L, 128)),
                full((128, L)),
            ]
            + anywhere(len(kept)),
            pl.BlockSpec(group, gsel(g)),
            sds((2, rows, wide), F32),
            [
                vmem((2, 128, 128), F32),
                vmem((128, 128), BF),
                vmem((256, wide), BF),
                vmem((L, wide), F32),
                vmem((256, 2 * wide), BF),
                vmem((L, 2 * wide), F32),
            ],
            (int(5e9), int(1e7)),
            "within_%d" % g,
            {7 + n: n for n in range(len(kept))},
        )(sc, xs3, blow, clow, cump, uvp, ct, *kept)

    within = within_of(1, [within_of(0, [])])
    nrm4, within = meet(nrm, within)

    gate, dgn, dbr = call(
        k4_body,
        (2, 3),
        [full((erows, dim)), full((rows, dim))] + [pl.BlockSpec(wblock, w_g)] * 4,
        [pl.BlockSpec((1, rows, 256), lambda g, n, sc: (g, 0, n))] * 2 + [full((rows, dim))],
        [sds((2, rows, wide), BF)] * 2 + [sds((rows, dim), BF)],
        [vmem((dim, wide), BF), vmem((dim, wide), BF)],
        (int(5e9), int(2e7)),
        "gate_and_out_backward",
    )(sc, nrm4, cot, wzm, wzr, wom, wor)

    gate, r2 = meet(gate, r2)
    r3 = lax.ppermute(r2, "tensor", [(2, 3)])

    def p_gs(phase):
        def index(p, g, s, sc):
            return (
                jnp.where(p == phase, g, 0 if phase else 1),
                jnp.where(p == phase, s, 0 if phase else slots - 1),
                0,
            )

        return index

    def p_mirror(phase):
        def index(p, g, s, sc):
            return mirror(jnp.where(p == phase, g, 0 if phase else 1), sc)

        return index

    def pgs(p, g, s, sc):
        return (g, s, 0)

    def p_w(p, g, s, sc):
        return (jnp.where(p == 1, g, 0), 0, 0, 0)

    out, gn, dg, dy, dp, prev, rowsum, dc5, small5 = call(
        k5_body,
        (2, 2, slots),
        [
            pl.BlockSpec(group, p_gs(0)),
            pl.BlockSpec(group, pgs),
            pl.BlockSpec(group, pgs),
            pl.BlockSpec(group, pgs),
            pl.BlockSpec((srows + 16, wide), p_mirror(0)),
            pl.BlockSpec((srows, wide), p_mirror(0)),
            pl.BlockSpec((srows, wide), p_mirror(0)),
            full((L, 128)),
            full((8, 128)),
            pl.BlockSpec((L, state), lambda p, g, s, sc: (s, 0)),
            pl.BlockSpec((1, 16, wide), lambda p, g, s, sc: (g, 0, 0)),
            pl.BlockSpec(wblock, p_w),
            pl.BlockSpec(wblock, p_w),
            full((rows, dim)),
        ],
        [
            full((rows, dim)),
            pl.BlockSpec(group, p_gs(1)),
            pl.BlockSpec(group, p_gs(1)),
            pl.BlockSpec(group, p_gs(1)),
            pl.BlockSpec((srows + 16, wide), p_mirror(1)),
            full((2, srows, wide)),
            full((L, 128)),
            full((rows, state)),
            full((2, 8, wide)),
        ],
        [
            sds((rows, dim), BF),
            sds((2, rows, wide), BF),
            sds((2, rows, wide), BF),
            sds((2, rows, wide), BF),
            sds((srows + 16, 2 * wide), BF),
            sds((2, srows, wide), BF),
            sds((L, 128), F32),
            sds((rows, state), F32),
            sds((2, 8, wide), F32),
        ],
        [
            vmem((2, rows, wide), F32),
            vmem((2, rows, 128), F32),
            vmem((rows, dim), F32),
            vmem((dim, wide), BF),
            vmem((rows, wide), BF),
            vmem((16, cols), F32),
            vmem((L, wide), BF),
            vmem((L, wide), BF),
            vmem((L, wide), BF),
            vmem((wide, 128), BF),
            vmem((state, wide), BF),
            vmem((256, wide), BF),
            vmem((L, wide), F32),
        ],
        (int(1.5e10), int(4e7)),
        "gated_norm",
        vmem_mib=K5_MIB,
    )(sc, within, gate, dgn, xl, r1, r2, r3, reachp, fac, clow, par, wom, wor, tok)

    q1 = lax.ppermute(dp, "tensor", [(1, 0), (3, 2)])

    gshape = (2, count, brow, cols)
    ok, osend, zk, zsend, nt, ngz = call(
        k6_body,
        (2,),
        [full((erows, dim)), full((rows, dim))]
        + [pl.BlockSpec((1, rows, wide), lambda g, sc: (g, 0, 0))] * 2
        + [pl.BlockSpec(wblock, w_g)] * 2,
        [pl.BlockSpec((1,) + gshape[1:], w_g)] * 4 + [full((dim, erows)), full((dim, 128))],
        [sds(gshape, BF)] * 4 + [sds((dim, erows), BF), sds((dim, 128), F32)],
        [vmem((dim, rows), BF), vmem((dim, wide), F32), vmem((dim, wide), BF)],
        (int(5e9), int(2e7)),
        "outer_weight_grads",
    )(sc, nrm, dbr, gn, dg, wzm, wzr)

    osend, q1 = meet(osend, q1)
    dy1, end = meet(dy, end_state(dp, q1))
    q2 = lax.ppermute(end, "tensor", [(2, 1)])

    def summed(a, b):
        return (a.astype(F32) + b.astype(F32)).astype(BF)

    def reduce_step(v, axis, mesh_axis, bit):
        keep = lax.index_in_dim(v, 0, axis, False)
        send = lax.index_in_dim(v, 1, axis, False)
        return summed(keep, flip(send, mesh_axis, bit))

    def reduce_x(v, axis):
        return reduce_step(v, axis, "tensor", 2)

    def reduce_dp(v, bit):
        v = v.reshape((v.shape[0] // 2, 2) + v.shape[1:])
        return reduce_step(v, 1, "dp", bit)

    def finish(v, bit):
        while bit < dpcount:
            v = reduce_dp(v, bit)
            bit *= 2
        return v[0].astype(F32)

    def reduce_slow(v):
        v = v.reshape(dpcount, shard, v.shape[-1])
        got = lax.all_to_all(v, "dp", split_axis=0, concat_axis=0, tiled=True)
        return got.astype(F32).sum(axis=0)

    def reduce_core(keep, send):
        return summed(keep, core(send))

    if fast:
        osr, zsr = core(osend), core(zsend)
    else:
        grad_w_out = reduce_slow(reduce_x(reduce_core(ok, osend), 0)[0])
        grad_w_z = reduce_slow(reduce_x(reduce_core(zk, zsend), 0)[0])

    def within_backward(g, dy, kept):
        return call(
            functools.partial(k7_body, g),
            (slots,),
            [
                pl.BlockSpec(group, gsel(g)),
                pl.BlockSpec(group, gsel(g)),
                pl.BlockSpec((L, state), lambda s, sc: (s, 0)),
                pl.BlockSpec((L, state), lambda s, sc: (s, 0)),
                full((L, 128)),
                full((L, 128)),
                full((128, L)),
            ]
            + anywhere(len(kept)),
            [
                pl.BlockSpec(group, gsel(g)),
                pl.BlockSpec((2, L, state), lambda s, sc: (0, s, 0)),
                full((L, 128)),
            ],
            [sds((2, rows, wide), F32), sds((2, rows, state), F32), sds((L, 128), F32)],
            [
                vmem((2, 128, 128), F32),
                vmem((128, 128), BF),
                vmem((128, wide), BF),
                vmem((128, wide), BF),
                vmem((256, wide), BF),
                vmem((L, wide), F32),
                vmem((256, 2 * wide), BF),
                vmem((L, 2 * wide), F32),
                vmem((wide, 128), BF),
                vmem((L, wide), BF),
            ],
            (int(1e10) if g else 1, int(2e7) if g else 1),
            "within_backward_%d" % g,
            {8 + n: n for n in range(len(kept))},
        )(sc, xs, dy, blow, clow, cump, uvp, ct, *kept)

    dxw, bc7a, corr_a = within_backward(1, dy1, [])
    if fast:
        dy0, osr, zsr, dxw = meet(dy, osr, zsr, dxw)
        vo = summed(ok, osr).reshape((2, count // 2, 2, brow, cols))
        vor = flip(vo[:, :, 1], "dp", 1)
    else:
        dy0 = dy
    dxw, bc7b, corr_b = within_backward(0, dy0, [dxw])

    def states_backward(g, last, nt, extra_in, extra_specs):
        width = cols + 256 if last else cols
        gshape = (count, brow, width)

        def at(s, sc):
            return (g, s, 0)

        in_specs = [
            full((dim, erows)),
            pl.BlockSpec(group, at),
            pl.BlockSpec(group, at),
            pl.BlockSpec(group, at),
            pl.BlockSpec(group, at),
            pl.BlockSpec((1, 16, wide), lambda s, sc: (g, rows // 16 + s, 0)),
            pl.BlockSpec(group, at),
            pl.BlockSpec((srows + 16, wide), lambda s, sc: mirror(g, sc)),
            pl.BlockSpec((srows, wide), lambda s, sc: mirror(g, sc)),
            pl.BlockSpec((srows, wide), lambda s, sc: mirror(g, sc)),
            pl.BlockSpec((1, srows, wide), lambda s, sc: (g, 0, 0)),
            pl.BlockSpec((L, state), lambda s, sc: (s, 0)),
            full((L, 128)),
            full((L, 128)),
            full((L + 8, 128)),
            full((2, 16, wide)) if last else pl.BlockSpec((1, 16, wide), lambda s, sc: (g, 0, 0)),
            pl.BlockSpec(p1block, lambda s, sc: (g, 0, 0, 0)),
            pl.BlockSpec(p1block, lambda s, sc: (g, 0, 0, 0)),
        ]
        if last:
            in_specs += [full((2,) + p1block[1:])] * 2
        else:
            in_specs += [pl.BlockSpec(p1block, lambda s, sc: (g, 0, 0, 0))] * 2
        in_specs += extra_specs
        outs = [
            (gshape, BF),
            (gshape, BF),
            ((erows, wide), BF),
            ((L, 128), F32),
            ((8, 128), F32),
            ((rows, state), F32),
            ((8, wide), F32),
            ((dim, 128), F32),
        ]
        scratch = [
            vmem((dim, wide), F32),
            vmem((dim, 256), F32),
            vmem((state, wide), F32),
            vmem((16, cols), F32),
            vmem((state, wide), BF),
            vmem((L, wide), BF),
            vmem((L, wide), BF),
            vmem((L, wide), BF),
            vmem((wide, 128), BF),
            vmem((dim, wide), BF),
        ]
        if last:
            outs += [((erows, 512), BF), ((2, 8, state), F32), ((8, 128), F32), ((8, dim), F32)]
            scratch += [
                vmem((dim, 512), BF),
                vmem((2, erows, state), F32),
                vmem((4, dim, 128), F32),
                vmem((brow, 128), F32),
            ]
        scratch += [vmem((L, wide), F32), vmem((6, L + 16, 128), F32), vmem((256, wide), BF)]
        scratch += [vmem((L, wide), F32), vmem((L, wide), F32)]
        return call(
            functools.partial(k8_body, g, last),
            (slots,),
            in_specs,
            [full(shape) for shape, _ in outs],
            [sds(shape, dtype) for shape, dtype in outs],
            scratch,
            (int(1e10), int(2e7)),
            "states_backward_%d" % g,
        )(sc, nt, xs, dy, dsl, inx, inx, dxw, q1, q2, q3, prev, blow, stepp, etp, back, par, wam, war, wbm, wbr, *extra_in)

    def normed_grad_z(g, dg):
        return call(
            k9z_body,
            (1,),
            [
                pl.BlockSpec((1, rows, wide), lambda i, sc: (g, 0, 0)),
                pl.BlockSpec(wblock, lambda i, sc: (g, 0, 0, 0)),
                pl.BlockSpec(wblock, lambda i, sc: (g, 0, 0, 0)),
            ],
            full((rows, dim)),
            sds((rows, dim), F32),
            [vmem((dim, wide), BF)],
            (1, 1),
            "normed_grad_z%d" % g,
        )(sc, dg, wzm, wzr)

    dga, dxw = meet(dg, dxw)
    dna = normed_grad_z(1, dga)
    if fast:
        dxw, q2, dna, vor, zk = meet(dxw, q2, dna, vor, zk)
        vo = summed(vo[:, :, 0], vor)
        vor = flip(vo[1], "tensor", 2)
        vz = summed(zk, zsr).reshape((2, count // 2, 2, brow, cols))
        vzr = flip(vz[:, :, 1], "dp", 1)
    else:
        dxw, q2, dna = meet(dxw, q2, dna)
    q3 = lax.ppermute(q2, "tensor", [(1, 0)])
    ka, sa, din1, seg1, end1, dba1, small1, nga = states_backward(1, False, nt, [], [])
    if fast:
        sa, vor, vzr = meet(sa, vor, vzr)
        vo = summed(vo[0], vor)
        vz = summed(vz[:, :, 0], vzr)
        vzr = flip(vz[1], "tensor", 2)
    sar = core(sa)
    dgb, _ = meet(dg, sa)
    dnb = normed_grad_z(0, dgb)
    nt0, sar, dnb = meet(nt, sar, dnb)
    va = summed(ka, sar)
    xa = flip(va, "tensor", 2)
    ks, ss, din0, _, _, _, small0, _, din5, sbc, sdt, ngo = states_backward(
        0,
        True,
        nt0,
        [fac, sigp, decay, gain, ngz, nga, conv_bc, bc7a, bc7b, corr_a, corr_b, dc5, rowsum, sin, dbc, seg1, end1, dba1],
        [
            full((8, 128)),
            full((L, 128)),
            full((L, 128)),
            full((1, dim)),
            full((dim, 128)),
            full((dim, 128)),
            full((4, 2 * state)),
            full((2, rows, state)),
            full((2, rows, state)),
            full((L, 128)),
            full((L, 128)),
            full((rows, state)),
            full((L, 128)),
            full((2, erows, state)),
            full((2, rows, state)),
            full((L, 128)),
            full((8, 128)),
            full((rows, state)),
        ],
    )

    if fast:
        ss, xa, vzr = meet(ss, xa, vzr)
        vw = jnp.stack([vo, summed(vz[0], vzr)]).reshape((2, count // 4, 2, brow, cols))
        vwr = flip(vw[:, :, 1], "dp", 2)
    dts = sdt[:2].reshape(2, slots, SPAN)[:, :, : 4 * heads].sum(axis=1).reshape(2, 2, 2, heads)
    dts = jnp.pad(dts, ((0, 0), (0, 0), (0, 0), (0, cols - heads)))
    dts = jnp.swapaxes(dts, 0, 1).reshape(2, 2, wide)
    mine = jnp.concatenate(
        [
            jnp.stack([small0[:5], small1[:5]]),
            small5[:, :2],
            dts,
            jnp.zeros((2, 7, wide), F32),
        ],
        axis=1,
    )
    flat = jnp.concatenate(
        [jnp.concatenate([sbc[0, :5], sbc[1, :5]], axis=1).reshape(-1), ngo[0]]
    )
    flat = jnp.pad(flat, (0, 8 * cols - flat.shape[0])).reshape(8, cols)
    send = jnp.concatenate([mine[:, :, cols:].reshape(32, cols), flat], axis=0)
    din0, ssr, got = meet(din0, core(ss), core(send))
    own = mine[:, :, :cols] + got[:32].reshape(2, 16, cols)
    flat = flat + got[32:]
    vb = summed(ks, ssr)
    px = flip(vb[..., cols + 128 :], "tensor", 2)
    vx = summed(vb[..., :cols], xa)
    if fast:
        vx = vx.reshape((count // 2, 2) + vx.shape[1:])
        vxr = flip(vx[:, 1], "dp", 1)
    both = jnp.concatenate([own[0], flat], axis=0)
    got = flip(jnp.concatenate([own[1], flat], axis=0), "tensor", 2)

    dn = call(
        k9_body,
        (2,),
        [
            full((erows, wide)),
            full((erows, wide)),
            pl.BlockSpec((erows, 256), lambda g, sc: (0, g)),
            full((rows, dim)),
            full((rows, dim)),
        ]
        + [pl.BlockSpec(p1block, w_g)] * 4,
        full((erows, dim)),
        sds((erows, dim), F32),
        [vmem((dim, wide), BF), vmem((dim, 256), BF)],
        (int(6e9), int(2e7)),
        "normed_grad",
    )(sc, din0, din1, din5, dna, dnb, wam, war, wbm, wbr)

    if fast:
        dn, px, vxr, got, vwr = meet(dn, px, vxr, got, vwr)
        vw = summed(vw[:, :, 0], vwr).reshape((2, count // 8, 2, brow, cols))
        vwr = flip(vw[:, :, 1], "dp", 4)
        vx = summed(vx[:, 0], vxr)
        vp = summed(vb[..., cols : cols + 128], px)
        vp = vp.reshape((count // 2, 2) + vp.shape[1:])
        vpr = flip(vp[:, 1], "dp", 1)
        both = both + got
        got = flip(both, "dp", 1)
    hr = lax.ppermute(dn[rows:].astype(BF), "tensor", [(a + 1, a) for a in range(tcount - 1)])
    if fast:
        hr, vpr, got, vwr = meet(hr, vpr, got, vwr)
        vw = summed(vw[:, :, 0], vwr)
        grad_w_out, grad_w_z = finish(vw[0], 8), finish(vw[1], 8)
        v1 = jnp.concatenate([vx, summed(vp[:, 0], vpr)], axis=-1)
        v1 = v1.reshape((count // 4, 2) + v1.shape[1:])
        v1r = flip(v1[:, 1], "dp", 2)
        both = both + got
        got = flip(both, "dp", 2)

    ig = call(
        k10_body,
        (slots,),
        [
            pl.BlockSpec((L, dim), lambda s, sc: (s, 0)),
            pl.BlockSpec((16, dim), lambda s, sc: (s, 0)),
            pl.BlockSpec((L, dim), lambda s, sc: (s, 0)),
            pl.BlockSpec((L, dim), lambda s, sc: (s, 0)),
            full((1, dim)),
        ],
        pl.BlockSpec((L, dim), lambda s, sc: (s, 0)),
        sds((rows, dim), BF),
        [],
        (int(1e9), int(1e7)),
        "input_grad",
    )(sc, dn, hr, tok, cot, gain)

    if fast:
        ig, v1r, got = meet(ig, v1r, got)
        v1 = summed(v1[:, 0], v1r)
        both = both + got
        bit = 4
        while bit < dpcount:
            both = both + flip(both, "dp", bit)
            v1 = reduce_dp(v1, bit)
            bit *= 2
        grad1 = v1[0].astype(F32)
    else:
        both = lax.psum(both + got, "dp")
        v1 = jnp.concatenate([vx, summed(vb[..., cols : cols + 128], px)], axis=-1)
        grad1 = reduce_slow(v1)
    own, flat = both[:16], both[16:].reshape(-1)
    bcs = flat[: 5 * 2 * state].reshape(5, 2 * state)
    ngain = flat[5 * 2 * state : 5 * 2 * state + dim]
    skip_grad = own[6].reshape(heads, cols // heads).sum(axis=1)

    mine_bc = grad1[:, cols : cols + bq]
    if fast:
        got = mine_bc.reshape(tcount, shard // tcount, bq)
    else:
        parts = mine_bc.reshape(tcount, shard // tcount, bq)
        got = lax.all_to_all(parts, "tensor", split_axis=0, concat_axis=0, tiled=True)
    grad_w_bc = jnp.swapaxes(got, 0, 1).reshape(shard // tcount, bq * tcount)

    return (
        out.reshape(tokens.shape),
        ig.reshape(tokens.shape),
        ngain,
        grad_w_z,
        grad1[:, :cols],
        grad_w_bc,
        grad1[:, cols + bq : cols + bq + heads],
        own[:4],
        own[4],
        bcs[:4],
        bcs[4],
        own[7, :heads],
        own[8, :heads],
        skip_grad,
        own[5],
        grad_w_out,
    )


def solution(mesh):
    return jax.shard_map(
        per_device,
        mesh=mesh,
        in_specs=(
            P("dp", "tensor", None), P("dp", None), P("dp", "tensor", None), P(),
            P("dp", "tensor"), P("dp", "tensor"), P("dp", None), P("dp", "tensor"),
            P(None, "tensor"), P("tensor"), P(), P(),
            P("tensor"), P("tensor"), P("tensor"), P("tensor"), P("dp", "tensor"),
        ),
        out_specs=(
            P("dp", "tensor", None), P("dp", "tensor", None), P(),
            P("dp", "tensor"), P("dp", "tensor"), P(("dp", "tensor"), None), P("dp", "tensor"),
            P(None, "tensor"), P("tensor"), P(), P(),
            P("tensor"), P("tensor"), P("tensor"), P("tensor"), P("dp", "tensor"),
        ),
        check_vma=False,
    )
```

time: 807 us -> 327 us (0.41)
  blocking collectives: 216 us -> 0 us
  Pallas kernels: 0 us -> 176 us
  matrix products: 145 us -> 0 us
  other arithmetic: 157 us -> 12.9 us
  local copies, waits for them, and re-layouts: 168 us -> 36.6 us
  waiting for transfers between devices: 96 us -> 33.3 us
  starting transfers between devices: 5.09 us -> 62.6 us
  between operations: 15.7 us -> 2.56 us
    pallas_call x0 -> x16, Pallas kernels: none -> 176 us  [the longest x2 40.7 us: states_backward(): call(functools.partial(k8_body, g, last), (slots,), in_specs, [full(shape...]
    all_gather x5 -> x0, blocking collectives: 156 us -> none  [the longest x1 33.8 us: per_device(): lax.all_gather(w_out, 'dp', axis=0, tiled=True)]
    dot_general x19 -> x0, matrix products: 144 us -> none  [the longest x1 24 us: mixer_backward(): jnp.einsum('cqhp,ckhp->chqk', dy_heads, x_heads, preferred_element_type=j...]
    reduce_scatter x3 -> x0, waiting for transfers between devices: 84.5 us -> none  [the longest x1 84.4 us: per_device(): lax.psum_scatter(lax.dot_general(columns, own_state, (((0,), (0,)), ((),...]
    reduce_sum x13 -> x2, other arithmetic: 69.7 us -> 0.65 us  [the longest x1 0.63 us: per_device(): skip_grad = own[6].reshape(heads, cols // heads).sum(axis=1)]
    ppermute x0 -> x47, starting transfers between devices: none -> 62.6 us  [the longest x39 40.4 us: flip(): return lax.ppermute(value, axis, [(a, a ^ bit) for a in range(count)])]
    psum x3 -> x0, blocking collectives: 60.1 us -> none  [the longest x1 39.5 us: per_device(): lax.psum((spread_cols(conv_x_grad, tensor_slot, tensor_count), spread_col...]
    reshape x13 -> x10, local copies, waits for them, and re-layouts: 40 us -> 1.7 us  [the longest x1 0.71 us: per_device(): grad_w_bc = jnp.swapaxes(got, 0, 1).reshape(shard // tcount, bq * tcount)]
  transfers between devices with their start and end apart: 7 -> 47, of which waited for: 2 -> 15; matrix products, arithmetic and copies ran while one was open for 36% -> 8% of each run, Pallas kernels for 0% -> 42%
where the time goes in v2:
time: 327 us; the launch traced here: 324 us
  Pallas kernels  176 us (54%)
  starting transfers between devices  62.6 us (19%)
  local copies, waits for them, and re-layouts  36.6 us (11%)
  waiting for transfers between devices  33.3 us (10%)
  other arithmetic  12.9 us (4%)
    pallas_call x2, Pallas kernels, states_backward(): call(functools.partial(k8_body, g, last), (slots,), in_specs, [full(shape...  40.7 us
    ppermute x39, starting transfers between devices, flip(): return lax.ppermute(value, axis, [(a, a ^ bit) for a in range(count)])  40.4 us
    pallas_call x1, Pallas kernels, per_device(): call(k5_body, (2, 2, slots), [pl.BlockSpec(group, p_gs(0)), pl.BlockSpec(...  38.7 us
    ppermute x39, waiting for transfers between devices, flip(): return lax.ppermute(value, axis, [(a, a ^ bit) for a in range(count)])  31.3 us
    unnamed x192, local copies, waits for them, and re-layouts  18.9 us
    pallas_call x2, Pallas kernels, within_backward(): call(functools.partial(k7_body, g), (slots,), [pl.BlockSpec(group, gsel(g...  17.5 us
    pallas_call x1, Pallas kernels, per_device(): call(k1_body, (2,), [full((rows, dim)), full((64, dim)), full((1, dim))]...  15.7 us
    pallas_call x2, Pallas kernels, conv_and_states(): call(functools.partial(k2_body, g), (slots,), [pl.BlockSpec(group, gsel(g...  15.1 us
  transfers between devices with their start and end apart: 47, of which 15 were waited for; matrix products, arithmetic and copies ran while one was open for 8% of the time, Pallas kernels for 42%

profile of v2, /device:TPU:0, one launch (start us, length us, event | category | flops | bytes accessed | tf_op | source)
XLA Modules:
  0.0 324.3 jit_solution(11970288951739915585)
XLA Ops:
  2.6 4.1 %collective-permute-start = (bf16[1,96,512]{2,1,0:T(8,128)(2,1)S(1)}, bf16[1,96,512]{2,1,0:T(8,128)(2,1)S(1)}, u32[]{:S(2)}, u32[]{:S(2)}) collective-permute-start(bf16[1,96,512]{2,1,0:T(8,128)(2,1)S(1)} %get-tuple-element.358), channel_id=1, source_target_pairs={{0,16},{4,20},{8,24},{12,28},{16,0},{20,4},{24,8},{28,12},{1,17},{... | collective-permute-start | bytes 294920 | tf_op jit(solution)/shard_map/ppermute | solution.py:928
  14.6 1.6 collective-permute-start.1
  16.2 1.3 collective-permute-start.3
  17.5 2.2 collective-permute-start.2
  19.7 1.8 collective-permute-done.2
  21.6 2.5 collective-permute-start.4
  24.1 1.5 collective-permute-start.5
  25.9 1.2 collective-permute-done.6
  27.2 7.7 %collective-permute-done.7 = bf16[1,2,96,384]{3,2,1,0:T(8,128)(2,1)S(1)} collective-permute-done((bf16[1,2,96,384]{3,2,1,0:T(8,128)(2,1)S(1)}, bf16[1,2,96,384]{3,2,1,0:T(8,128)(2,1)S(1)}, u32[]{:S(2)}, u32[]{:S(2)}) %collective-permute-start.7) | collective-permute-done | bytes 147488 | tf_op jit(solution)/shard_map/ppermute | solution.py:928
  36.3 8.3 %collective-permute-done.10 = bf16[2,2,96,384]{3,2,1,0:T(8,128)(2,1)S(1)} collective-permute-done((bf16[2,2,96,384]{3,2,1,0:T(8,128)(2,1)S(1)}, bf16[2,2,96,384]{3,2,1,0:T(8,128)(2,1)S(1)}, u32[]{:S(2)}, u32[]{:S(2)}) %collective-permute-start.10) | collective-permute-done | bytes 294944 | tf_op jit(solution)/shard_map/ppermute | solution.py:928
  44.6 1.4 collective-permute-done.9
  47.5 1.6 collective-permute-start.13
  50.0 15.7 %projections.1 = (bf16[1088,768]{1,0:T(8,128)(2,1)}, bf16[2,1088,768]{2,1,0:T(8,128)(2,1)}, bf16[1024,128]{1,0:T(8,128)(2,1)}, bf16[1024,128]{1,0:T(8,128)(2,1)}...) custom-call(s32[16]{0:T(128)S(1)} %pad_add_fusion.1.sc, ...), custom_call_target="tpu_custom_call" | custom-call | flops 7000000000 | bytes 20000000 | tf_op jit(solution)/shard_map/projections/pallas_call | solution.py:1051
  65.9 1.3 collective-permute-start.15
  68.2 1.9 copy-done.2
  70.1 7.5 %conv_and_states_0.1 = (bf16[2,1024,768]{2,1,0:T(8,128)(2,1)}, bf16[2,1024,768]{2,1,0:T(8,128)(2,1)}, bf16[2,1024,768]{2,1,0:T(8,128)(2,1)}, bf16[528,1536]{1,0:T(8,128)(2,1)}) custom-call(s32[16]{0:T(128)S(1)} %pad_add_fusion.1.sc, bf16[2,1088,768]{2,1,0:T(8,128)(2,1)S(1)} %copy-done.2, bf16[2,1088,768]{2,1,0:T(8,128)(2,1)S(1)} %copy-done.2, ...), custom_call_target="tpu_custom_call" | custom-call | flops 1 | bytes 1 | tf_op jit(solution)/shard_map/conv_and_states_0/pallas_call | solution.py:1109
  77.7 7.5 %conv_and_states_1.1 = (bf16[2,1024,768]{2,1,0:T(8,128)(2,1)}, bf16[2,1024,768]{2,1,0:T(8,128)(2,1)}, bf16[2,1024,768]{2,1,0:T(8,128)(2,1)}, bf16[528,1536]{1,0:T(8,128)(2,1)}) custom-call(s32[16]{0:T(128)S(1)} %pad_add_fusion.1.sc, bf16[2,1088,768]{2,1,0:T(8,128)(2,1)S(1)} %copy-done.2, ...), custom_call_target="tpu_custom_call", output_to_operand_aliasing={{0}: (9, {}), {1}: (10, {}), {2}: (11, {}), {3}: (12, {})} | custom-call | flops 5000000000 | bytes 20000000 | tf_op jit(solution)/shard_map/conv_and_states_1/pallas_call | solution.py:1109
  85.2 1.6 collective-permute-start.17
  88.9 1.1 collective-permute-done.17.r1
  91.2 1.1 collective-permute-start.20
  92.4 5.7 %within_0.1.rest_0_ = f32[2,1024,768]{2,1,0:T(8,128)} custom-call(s32[16]{0:T(128)S(1)} %pad_add_fusion.1.sc, bf16[2,1024,768]{2,1,0:T(8,128)(2,1)S(1)} %copy-done.6, bf16[1024,128]{1,0:T(8,128)(2,1)S(1)} %copy-done.32, bf16[1024,128]{1,0:T(8,128)(2,1)S(1)} %copy-done.48, f32[256,128]{1,0:T(8,128)S(1)} %copy-done.53, f32[256,128]{1,0:T(8,128)S(1)} %copy-done.55, ...), custom_call_target="tpu_custom_call" | custom-call | flops 5000000000 | bytes 10000000 | tf_op jit(solution)/shard_map/within_0/pallas_call | solution.py:1168
  98.2 5.9 %within_1.1.within = f32[2,1024,768]{2,1,0:T(8,128)} custom-call(s32[16]{0:T(128)S(1)} %pad_add_fusion.1.sc, bf16[2,1024,768]{2,1,0:T(8,128)(2,1)S(1)} %copy-done.6, bf16[1024,128]{1,0:T(8,128)(2,1)S(1)} %copy-done.32, bf16[1024,128]{1,0:T(8,128)(2,1)S(1)} %copy-done.48, f32[256,128]{1,0:T(8,128)S(1)} %copy-done.53, ...), custom_call_target="tpu_custom_call", output_to_operand_aliasing={{}: (7, {})} | custom-call | flops 5000000000 | bytes 10000000 | tf_op jit(solution)/shard_map/within_1/pallas_call | solution.py:1168
  104.1 8.5 %gate_and_out_backward.1 = (bf16[2,1024,768]{2,1,0:T(8,128)(2,1)}, bf16[2,1024,768]{2,1,0:T(8,128)(2,1)}, bf16[1024,768]{1,0:T(8,128)(2,1)}) custom-call(s32[16]{0:T(128)S(1)} %pad_add_fusion.1.sc, bf16[1088,768]{1,0:T(8,128)(2,1)S(1)} %copy-done.76, bf16[1024,768]{1,0:T(8,128)(2,1)S(1)} %bitcast.231, bf16[2,8,96,384]{3,2,1,0:T(8,128)(2,1)S(1)} %bitcast.219, ...), custom_call_target="tpu_custom_call" | custom-call | flops 5000000000 | bytes 20000000 | tf_op jit(solution)/shard_map/gate_and_out_backward/pallas_call | solution.py:1198
  114.6 38.7 %gated_norm.1 = (bf16[1024,768]{1,0:T(8,128)(2,1)}, bf16[2,1024,768]{2,1,0:T(8,128)(2,1)}, bf16[2,1024,768]{2,1,0:T(8,128)(2,1)}, bf16[2,1024,768]{2,1,0:T(8,128...) custom-call(s32[16]{0:T(128)} %copy-done.64, ...), custom_call_target="tpu_custom_call" | custom-call | flops 15000000512 | bytes 40000000 | tf_op jit(solution)/shard_map/gated_norm/pallas_call | solution.py:1234
  153.2 1.3 collective-permute-start.22
  154.6 1.9 copy-done.4
  156.4 1.9 copy-done.75
  158.3 1.4 copy-done.77
  159.8 1.4 copy-done.78
  161.2 10.5 %outer_weight_grads.1 = (bf16[2,8,96,384]{3,2,1,0:T(8,128)(2,1)}, bf16[2,8,96,384]{3,2,1,0:T(8,128)(2,1)}, bf16[2,8,96,384]{3,2,1,0:T(8,128)(2,1)}, bf16[2,8,96,...) custom-call(s32[16]{0:T(128)S(1)} %copy-done.65, bf16[1088,768]{1,0:T(8,128)(2,1)S(1)} %copy-done.77, ...), custom_call_target="tpu_custom_call" | custom-call | flops 5000000000 | bytes 20000000 | tf_op jit(solution)/shard_map/outer_weight_grads/pallas_call | solution.py:1298
  171.7 2.5 collective-permute-start.24
  174.8 13.4 %collective-permute-start.25 = (bf16[512,1536]{1,0:T(8,128)(2,1)S(1)}, bf16[512,1536]{1,0:T(8,128)(2,1)S(1)}, u32[]{:S(2)}, u32[]{:S(2)}) collective-permute-start(bf16[512,1536]{1,0:T(8,128)(2,1)S(1)} %fusion.1), channel_id=1, source_target_pairs={{2,1},{6,5},{10,9},{14,13},{18,17},{22,21},{26,25},{30,29}} | collective-permute-start | bytes 4718600 | tf_op jit(solution)/shard_map/ppermute | solution.py:1313
  188.2 8.7 %within_backward_1.1 = (f32[2,1024,768]{2,1,0:T(8,128)}, f32[2,1024,128]{2,1,0:T(8,128)}, f32[256,128]{1,0:T(8,128)}) custom-call(s32[16]{0:T(128)S(1)} %copy-done.65, bf16[2,1024,768]{2,1,0:T(8,128)(2,1)S(1)} %copy-done.6, bf16[2,1024,768]{2,1,0:T(8,128)(2,1)S(1)} %copy-done.3, bf16[1024,128]{1,0:T(8,128)(2,1)S(1)} %copy-done.32, ...), custom_call_target="tpu_custom_call" | custom-call | flops 10000000000 | bytes 20000000 | tf_op jit(solution)/shard_map/within_backward_1/pallas_call | solution.py:1351
  198.0 1.1 collective-permute-start.26
  199.1 8.8 %within_backward_0.1 = (f32[2,1024,768]{2,1,0:T(8,128)}, f32[2,1024,128]{2,1,0:T(8,128)}, f32[256,128]{1,0:T(8,128)}) custom-call(s32[16]{0:T(128)S(1)} %copy-done.65, bf16[2,1024,768]{2,1,0:T(8,128)(2,1)S(1)} %copy-done.6, bf16[2,1024,768]{2,1,0:T(8,128)(2,1)S(1)} %copy-done.3, bf16[1024,128]{1,0:T(8,128)(2,1)S(1)} %copy-done.32, ...), custom_call_target="tpu_custom_call", output_to_operand_aliasing={{0}: (8, {})} | custom-call | flops 1 | bytes 1 | tf_op jit(solution)/shard_map/within_backward_0/pallas_call | solution.py:1351
  207.9 3.7 %normed_grad_z1.1.dna = f32[1024,768]{1,0:T(8,128)} custom-call(s32[16]{0:T(128)S(1)} %copy-done.65, bf16[2,1024,768]{2,1,0:T(8,128)(2,1)S(1)} %copy-done.4, bf16[2,8,96,384]{3,2,1,0:T(8,128)(2,1)S(1)} %bitcast.221, bf16[2,8,96,384]{3,2,1,0:T(8,128)(2,1)S(1)} %collective-permute-done.18.wzr), custom_call_target="tpu_custom_call" | custom-call | flops 1 | bytes 1 | tf_op jit(solution)/shard_map/normed_grad_z1/pallas_call | solution.py:1472
  211.7 2.6 collective-permute-done.26
  214.2 1.3 collective-permute-start.27
  216.9 1.1 collective-permute-start.29
  218.1 3.4 %collective-permute-start.28 = (bf16[4,96,384]{2,1,0:T(8,128)(2,1)S(1)}, bf16[4,96,384]{2,1,0:T(8,128)(2,1)S(1)}, u32[]{:S(2)}, u32[]{:S(2)}) collective-permute-start(bf16[4,96,384]{2,1,0:T(8,128)(2,1)S(1)} %slice_bitcast_fusion.9), channel_id=1, source_target_pairs={{0,2},{1,3},{2,0},{3,1},{4,6},{5,7},{6,4},{7,5},{8,10},{9,11},{10,... | collective-permute-start | bytes 884744 | tf_op jit(solution)/shard_map/ppermute | solution.py:928
  221.6 16.2 %states_backward_1.1 = (bf16[8,96,384]{2,1,0:T(8,128)(2,1)}, bf16[8,96,384]{2,1,0:T(8,128)(2,1)}, bf16[1088,768]{1,0:T(8,128)(2,1)}, f32[256,128]{1,0:T(8,128)},...) custom-call(s32[16]{0:T(128)S(1)} %copy-done.65, ...), custom_call_target="tpu_custom_call" | custom-call | flops 10000000000 | bytes 20000000 | tf_op jit(solution)/shard_map/states_backward_1/pallas_call | solution.py:1460
  240.8 3.7 %normed_grad_z0.1.dnb = f32[1024,768]{1,0:T(8,128)} custom-call(s32[16]{0:T(128)S(1)} %copy-done.65, bf16[2,1024,768]{2,1,0:T(8,128)(2,1)S(1)} %copy-done.5, bf16[2,8,96,384]{3,2,1,0:T(8,128)(2,1)S(1)} %bitcast.222, bf16[2,8,96,384]{3,2,1,0:T(8,128)(2,1)S(1)} %collective-permute-done.18.wzr), custom_call_target="tpu_custom_call" | custom-call | flops 1 | bytes 1 | tf_op jit(solution)/shard_map/normed_grad_z0/pallas_call | solution.py:1472
  244.7 1.0 add_convert_fusion.4
  245.7 1.1 collective-permute-start.31
  246.9 24.5 %states_backward_0.1 = (bf16[8,96,640]{2,1,0:T(8,128)(2,1)}, bf16[8,96,640]{2,1,0:T(8,128)(2,1)}, bf16[1088,768]{1,0:T(8,128)(2,1)}, f32[256,128]{1,0:T(8,128)},...) custom-call(s32[16]{0:T(128)S(1)} %copy-done.65, ...), custom_call_target="tpu_custom_call" | custom-call | flops 10000000000 | bytes 20000000 | tf_op jit(solution)/shard_map/states_backward_0/pallas_call | solution.py:1460
  275.4 1.2 fusion.8
  276.8 1.0 collective-permute-start.37
  277.8 1.9 add_convert_fusion.2
  279.8 1.2 add_convert_fusion.3
  282.0 1.2 collective-permute-start.35
  283.2 1.4 copy-done.70
  284.7 1.2 copy-done.72
  285.9 1.4 copy-done.74
  287.4 7.3 %normed_grad.1.dn = f32[1088,768]{1,0:T(8,128)} custom-call(s32[16]{0:T(128)S(1)} %copy-done.65, bf16[1088,768]{1,0:T(8,128)(2,1)S(1)} %copy-done.70, bf16[1088,768]{1,0:T(8,128)(2,1)S(1)} %copy-done.74, bf16[1088,512]{1,0:T(8,128)(2,1)S(1)} %copy-done.72, f32[1024,768]{1,0:T(8,128)S(1)} %copy-done.9, f32[1024,768]{1,0:T(8,128)S(1)} %copy-done.10, ...), custom_call_target="tpu_custom_call" | custom-call | flops 6000000000 | bytes 20000000 | tf_op jit(solution)/shard_map/normed_grad/pallas_call | solution.py:1570
  294.9 1.1 collective-permute-start.41
  296.0 1.1 collective-permute-start.40
  298.1 1.6 collective-permute-start.39
  301.5 2.3 collective-permute-done.42
  304.0 2.1 collective-permute-start.43
  306.9 3.3 %input_grad.1 = bf16[1024,768]{1,0:T(8,128)(2,1)} custom-call(s32[16]{0:T(128)S(1)} %copy-done.65, f32[1088,768]{1,0:T(8,128)S(1)} %copy-done.8, bf16[64,768]{1,0:T(8,128)(2,1)S(1)} %collective-permute-done.39.hr, bf16[1024,768]{1,0:T(8,128)(2,1)S(1)} %bitcast.230, bf16[1024,768]{1,0:T(8,128)(2,1)S(1)} %bitcast.232, f32[1,768]{1,0:T(1,128)S(1)} %reshape.209.gain.rest_3_), custom_call_target="tpu_custom_call" | custom-call | flops 1000000000 | bytes 10000000 | tf_op jit(solution)/shard_map/input_grad/pallas_call | solution.py:1609
  310.2 1.7 collective-permute-done.43
  312.0 1.9 collective-permute-start.45
  313.9 1.2 collective-permute-start.46
  315.1 2.3 collective-permute-done.45
  (361 shorter events, 42.1 us)
Async XLA Ops:
  2.6 11.9 %collective-permute-start = (bf16[1,96,512]{2,1,0:T(8,128)(2,1)S(1)}, bf16[1,96,512]{2,1,0:T(8,128)(2,1)S(1)}, u32[]{:S(2)}, u32[]{:S(2)}) collective-permute-start(bf16[1,96,512]{2,1,0:T(8,128)(2,1)S(1)} %get-tuple-element.358), channel_id=1, source_target_pairs={{0,16},{4,20},{8,24},{12,28},{16,0},{20,4},{24,8},{28,12},{1,17},{... | collective-permute-start | bytes 294920 | tf_op jit(solution)/shard_map/ppermute | solution.py:928
  14.5 89.5 %copy-start.64 = (s32[16]{0:T(128)}, s32[16]{0:T(128)S(1)}, u32[]{:S(2)}) copy-start(s32[16]{0:T(128)S(1)} %pad_add_fusion.1.sc) | copy-start | bytes 196
  14.6 6.9 %collective-permute-start.1 = (bf16[2,96,512]{2,1,0:T(8,128)(2,1)S(1)}, bf16[2,96,512]{2,1,0:T(8,128)(2,1)S(1)}, u32[]{:S(2)}, u32[]{:S(2)}) collective-permute-start(bf16[2,96,512]{2,1,0:T(8,128)(2,1)S(1)} %get-tuple-element.354), channel_id=1, source_target_pairs={{0,8},{4,12},{8,0},{12,4},{16,24},{20,28},{24,16},{28,20},{1,9},{5... | collective-permute-start | bytes 589832 | tf_op jit(solution)/shard_map/ppermute | solution.py:928
  16.2 5.3 %collective-permute-start.3 = (bf16[64,768]{1,0:T(8,128)(2,1)S(1)}, bf16[64,768]{1,0:T(8,128)(2,1)S(1)}, u32[]{:S(2)}, u32[]{:S(2)}) collective-permute-start(bf16[64,768]{1,0:T(8,128)(2,1)S(1)} %bitcast.271), channel_id=1, source_target_pairs={{0,1},{1,2},{2,3},{4,5},{5,6},{6,7},{8,9},{9,10},{10,11},{12,13},{... | collective-permute-start | bytes 294920 | tf_op jit(solution)/shard_map/ppermute | solution.py:1013
  17.5 4.0 %collective-permute-start.2 = (f32[16,384]{1,0:T(8,128)S(1)}, f32[16,384]{1,0:T(8,128)S(1)}, u32[]{:S(2)}, u32[]{:S(2)}) collective-permute-start(f32[16,384]{1,0:T(8,128)S(1)} %concatenate.38), channel_id=1, source_target_pairs={{0,2},{1,3},{2,0},{3,1},{4,6},{5,7},{6,4},{7,5},{8,10},{9,11},{10,... | collective-permute-start | bytes 73736 | tf_op jit(solution)/shard_map/ppermute | solution.py:928
  21.6 13.2 %collective-permute-start.4 = (bf16[4,96,256]{2,1,0:T(8,128)(2,1)S(1)}, bf16[4,96,256]{2,1,0:T(8,128)(2,1)S(1)}, u32[]{:S(2)}, u32[]{:S(2)}) collective-permute-start(bf16[4,96,256]{2,1,0:T(8,128)(2,1)S(1)} %get-tuple-element.350), channel_id=1, source_target_pairs={{0,2},{1,3},{2,0},{3,1},{4,6},{5,7},{6,4},{7,5},{8,10},{9,11},{10,... | collective-permute-start | bytes 589832 | tf_op jit(solution)/shard_map/ppermute | solution.py:928
  24.1 10.8 %collective-permute-start.5 = (bf16[4,96,256]{2,1,0:T(8,128)(2,1)S(1)}, bf16[4,96,256]{2,1,0:T(8,128)(2,1)S(1)}, u32[]{:S(2)}, u32[]{:S(2)}) collective-permute-start(bf16[4,96,256]{2,1,0:T(8,128)(2,1)S(1)} %get-tuple-element.349), channel_id=1, source_target_pairs={{0,4},{4,0},{8,12},{12,8},{16,20},{20,16},{24,28},{28,24},{1,5},{5... | collective-permute-start | bytes 589832 | tf_op jit(solution)/shard_map/ppermute | solution.py:928
  25.6 9.3 %collective-permute-start.7 = (bf16[1,2,96,384]{3,2,1,0:T(8,128)(2,1)S(1)}, bf16[1,2,96,384]{3,2,1,0:T(8,128)(2,1)S(1)}, u32[]{:S(2)}, u32[]{:S(2)}) collective-permute-start(bf16[1,2,96,384]{3,2,1,0:T(8,128)(2,1)S(1)} %maximum_bitcast_fusion), channel_id=1, source_target_pairs={{0,16},{4,20},{8,24},{12,28},{16,0},{20,4},{24,8},{28,12},{1,17},{... | collective-permute-start | bytes 442376 | tf_op jit(solution)/shard_map/ppermute | solution.py:928
  25.9 1.2 collective-permute-start.6
  34.9 11.1 %collective-permute-start.9 = (bf16[4,2,96,256]{3,2,0,1:T(8,128)(2,1)S(1)}, bf16[4,2,96,256]{3,2,0,1:T(8,128)(2,1)S(1)}, u32[]{:S(2)}, u32[]{:S(2)}) collective-permute-start(bf16[4,2,96,256]{3,2,0,1:T(8,128)(2,1)S(1)} %pad_maximum_fusion.9), channel_id=1, source_target_pairs={{0,2},{1,3},{2,0},{3,1},{4,6},{5,7},{6,4},{7,5},{8,10},{9,11},{10,... | collective-permute-start | bytes 1179656 | tf_op jit(solution)/shard_map/ppermute | solution.py:928
  35.5 10.8 %collective-permute-start.8 = (bf16[2,4,96,256]{3,2,1,0:T(8,128)(2,1)S(1)}, bf16[2,4,96,256]{3,2,1,0:T(8,128)(2,1)S(1)}, u32[]{:S(2)}, u32[]{:S(2)}) collective-permute-start(bf16[2,4,96,256]{3,2,1,0:T(8,128)(2,1)S(1)} %get-tuple-element.346), channel_id=1, source_target_pairs={{0,4},{4,0},{8,12},{12,8},{16,20},{20,16},{24,28},{28,24},{1,5},{5... | collective-permute-start | bytes 1179656 | tf_op jit(solution)/shard_map/ppermute | solution.py:928
  36.1 8.4 %collective-permute-start.10 = (bf16[2,2,96,384]{3,2,1,0:T(8,128)(2,1)S(1)}, bf16[2,2,96,384]{3,2,1,0:T(8,128)(2,1)S(1)}, u32[]{:S(2)}, u32[]{:S(2)}) collective-permute-start(bf16[2,2,96,384]{3,2,1,0:T(8,128)(2,1)S(1)} %get-tuple-element.352), channel_id=1, source_target_pairs={{0,8},{4,12},{8,0},{12,4},{16,24},{20,28},{24,16},{28,20},{1,9},{5... | collective-permute-start | bytes 884744 | tf_op jit(solution)/shard_map/ppermute | solution.py:928
  36.3 41.4 %copy-start.33 = (f32[2,16,768]{2,1,0:T(8,128)}, f32[2,16,768]{2,1,0:T(8,128)S(1)}, u32[]{:S(2)}) copy-start(f32[2,16,768]{2,1,0:T(8,128)S(1)} %pad_maximum_fusion.14.par) | copy-start | bytes 294916
  46.5 3.1 collective-permute-start.12
  46.7 19.0 %copy-start.14 = (bf16[2,4,2,96,256]{4,3,2,1,0:T(8,128)(2,1)}, bf16[2,4,2,96,256]{4,3,2,1,0:T(8,128)(2,1)S(1)}, u32[]{:S(2)}) copy-start(bf16[2,4,2,96,256]{4,3,2,1,0:T(8,128)(2,1)S(1)} %copy.78) | copy-start | bytes 2359300
  46.7 3.2 collective-permute-start.11
  47.5 18.3 %collective-permute-start.13 = (bf16[4,96,384]{2,1,0:T(8,128)(2,1)S(1)}, bf16[4,96,384]{2,1,0:T(8,128)(2,1)S(1)}, u32[]{:S(2)}, u32[]{:S(2)}) collective-permute-start(bf16[4,96,384]{2,1,0:T(8,128)(2,1)S(1)} %get-tuple-element.344), channel_id=1, source_target_pairs={{0,2},{1,3},{2,0},{3,1},{4,6},{5,7},{6,4},{7,5},{8,10},{9,11},{10,... | collective-permute-start | bytes 884744 | tf_op jit(solution)/shard_map/ppermute | solution.py:928
  49.1 16.7 %collective-permute-start.14 = (bf16[4,96,384]{2,1,0:T(8,128)(2,1)S(1)}, bf16[4,96,384]{2,1,0:T(8,128)(2,1)S(1)}, u32[]{:S(2)}, u32[]{:S(2)}) collective-permute-start(bf16[4,96,384]{2,1,0:T(8,128)(2,1)S(1)} %get-tuple-element.342), channel_id=1, source_target_pairs={{0,4},{4,0},{8,12},{12,8},{16,20},{20,16},{24,28},{28,24},{1,5},{5... | collective-permute-start | bytes 884744 | tf_op jit(solution)/shard_map/ppermute | solution.py:928
  49.6 16.1 %copy-start.35 = (bf16[2,8,96,256]{3,2,1,0:T(8,128)(2,1)}, bf16[2,8,96,256]{3,2,1,0:T(8,128)(2,1)S(1)}, u32[]{:S(2)}) copy-start(bf16[2,8,96,256]{3,2,1,0:T(8,128)(2,1)S(1)} %collective-permute-done.12.br) | copy-start | bytes 2359300
  49.9 15.8 %copy-start.38 = (bf16[2,8,96,256]{3,2,1,0:T(8,128)(2,1)}, bf16[2,8,96,256]{3,2,1,0:T(8,128)(2,1)S(1)}, u32[]{:S(2)}) copy-start(bf16[2,8,96,256]{3,2,1,0:T(8,128)(2,1)S(1)} %collective-permute-done.11.ar) | copy-start | bytes 2359300
  65.9 19.3 %collective-permute-start.15 = (bf16[2,4,96,384]{3,2,1,0:T(8,128)(2,1)S(1)}, bf16[2,4,96,384]{3,2,1,0:T(8,128)(2,1)S(1)}, u32[]{:S(2)}, u32[]{:S(2)}) collective-permute-start(bf16[2,4,96,384]{3,2,1,0:T(8,128)(2,1)S(1)} %get-tuple-element.340), channel_id=1, source_target_pairs={{0,4},{4,0},{8,12},{12,8},{16,20},{20,16},{24,28},{28,24},{1,5},{5... | collective-permute-start | bytes 1769480 | tf_op jit(solution)/shard_map/ppermute | solution.py:928
  67.3 18.0 %collective-permute-start.16 = (bf16[4,2,96,384]{3,2,1,0:T(8,128)(2,1)S(1)}, bf16[4,2,96,384]{3,2,1,0:T(8,128)(2,1)S(1)}, u32[]{:S(2)}, u32[]{:S(2)}) collective-permute-start(bf16[4,2,96,384]{3,2,1,0:T(8,128)(2,1)S(1)} %pad_maximum_fusion.6), channel_id=1, source_target_pairs={{0,2},{1,3},{2,0},{3,1},{4,6},{5,7},{6,4},{7,5},{8,10},{9,11},{10,... | collective-permute-start | bytes 1769480 | tf_op jit(solution)/shard_map/ppermute | solution.py:928
  85.2 4.8 %collective-permute-start.17 = (bf16[528,1536]{1,0:T(8,128)(2,1)}, bf16[528,1536]{1,0:T(8,128)(2,1)S(1)}, u32[]{:S(2)}, u32[]{:S(2)}) collective-permute-start(bf16[528,1536]{1,0:T(8,128)(2,1)} %get-tuple-element.185), channel_id=1, source_target_pairs={{0,1},{2,3},{4,5},{6,7},{8,9},{10,11},{12,13},{14,15},{16,17},{18,... | collective-permute-start | bytes 4866056 | tf_op jit(solution)/shard_map/ppermute | solution.py:1162
  87.0 17.1 %copy-start.27 = (bf16[2,8,96,384]{3,2,1,0:T(8,128)(2,1)}, bf16[2,8,96,384]{3,2,1,0:T(8,128)(2,1)S(1)}, u32[]{:S(2)}) copy-start(bf16[2,8,96,384]{3,2,1,0:T(8,128)(2,1)S(1)} %pad_maximum_fusion.1.wom) | copy-start | bytes 3538948
  87.0 17.0 %collective-permute-start.19 = (bf16[2,8,96,384]{3,2,1,0:T(8,128)(2,1)S(1)}, bf16[2,8,96,384]{3,2,1,0:T(8,128)(2,1)S(1)}, u32[]{:S(2)}, u32[]{:S(2)}) collective-permute-start(bf16[2,8,96,384]{3,2,1,0:T(8,128)(2,1)S(1)} %pad_maximum_fusion.1.wom), channel_id=1, source_target_pairs={{0,1},{1,0},{2,3},{3,2},{4,5},{5,4},{6,7},{7,6},{8,9},{9,8},{10,11... | collective-permute-start | bytes 3538952 | tf_op jit(solution)/shard_map/ppermute | solution.py:928
  87.4 16.6 %collective-permute-start.18 = (bf16[2,8,96,384]{3,2,1,0:T(8,128)(2,1)S(1)}, bf16[2,8,96,384]{3,2,1,0:T(8,128)(2,1)S(1)}, u32[]{:S(2)}, u32[]{:S(2)}) collective-permute-start(bf16[2,8,96,384]{3,2,1,0:T(8,128)(2,1)S(1)} %bitcast.218), channel_id=1, source_target_pairs={{0,1},{1,0},{2,3},{3,2},{4,5},{5,4},{6,7},{7,6},{8,9},{9,8},{10,11... | collective-permute-start | bytes 3538952 | tf_op jit(solution)/shard_map/ppermute | solution.py:928
  91.2 21.4 %collective-permute-start.20 = (bf16[512,1536]{1,0:T(8,128)(2,1)S(1)}, bf16[512,1536]{1,0:T(8,128)(2,1)S(1)}, u32[]{:S(2)}, u32[]{:S(2)}) collective-permute-start(bf16[512,1536]{1,0:T(8,128)(2,1)S(1)} %fusion.3), channel_id=1, source_target_pairs={{1,2},{5,6},{9,10},{13,14},{17,18},{21,22},{25,26},{29,30}} | collective-permute-start | bytes 4718600 | tf_op jit(solution)/shard_map/ppermute | solution.py:1164
  112.6 0.8 collective-permute-start.21
  114.6 40.0 %copy-start.65 = (s32[16]{0:T(128)S(1)}, s32[16]{0:T(128)}, u32[]{:S(2)}) copy-start(s32[16]{0:T(128)} %copy-done.64) | copy-start | bytes 196
  153.2 20.9 %collective-permute-start.22 = (bf16[528,1536]{1,0:T(8,128)(2,1)}, bf16[528,1536]{1,0:T(8,128)(2,1)S(1)}, u32[]{:S(2)}, u32[]{:S(2)}) collective-permute-start(bf16[528,1536]{1,0:T(8,128)(2,1)} %get-tuple-element.210), channel_id=1, source_target_pairs={{1,0},{3,2},{5,4},{7,6},{9,8},{11,10},{13,12},{15,14},{17,16},{19,... | collective-permute-start | bytes 4866056 | tf_op jit(solution)/shard_map/ppermute | solution.py:1295
  171.7 25.3 %collective-permute-start.24 = (bf16[2,8,96,384]{3,2,1,0:T(8,128)(2,1)}, bf16[2,8,96,384]{3,2,1,0:T(8,128)(2,1)S(1)}, u32[]{:S(2)}, u32[]{:S(2)}) collective-permute-start(bf16[2,8,96,384]{3,2,1,0:T(8,128)(2,1)} %get-tuple-element.212), channel_id=1, source_target_pairs={{0,1},{1,0},{2,3},{3,2},{4,5},{5,4},{6,7},{7,6},{8,9},{9,8},{10,11... | collective-permute-start | bytes 3538952 | tf_op jit(solution)/shard_map/ppermute | solution.py:928
  174.2 47.3 %copy-start.7 = (bf16[528,1536]{1,0:T(8,128)(2,1)}, bf16[528,1536]{1,0:T(8,128)(2,1)S(1)}, u32[]{:S(2)}) copy-start(bf16[528,1536]{1,0:T(8,128)(2,1)S(1)} %collective-permute-done.22.q1) | copy-start | bytes 4866052
  174.2 22.8 %collective-permute-start.23 = (bf16[2,8,96,384]{3,2,1,0:T(8,128)(2,1)}, bf16[2,8,96,384]{3,2,1,0:T(8,128)(2,1)S(1)}, u32[]{:S(2)}, u32[]{:S(2)}) collective-permute-start(bf16[2,8,96,384]{3,2,1,0:T(8,128)(2,1)} %get-tuple-element.211), channel_id=1, source_target_pairs={{0,1},{1,0},{2,3},{3,2},{4,5},{5,4},{6,7},{7,6},{8,9},{9,8},{10,11... | collective-permute-start | bytes 3538952 | tf_op jit(solution)/shard_map/ppermute | solution.py:928
  174.8 22.2 %copy-start.89 = (bf16[2,8,96,384]{3,2,1,0:T(8,128)(2,1)S(1)}, bf16[2,8,96,384]{3,2,1,0:T(8,128)(2,1)}, u32[]{:S(2)}) copy-start(bf16[2,8,96,384]{3,2,1,0:T(8,128)(2,1)} %get-tuple-element.222) | copy-start | bytes 3538948
  174.8 36.8 %collective-permute-start.25 = (bf16[512,1536]{1,0:T(8,128)(2,1)S(1)}, bf16[512,1536]{1,0:T(8,128)(2,1)S(1)}, u32[]{:S(2)}, u32[]{:S(2)}) collective-permute-start(bf16[512,1536]{1,0:T(8,128)(2,1)S(1)} %fusion.1), channel_id=1, source_target_pairs={{2,1},{6,5},{10,9},{14,13},{18,17},{22,21},{26,25},{30,29}} | collective-permute-start | bytes 4718600 | tf_op jit(solution)/shard_map/ppermute | solution.py:1313
  198.0 16.2 %collective-permute-start.26 = (bf16[2,4,96,384]{3,2,1,0:T(8,128)(2,1)S(1)}, bf16[2,4,96,384]{3,2,1,0:T(8,128)(2,1)S(1)}, u32[]{:S(2)}, u32[]{:S(2)}) collective-permute-start(bf16[2,4,96,384]{3,2,1,0:T(8,128)(2,1)S(1)} %slice_bitcast_fusion.3), channel_id=1, source_target_pairs={{0,4},{4,0},{8,12},{12,8},{16,20},{20,16},{24,28},{28,24},{1,5},{5... | collective-permute-start | bytes 1769480 | tf_op jit(solution)/shard_map/ppermute | solution.py:928
  214.2 7.3 %collective-permute-start.27 = (bf16[512,1536]{1,0:T(8,128)(2,1)S(1)}, bf16[512,1536]{1,0:T(8,128)(2,1)S(1)}, u32[]{:S(2)}, u32[]{:S(2)}) collective-permute-start(bf16[512,1536]{1,0:T(8,128)(2,1)S(1)} %collective-permute-done.25.q2), channel_id=1, source_target_pairs={{1,0},{5,4},{9,8},{13,12},{17,16},{21,20},{25,24},{29,28}} | collective-permute-start | bytes 4718600 | tf_op jit(solution)/shard_map/ppermute | solution.py:1497
  216.9 20.9 %collective-permute-start.29 = (bf16[2,4,96,384]{3,2,1,0:T(8,128)(2,1)S(1)}, bf16[2,4,96,384]{3,2,1,0:T(8,128)(2,1)S(1)}, u32[]{:S(2)}, u32[]{:S(2)}) collective-permute-start(bf16[2,4,96,384]{3,2,1,0:T(8,128)(2,1)S(1)} %slice_bitcast_fusion.1), channel_id=1, source_target_pairs={{0,4},{4,0},{8,12},{12,8},{16,20},{20,16},{24,28},{28,24},{1,5},{5... | collective-permute-start | bytes 1769480 | tf_op jit(solution)/shard_map/ppermute | solution.py:928
  218.1 19.7 %collective-permute-start.28 = (bf16[4,96,384]{2,1,0:T(8,128)(2,1)S(1)}, bf16[4,96,384]{2,1,0:T(8,128)(2,1)S(1)}, u32[]{:S(2)}, u32[]{:S(2)}) collective-permute-start(bf16[4,96,384]{2,1,0:T(8,128)(2,1)S(1)} %slice_bitcast_fusion.9), channel_id=1, source_target_pairs={{0,2},{1,3},{2,0},{3,1},{4,6},{5,7},{6,4},{7,5},{8,10},{9,11},{10,... | collective-permute-start | bytes 884744 | tf_op jit(solution)/shard_map/ppermute | solution.py:928
  221.5 16.3 %copy-start.23 = (bf16[512,1536]{1,0:T(8,128)(2,1)}, bf16[512,1536]{1,0:T(8,128)(2,1)S(1)}, u32[]{:S(2)}) copy-start(bf16[512,1536]{1,0:T(8,128)(2,1)S(1)} %collective-permute-done.27.q3) | copy-start | bytes 4718596
  221.6 19.1 %copy-start.5 = (bf16[2,1024,768]{2,1,0:T(8,128)(2,1)S(1)}, bf16[2,1024,768]{2,1,0:T(8,128)(2,1)}, u32[]{:S(2)}) copy-start(bf16[2,1024,768]{2,1,0:T(8,128)(2,1)} %get-tuple-element.234.dg) | copy-start | bytes 9437188
  238.8 5.8 %collective-permute-start.30 = (bf16[8,96,384]{2,1,0:T(8,128)(2,1)S(1)}, bf16[8,96,384]{2,1,0:T(8,128)(2,1)S(1)}, u32[]{:S(2)}, u32[]{:S(2)}) collective-permute-start(bf16[8,96,384]{2,1,0:T(8,128)(2,1)S(1)} %copy-done.94), channel_id=1, source_target_pairs={{0,1},{1,0},{2,3},{3,2},{4,5},{5,4},{6,7},{7,6},{8,9},{9,8},{10,11... | collective-permute-start | bytes 1769480 | tf_op jit(solution)/shard_map/ppermute | solution.py:928
  239.7 33.5 %collective-permute-start.32 = (bf16[4,96,384]{2,1,0:T(8,128)(2,1)}, bf16[4,96,384]{2,1,0:T(8,128)(2,1)}, u32[]{:S(2)}, u32[]{:S(2)}) collective-permute-start(bf16[4,96,384]{2,1,0:T(8,128)(2,1)} %slice_bitcast_fusion.8), channel_id=1, source_target_pairs={{0,2},{1,3},{2,0},{3,1},{4,6},{5,7},{6,4},{7,5},{8,10},{9,11},{10,... | collective-permute-start | bytes 884744 | tf_op jit(solution)/shard_map/ppermute | solution.py:928
  244.7 31.9 %copy-start.79 = (bf16[4,96,384]{2,1,0:T(8,128)(2,1)}, bf16[4,96,384]{2,1,0:T(8,128)(2,1)S(1)}, u32[]{:S(2)}) copy-start(bf16[4,96,384]{2,1,0:T(8,128)(2,1)S(1)} %fusion.9) | copy-start | bytes 884740
  245.7 27.6 %collective-permute-start.31 = (bf16[8,96,384]{2,1,0:T(8,128)(2,1)}, bf16[8,96,384]{2,1,0:T(8,128)(2,1)}, u32[]{:S(2)}, u32[]{:S(2)}) collective-permute-start(bf16[8,96,384]{2,1,0:T(8,128)(2,1)} %add_convert_fusion.4), channel_id=1, source_target_pairs={{0,2},{1,3},{2,0},{3,1},{4,6},{5,7},{6,4},{7,5},{8,10},{9,11},{10,... | collective-permute-start | bytes 1769480 | tf_op jit(solution)/shard_map/ppermute | solution.py:928
  246.9 28.5 %copy-start.82 = (bf16[2,4,96,384]{3,2,1,0:T(8,128)(2,1)S(1)}, bf16[2,4,96,384]{3,2,1,0:T(8,128)(2,1)}, u32[]{:S(2)}) copy-start(bf16[2,4,96,384]{3,2,1,0:T(8,128)(2,1)} %copy-done.81) | copy-start | bytes 1769476
  246.9 36.3 %copy-start.37 = (bf16[2,8,96,256]{3,2,1,0:T(8,128)(2,1)S(1)}, bf16[2,8,96,256]{3,2,1,0:T(8,128)(2,1)}, u32[]{:S(2)}) copy-start(bf16[2,8,96,256]{3,2,1,0:T(8,128)(2,1)} %copy-done.35) | copy-start | bytes 2359300
  246.9 36.3 %copy-start.40 = (bf16[2,8,96,256]{3,2,1,0:T(8,128)(2,1)S(1)}, bf16[2,8,96,256]{3,2,1,0:T(8,128)(2,1)}, u32[]{:S(2)}) copy-start(bf16[2,8,96,256]{3,2,1,0:T(8,128)(2,1)} %copy-done.38) | copy-start | bytes 2359300
  273.3 3.5 %collective-permute-start.33 = (bf16[8,96,640]{2,1,0:T(8,128)(2,1)}, bf16[8,96,640]{2,1,0:T(8,128)(2,1)}, u32[]{:S(2)}, u32[]{:S(2)}) collective-permute-start(bf16[8,96,640]{2,1,0:T(8,128)(2,1)} %get-tuple-element.256), channel_id=1, source_target_pairs={{0,1},{1,0},{2,3},{3,2},{4,5},{5,4},{6,7},{7,6},{8,9},{9,8},{10,11... | collective-permute-start | bytes 2949128 | tf_op jit(solution)/shard_map/ppermute | solution.py:928
  274.9 1.9 collective-permute-start.34
  276.6 18.0 %collective-permute-start.38 = (bf16[2,2,96,384]{3,2,1,0:T(8,128)(2,1)S(1)}, bf16[2,2,96,384]{3,2,1,0:T(8,128)(2,1)S(1)}, u32[]{:S(2)}, u32[]{:S(2)}) collective-permute-start(bf16[2,2,96,384]{3,2,1,0:T(8,128)(2,1)S(1)} %fusion.13), channel_id=1, source_target_pairs={{0,8},{4,12},{8,0},{12,4},{16,24},{20,28},{24,16},{28,20},{1,9},{5... | collective-permute-start | bytes 884744 | tf_op jit(solution)/shard_map/ppermute | solution.py:928
  276.8 17.8 %collective-permute-start.37 = (f32[24,384]{1,0:T(8,128)S(1)}, f32[24,384]{1,0:T(8,128)S(1)}, u32[]{:S(2)}, u32[]{:S(2)}) collective-permute-start(f32[24,384]{1,0:T(8,128)S(1)} %pad_maximum_fusion.18), channel_id=1, source_target_pairs={{0,2},{1,3},{2,0},{3,1},{4,6},{5,7},{6,4},{7,5},{8,10},{9,11},{10,... | collective-permute-start | bytes 110600 | tf_op jit(solution)/shard_map/ppermute | solution.py:928
  281.0 13.6 %collective-permute-start.36 = (bf16[4,96,384]{2,1,0:T(8,128)(2,1)S(1)}, bf16[4,96,384]{2,1,0:T(8,128)(2,1)S(1)}, u32[]{:S(2)}, u32[]{:S(2)}) collective-permute-start(bf16[4,96,384]{2,1,0:T(8,128)(2,1)S(1)} %slice_bitcast_fusion.7), channel_id=1, source_target_pairs={{0,4},{4,0},{8,12},{12,8},{16,20},{20,16},{24,28},{28,24},{1,5},{5... | collective-permute-start | bytes 884744 | tf_op jit(solution)/shard_map/ppermute | solution.py:928
  282.0 12.7 %collective-permute-start.35 = (bf16[8,96,128]{2,1,0:T(8,128)(2,1)S(1)}, bf16[8,96,128]{2,1,0:T(8,128)(2,1)S(1)}, u32[]{:S(2)}, u32[]{:S(2)}) collective-permute-start(bf16[8,96,128]{2,1,0:T(8,128)(2,1)S(1)} %slice.303), channel_id=1, source_target_pairs={{0,2},{1,3},{2,0},{3,1},{4,6},{5,7},{6,4},{7,5},{8,10},{9,11},{10,... | collective-permute-start | bytes 589832 | tf_op jit(solution)/shard_map/ppermute | solution.py:928
  287.4 19.5 %copy-start.26 = (bf16[4,256,768]{2,1,0:T(8,128)(2,1)S(1)}, bf16[4,256,768]{2,1,0:T(8,128)(2,1)}, u32[]{:S(2)}) copy-start(bf16[4,256,768]{2,1,0:T(8,128)(2,1)} %param.19) | copy-start | bytes 4718596
  294.8 9.1 %collective-permute-start.42 = (bf16[2,1,96,384]{3,2,0,1:T(8,128)(2,1)S(1)}, bf16[2,1,96,384]{3,2,0,1:T(8,128)(2,1)S(1)}, u32[]{:S(2)}, u32[]{:S(2)}) collective-permute-start(bf16[2,1,96,384]{3,2,0,1:T(8,128)(2,1)S(1)} %slice_bitcast_fusion.15), channel_id=1, source_target_pairs={{0,16},{4,20},{8,24},{12,28},{16,0},{20,4},{24,8},{28,12},{1,17},{... | collective-permute-start | bytes 442376 | tf_op jit(solution)/shard_map/ppermute | solution.py:928
  294.9 4.8 %collective-permute-start.41 = (f32[24,384]{1,0:T(8,128)S(1)}, f32[24,384]{1,0:T(8,128)S(1)}, u32[]{:S(2)}, u32[]{:S(2)}) collective-permute-start(f32[24,384]{1,0:T(8,128)S(1)} %fusion.27), channel_id=1, source_target_pairs={{0,4},{4,0},{8,12},{12,8},{16,20},{20,16},{24,28},{28,24},{1,5},{5... | collective-permute-start | bytes 110600 | tf_op jit(solution)/shard_map/ppermute | solution.py:928
  296.0 4.7 %collective-permute-start.40 = (bf16[4,96,128]{2,1,0:T(8,128)(2,1)S(1)}, bf16[4,96,128]{2,1,0:T(8,128)(2,1)S(1)}, u32[]{:S(2)}, u32[]{:S(2)}) collective-permute-start(bf16[4,96,128]{2,1,0:T(8,128)(2,1)S(1)} %slice_bitcast_fusion.19), channel_id=1, source_target_pairs={{0,4},{4,0},{8,12},{12,8},{16,20},{20,16},{24,28},{28,24},{1,5},{5... | collective-permute-start | bytes 294920 | tf_op jit(solution)/shard_map/ppermute | solution.py:928
  298.1 3.5 %collective-permute-start.39 = (bf16[64,768]{1,0:T(8,128)(2,1)S(1)}, bf16[64,768]{1,0:T(8,128)(2,1)S(1)}, u32[]{:S(2)}, u32[]{:S(2)}) collective-permute-start(bf16[64,768]{1,0:T(8,128)(2,1)S(1)} %slice.422), channel_id=1, source_target_pairs={{1,0},{2,1},{3,2},{5,4},{6,5},{7,6},{9,8},{10,9},{11,10},{13,12},{... | collective-permute-start | bytes 294920 | tf_op jit(solution)/shard_map/ppermute | solution.py:1598
  303.9 6.3 %collective-permute-start.44 = (f32[24,384]{1,0:T(8,128)S(1)}, f32[24,384]{1,0:T(8,128)S(1)}, u32[]{:S(2)}, u32[]{:S(2)}) collective-permute-start(f32[24,384]{1,0:T(8,128)S(1)} %add.117), channel_id=1, source_target_pairs={{0,8},{4,12},{8,0},{12,4},{16,24},{20,28},{24,16},{28,20},{1,9},{5... | collective-permute-start | bytes 110600 | tf_op jit(solution)/shard_map/ppermute | solution.py:928
  304.0 7.9 %collective-permute-start.43 = (bf16[2,96,512]{2,1,0:T(8,128)(2,1)S(1)}, bf16[2,96,512]{2,1,0:T(8,128)(2,1)S(1)}, u32[]{:S(2)}, u32[]{:S(2)}) collective-permute-start(bf16[2,96,512]{2,1,0:T(8,128)(2,1)S(1)} %slice_bitcast_fusion.13), channel_id=1, source_target_pairs={{0,8},{4,12},{8,0},{12,4},{16,24},{20,28},{24,16},{28,20},{1,9},{5... | collective-permute-start | bytes 589832 | tf_op jit(solution)/shard_map/ppermute | solution.py:928
  306.9 17.2 %copy-start.1 = (bf16[96,256]{1,0:T(8,128)(2,1)S(1)}, bf16[96,256]{1,0:T(8,128)(2,1)}, u32[]{:S(2)}) copy-start(bf16[96,256]{1,0:T(8,128)(2,1)} %param.23) | copy-start | bytes 147460
  312.0 5.3 %collective-permute-start.45 = (f32[24,384]{1,0:T(8,128)S(1)}, f32[24,384]{1,0:T(8,128)S(1)}, u32[]{:S(2)}, u32[]{:S(2)}) collective-permute-start(f32[24,384]{1,0:T(8,128)S(1)} %add.118), channel_id=1, source_target_pairs={{0,16},{4,20},{8,24},{12,28},{16,0},{20,4},{24,8},{28,12},{1,17},{... | collective-permute-start | bytes 110600 | tf_op jit(solution)/shard_map/ppermute | solution.py:928
  313.9 7.9 %collective-permute-start.46 = (bf16[1,96,512]{2,1,0:T(8,128)(2,1)S(1)}, bf16[1,96,512]{2,1,0:T(8,128)(2,1)S(1)}, u32[]{:S(2)}, u32[]{:S(2)}) collective-permute-start(bf16[1,96,512]{2,1,0:T(8,128)(2,1)S(1)} %slice_bitcast_fusion.16), channel_id=1, source_target_pairs={{0,16},{4,20},{8,24},{12,28},{16,0},{20,4},{24,8},{28,12},{1,17},{... | collective-permute-start | bytes 294920 | tf_op jit(solution)/shard_map/ppermute | solution.py:928
  (78 other events, 397.0 us)

commit v3 on v2

--- a/solution.py
+++ b/solution.py
@@ -166,11 +166,27 @@
     return pl.ds(pl.multiple_of(384 * (c ^ (me_t % 2)), 128), 384)
 
 
+def k0_body(sc, conv_x, bias_x, out_gain, dt_bias, a_log, skip_d, norm_gain, bias_bc, par, gain, bbc, row):
+    par[...] = jnp.zeros_like(par)
+    par[0:4] = conv_x[...]
+    par[4] = bias_x[...]
+    par[5] = out_gain[...]
+    par[6, : dt_bias.shape[0]] = dt_bias[...]
+    par[7, : a_log.shape[0]] = a_log[...]
+    row[...] = jnp.zeros_like(row)
+    row[0, : skip_d.shape[0]] = skip_d[...]
+    r = lax.broadcasted_iota(jnp.int32, (128, 384), 0)
+    c = lax.broadcasted_iota(jnp.int32, (128, 384), 1)
+    par[8:9] = dot_high(row[...], jnp.where(r == c // HD, 1.0, 0.0))[0:1]
+    gain[0] = norm_gain[...]
+    bbc[0] = bias_bc[...]
+
+
 def k1_body(
     sc, tok, halo, gain, am, ar, bm, br, par, cbc, bbc,
     nrm, inx, blow, clow, bto, sin, dbc,
     cumo, stepo, sigo, eto, reacho, decayo, faco, uvo, masko, backo, ct,
-    wbuf, wpc, pcs, dtacc, ext,
+    wbuf, wbc, wdt, pcs, ext,
 ):
     g = pl.program_id(0)
     me_t, me_dp = sc[8], sc[9]
@@ -187,34 +203,40 @@
             nrm[rows_of(s, 64)] = norm(tok[rows_of(s, 64)])
 
         nrm[4 * L :] = norm(halo[...])
-        dtacc[...] = jnp.zeros_like(dtacc)
-        sin[...] = jnp.zeros_like(sin)
-
-    place_p1(wbuf, am, bm, ar, br, me_dp, wpc)
+        wbc[...] = jnp.zeros_like(wbc)
+        wdt[...] = jnp.zeros_like(wdt)
+
+    place_rows(wbuf, am, me_dp, 0)
+    place_rows(wbuf, bm, me_dp, 256, 0, 128)
+    place_rows(wbuf, ar, me_dp, 384)
+    place_rows(wbuf, br, me_dp, 640, 0, 128)
+    count, brow = bm.shape[1:3]
+    for c, blocks in ((0, bm), (1, br)):
+        i = 2 * g + c
+        t = i ^ me_t
+        at = pl.ds(pl.multiple_of(128 * (t // 2), 128), 128)
+        for n in range(count):
+            start = pl.multiple_of((n ^ me_dp) * brow, brow) if count > 1 else 0
+            r = pl.ds(start, brow)
+            piece = blocks[0, n, :, 128:].astype(F32)
+            lane = lane_iota(brow)
+            own = pltpu.roll(jnp.where(lane < 64, piece, 0.0), 64 * (t % 2), 1)
+            wbc[r, at] += own.astype(BF)
+            own = pltpu.roll(jnp.where(lane >= 64, piece, 0.0), (i * 6 + 64) % 128, 1)
+            wdt[r] += own.astype(BF)
     for n in range(3):
         cols = slice(256 * n, 256 * n + 256)
         inx[0, :, cols] = dot(nrm[...], wbuf[:, cols]).astype(BF)
-    pcs[...] = dot(nrm[...], wpc[...])
-
-    for c in range(2):
-        i = 2 * g + c
-        t = i ^ me_t
-        turn = 64 * (t % 2)
-
-        @pl.loop(0, 4)
-        def _(s):
-            last = pcs[rows_of(s), tile(c)]
-            lane = lane_iota(L)
-            sin[t // 2, rows_of(s)] += pltpu.roll(jnp.where(lane < 64, last, 0.0), turn, 1)
-            dtacc[...] += pltpu.roll(
-                jnp.where(lane >= 64, last, 0.0), (s * SPAN + i * 6 + 64) % 128, 1
-            )
-
-        last = pcs[4 * L :, tile(c)]
-        sin[t // 2, 4 * L :] += pltpu.roll(jnp.where(lane_iota(64) < 64, last, 0.0), turn, 1)
 
     @pl.when(g == 1)
     def _():
+        pcs[...] = dot(nrm[...], wbc[...])
+        sin[0] = pcs[:, :128]
+        sin[1] = pcs[:, 128:]
+        pcs[0 : 4 * L, 0:128] = dot(nrm[0 : 4 * L], wdt[...])
+        dtacc = pcs[0:L, 0:128]
+        for s in range(1, 4):
+            dtacc = dtacc + pltpu.roll(pcs[L * s : L * s + L, 0:128], s * SPAN, 1)
         dtb = jnp.zeros((1, 128), F32)
         alog = jnp.zeros((1, 128), F32)
         for i in range(4):
@@ -222,7 +244,7 @@
                 at = slice(384 * (i % 2), 384 * (i % 2) + 128)
                 dtb += pltpu.roll(par[i // 2, 6:7, at], s * SPAN + i * 6, 1)
                 alog += pltpu.roll(par[i // 2, 7:8, at], s * SPAN + i * 6, 1)
-        raw = dtacc[...] + dtb
+        raw = dtacc + dtb
         step = jnp.maximum(raw, 0.0) + jnp.log1p(jnp.exp(-jnp.abs(raw)))
         sig = 1.0 / (1.0 + jnp.exp(-raw))
         decay = step * -jnp.exp(alog)
@@ -653,9 +675,9 @@
 ):
     if last:
         (
-            fac, sigp, decay, gain, ngz, nga, cbc, bc7a, bc7b, corr_a, corr_b, dc3, rowsum, sin, dbc, sega, enda, dba,
-            keep, send, din, seg, end, dba_o, small, ngx, din5, sbc, sdt, ngo,
-            val, hsum, gsc, gf, glow, xe, seg_h, seg_l, pick, wbuf, wpc, gbuf, pcs, pblk, ub, ext, spread, stepx, etx,
+            fac, sigp, decay, gain, ngz, nga, cbc, small1, small5, bc7a, bc7b, corr_a, corr_b, dc3, rowsum, sin, dbc, sega, enda, dba,
+            keep, send, din, seg, end, dba_o, small, ngx, din5, skeep, ssend,
+            val, hsum, gsc, gf, glow, xe, seg_h, seg_l, pick, wbuf, wpc, gbuf, pcs, pblk, sbc, spack, ub, ext, spread, stepx, etx,
         ) = rest
     else:
         (
@@ -793,7 +815,7 @@
         step_all, sig = stepp[...], sigp[...]
         ratio = jnp.where(step_all > 1e-30, sig / jnp.maximum(step_all, 1e-30), 1.0)
         ddt = ratio * col - sig * jnp.exp(alog) * dlog
-        sdt[...] = jnp.concatenate(
+        dts = jnp.concatenate(
             [
                 jnp.sum(ddt, axis=0, keepdims=True),
                 jnp.sum(dlog * decay[...], axis=0, keepdims=True),
@@ -801,6 +823,21 @@
             ],
             axis=0,
         )
+        dts = dts + pltpu.roll(dts, 64, 1)
+        dts = dts + pltpu.roll(dts, 32, 1)
+        spack[...] = jnp.zeros_like(spack)
+        for x in range(2):
+            spack[x, 0:5] = (small if x == 0 else small1)[0:5]
+            spack[x, 5:7] = small5[x, 0:2]
+            for c in range(2):
+                own = pltpu.roll(dts, (128 - 6 * (2 * x + c)) % 128, 1)
+                own = jnp.where(lane_iota(8) < 6, own, 0.0)
+                spack[x, 7:9, 384 * c : 384 * c + 128] = own[0:2]
+            skeep[16 * x : 16 * x + 16] = spack[x, :, :384]
+            ssend[16 * x : 16 * x + 16] = spack[x, :, 384:]
+        ssend[32:40] = jnp.zeros((8, 384), F32)
+        for q in range(2):
+            ssend[32:37, tile(q)] = sbc[q, 0:5]
         for n in range(4):
             t = n ^ me_t
             turn = (64 * (t % 2)) % 128
@@ -825,7 +862,7 @@
             place_rows(wpc, bm, me_dp, 256 * n, 128, 128, n)
             place_rows(wpc, br, me_dp, 256 * n + 128, 128, 128, n)
         add_weighted(ngx, pcs, wpc, (0,))
-        ngo[...] = (
+        gain_grad = (
             lax.dot_general(
                 jnp.ones((8, 128), F32),
                 ngx[...],
@@ -835,6 +872,8 @@
             )
             / gain[...]
         )
+        ssend[37:38] = gain_grad[0:1, :384]
+        ssend[38:39] = gain_grad[0:1, 384:]
         count, brow = keep.shape[0], keep.shape[1]
         for n in range(4):
             ref = keep if n % 2 == 0 else send
@@ -892,6 +931,43 @@
     ig[...] = (res + r * (gd - tr * inner)).astype(BF)
 
 
+def FINAL_SHAPES(dim, cols, heads, state, shard, tcount):
+    return [
+        (dim,), (shard, cols), (shard // tcount, 2 * state), (heads, shard), (4, cols), (cols,),
+        (4, 2 * state), (2 * state,), (heads,), (heads,), (heads,), (cols,),
+    ]
+
+
+def k11_body(
+    sc, va, vr, both, got,
+    ngain, wx, wbc, wdt, cx, bx, cb, bb, dtb, alog, skip, og,
+    g, sm,
+):
+    g[...] = va[...].astype(F32) + vr[...].astype(F32)
+    sm[...] = both[...] + got[...]
+    wx[...] = g[:, :384]
+    quarter = g.shape[0] // 4
+    lane = lane_iota(quarter)
+    parts = [g[quarter * c : quarter * c + quarter, 384:512] for c in range(4)]
+    for t in range(2):
+        wbc[:, tile(t)] = jnp.where(lane < 64, parts[2 * t], pltpu.roll(parts[2 * t + 1], 64, 1))
+    wdt[...] = pltpu.roll(g[:, 384:512], 64, 1).T[: wdt.shape[0]]
+    cx[...] = sm[0:4]
+    bx[...] = sm[4]
+    og[...] = sm[5]
+    r = lax.broadcasted_iota(jnp.int32, (384, 128), 0)
+    c = lax.broadcasted_iota(jnp.int32, (384, 128), 1)
+    sums = dot_high(sm[0:8], jnp.where(c == r // HD, 1.0, 0.0))
+    skip[...] = sums[6, : skip.shape[0]]
+    dtb[...] = sm[7, : dtb.shape[0]]
+    alog[...] = sm[8, : alog.shape[0]]
+    cb[...] = sm[16:20, : cb.shape[1]]
+    bb[...] = sm[20, : bb.shape[0]]
+    half = sm.shape[1]
+    ngain[0:half] = sm[21]
+    ngain[half : 2 * half] = sm[22]
+
+
 def full(shape):
     return pl.BlockSpec(shape, lambda *a: (0,) * len(shape))
 
@@ -960,7 +1036,6 @@
     ).astype(jnp.int32)
     tok = tokens.reshape(rows, dim)
     cot = cotangent.reshape(rows, dim)
-    gain = norm_gain.reshape(1, dim)
 
     bq = w_bc.shape[1] // tcount
     state = w_bc.shape[1] // 2
@@ -981,19 +1056,20 @@
     def core(v):
         return flip(v, "tensor", 1)
 
-    par = jnp.concatenate(
+    par, gain, bbc = call(
+        k0_body,
+        (1,),
         [
-            conv_x,
-            bias_x[None],
-            out_gain[None],
-            jnp.pad(dt_bias, (0, cols - heads))[None],
-            jnp.pad(a_log, (0, cols - heads))[None],
-            jnp.repeat(skip_d, cols // heads)[None],
-            jnp.zeros((7, cols), F32),
+            full(v.shape)
+            for v in (conv_x, bias_x, out_gain, dt_bias, a_log, skip_d, norm_gain, bias_bc)
         ],
-        axis=0,
-    )
-    bbc = bias_bc.reshape(1, -1)
+        [full((16, cols)), full((1, dim)), full((1, 2 * state))],
+        [sds((16, cols), F32), sds((1, dim), F32), sds((1, 2 * state), F32)],
+        [pltpu.VMEM((8, 128), F32)],
+        (1, 1),
+        "parameters",
+        vmem_mib=K5_MIB,
+    )(sc, conv_x, bias_x, out_gain, dt_bias, a_log, skip_d, norm_gain, bias_bc)
 
     def grown(v, got, at):
         v = jnp.stack([v, got], axis=at)
@@ -1080,8 +1156,8 @@
         [
             vmem((dim, wide), BF),
             vmem((dim, 256), BF),
+            vmem((dim, 128), BF),
             vmem((erows, 256), F32),
-            vmem((L, 128), F32),
             vmem((L + 8, 128), F32),
         ],
         (int(7e9), int(2e7)),
@@ -1306,6 +1382,7 @@
         [vmem((dim, rows), BF), vmem((dim, wide), F32), vmem((dim, wide), BF)],
         (int(5e9), int(2e7)),
         "outer_weight_grads",
+        vmem_mib=K5_MIB,
     )(sc, nrm, dbr, gn, dg, wzm, wzr)
 
     osend, q1 = meet(osend, q1)
@@ -1448,12 +1525,14 @@
             vmem((dim, wide), BF),
         ]
         if last:
-            outs += [((erows, 512), BF), ((2, 8, state), F32), ((8, 128), F32), ((8, dim), F32)]
+            outs += [((erows, 512), BF), ((32, cols), F32), ((40, cols), F32)]
             scratch += [
                 vmem((dim, 512), BF),
                 vmem((2, erows, state), F32),
                 vmem((4, dim, 128), F32),
                 vmem((brow, 128), F32),
+                vmem((2, 8, state), F32),
+                vmem((2, 16, wide), F32),
             ]
         scratch += [vmem((L, wide), F32), vmem((6, L + 16, 128), F32), vmem((256, wide), BF)]
         scratch += [vmem((L, wide), F32), vmem((L, wide), F32)]
@@ -1507,11 +1586,11 @@
     nt0, sar, dnb = meet(nt, sar, dnb)
     va = summed(ka, sar)
     xa = flip(va, "tensor", 2)
-    ks, ss, din0, _, _, _, small0, _, din5, sbc, sdt, ngo = states_backward(
+    ks, ss, din0, _, _, _, _, _, din5, skeep, ssend = states_backward(
         0,
         True,
         nt0,
-        [fac, sigp, decay, gain, ngz, nga, conv_bc, bc7a, bc7b, corr_a, corr_b, dc5, rowsum, sin, dbc, seg1, end1, dba1],
+        [fac, sigp, decay, gain, ngz, nga, conv_bc, small1, small5, bc7a, bc7b, corr_a, corr_b, dc5, rowsum, sin, dbc, seg1, end1, dba1],
         [
             full((8, 128)),
             full((L, 128)),
@@ -1520,6 +1599,8 @@
             full((dim, 128)),
             full((dim, 128)),
             full((4, 2 * state)),
+            full((8, wide)),
+            full((2, 8, wide)),
             full((2, rows, state)),
             full((2, rows, state)),
             full((L, 128)),
@@ -1538,29 +1619,12 @@
         ss, xa, vzr = meet(ss, xa, vzr)
         vw = jnp.stack([vo, summed(vz[0], vzr)]).reshape((2, count // 4, 2, brow, cols))
         vwr = flip(vw[:, :, 1], "dp", 2)
-    dts = sdt[:2].reshape(2, slots, SPAN)[:, :, : 4 * heads].sum(axis=1).reshape(2, 2, 2, heads)
-    dts = jnp.pad(dts, ((0, 0), (0, 0), (0, 0), (0, cols - heads)))
-    dts = jnp.swapaxes(dts, 0, 1).reshape(2, 2, wide)
-    mine = jnp.concatenate(
-        [
-            jnp.stack([small0[:5], small1[:5]]),
-            small5[:, :2],
-            dts,
-            jnp.zeros((2, 7, wide), F32),
-        ],
-        axis=1,
-    )
-    flat = jnp.concatenate(
-        [jnp.concatenate([sbc[0, :5], sbc[1, :5]], axis=1).reshape(-1), ngo[0]]
-    )
-    flat = jnp.pad(flat, (0, 8 * cols - flat.shape[0])).reshape(8, cols)
-    send = jnp.concatenate([mine[:, :, cols:].reshape(32, cols), flat], axis=0)
-    din0, ssr, got = meet(din0, core(ss), core(send))
-    own = mine[:, :, :cols] + got[:32].reshape(2, 16, cols)
-    flat = flat + got[32:]
-    vb = summed(ks, ssr)
-    px = flip(vb[..., cols + 128 :], "tensor", 2)
-    vx = summed(vb[..., :cols], xa)
+    din0, ssr, got = meet(din0, core(ss), core(ssend))
+    own = (skeep + got[:32]).reshape(2, 16, cols)
+    flat = ssend[32:] + got[32:]
+    vb = summed(ks[..., cols:], ssr[..., cols:])
+    px = flip(vb[..., 128:], "tensor", 2)
+    vx = (ks[..., :cols].astype(F32) + ssr[..., :cols].astype(F32) + xa.astype(F32)).astype(BF)
     if fast:
         vx = vx.reshape((count // 2, 2) + vx.shape[1:])
         vxr = flip(vx[:, 1], "dp", 1)
@@ -1590,16 +1654,14 @@
         vw = summed(vw[:, :, 0], vwr).reshape((2, count // 8, 2, brow, cols))
         vwr = flip(vw[:, :, 1], "dp", 4)
         vx = summed(vx[:, 0], vxr)
-        vp = summed(vb[..., cols : cols + 128], px)
+        vp = summed(vb[..., :128], px)
         vp = vp.reshape((count // 2, 2) + vp.shape[1:])
         vpr = flip(vp[:, 1], "dp", 1)
         both = both + got
         got = flip(both, "dp", 1)
     hr = lax.ppermute(dn[rows:].astype(BF), "tensor", [(a + 1, a) for a in range(tcount - 1)])
     if fast:
-        hr, vpr, got, vwr = meet(hr, vpr, got, vwr)
-        vw = summed(vw[:, :, 0], vwr)
-        grad_w_out, grad_w_z = finish(vw[0], 8), finish(vw[1], 8)
+        hr, vpr, got = meet(hr, vpr, got)
         v1 = jnp.concatenate([vx, summed(vp[:, 0], vpr)], axis=-1)
         v1 = v1.reshape((count // 4, 2) + v1.shape[1:])
         v1r = flip(v1[:, 1], "dp", 2)
@@ -1624,48 +1686,71 @@
     )(sc, dn, hr, tok, cot, gain)
 
     if fast:
-        ig, v1r, got = meet(ig, v1r, got)
+        ig, v1r, got, vwr = meet(ig, v1r, got, vwr)
+        vw = summed(vw[:, :, 0], vwr)
+        grad_w_out, grad_w_z = finish(vw[0], 8), finish(vw[1], 8)
         v1 = summed(v1[:, 0], v1r)
         both = both + got
         bit = 4
-        while bit < dpcount:
+        while 2 * bit < dpcount:
             both = both + flip(both, "dp", bit)
             v1 = reduce_dp(v1, bit)
             bit *= 2
-        grad1 = v1[0].astype(F32)
+        got = flip(both, "dp", bit)
+        v1 = v1.reshape((2,) + v1.shape[1:]) if v1.shape[0] == 2 else v1
+        v1a, v1r = v1[0], flip(v1[1], "dp", bit)
     else:
         both = lax.psum(both + got, "dp")
-        v1 = jnp.concatenate([vx, summed(vb[..., cols : cols + 128], px)], axis=-1)
+        v1 = jnp.concatenate([vx, summed(vb[..., :128], px)], axis=-1)
         grad1 = reduce_slow(v1)
-    own, flat = both[:16], both[16:].reshape(-1)
-    bcs = flat[: 5 * 2 * state].reshape(5, 2 * state)
-    ngain = flat[5 * 2 * state : 5 * 2 * state + dim]
-    skip_grad = own[6].reshape(heads, cols // heads).sum(axis=1)
-
-    mine_bc = grad1[:, cols : cols + bq]
     if fast:
-        got = mine_bc.reshape(tcount, shard // tcount, bq)
+        last = call(
+            k11_body,
+            (1,),
+            [full((shard, 512))] * 2 + [full((24, cols))] * 2,
+            [full(shape) for shape in FINAL_SHAPES(dim, cols, heads, state, shard, tcount)],
+            [
+                sds(shape, F32)
+                for shape in FINAL_SHAPES(dim, cols, heads, state, shard, tcount)
+            ],
+            [vmem((shard, 512), F32), vmem((24, cols), F32)],
+            (int(1e6), int(1e6)),
+            "last_sums",
+        )(sc, v1a, v1r, both, got)
+        (
+            ngain, grad_w_x, grad_w_bc, grad_w_dt, grad_conv_x, grad_bias_x, grad_conv_bc,
+            grad_bias_bc, grad_dt_bias, grad_a_log, grad_skip, grad_out_gain,
+        ) = last
+        grad_w_dt = grad_w_dt.T
     else:
-        parts = mine_bc.reshape(tcount, shard // tcount, bq)
+        own, flat = both[:16], both[16:]
+        ngain = flat[5:7].reshape(dim)
+        grad_w_x = grad1[:, :cols]
+        parts = grad1[:, cols : cols + bq].reshape(tcount, shard // tcount, bq)
         got = lax.all_to_all(parts, "tensor", split_axis=0, concat_axis=0, tiled=True)
-    grad_w_bc = jnp.swapaxes(got, 0, 1).reshape(shard // tcount, bq * tcount)
+        grad_w_bc = jnp.swapaxes(got, 0, 1).reshape(shard // tcount, bq * tcount)
+        grad_w_dt = grad1[:, cols + bq : cols + bq + heads]
+        grad_conv_x, grad_bias_x, grad_out_gain = own[:4], own[4], own[5]
+        grad_conv_bc, grad_bias_bc = flat[:4, : 2 * state], flat[4, : 2 * state]
+        grad_dt_bias, grad_a_log = own[7, :heads], own[8, :heads]
+        grad_skip = own[6].reshape(heads, cols // heads).sum(axis=1)
 
     return (
         out.reshape(tokens.shape),
         ig.reshape(tokens.shape),
         ngain,
         grad_w_z,
-        grad1[:, :cols],
+        grad_w_x,
         grad_w_bc,
-        grad1[:, cols + bq : cols + bq + heads],
-        own[:4],
-        own[4],
-        bcs[:4],
-        bcs[4],
-        own[7, :heads],
-        own[8, :heads],
-        skip_grad,
-        own[5],
+        grad_w_dt,
+        grad_conv_x,
+        grad_bias_x,
+        grad_conv_bc,
+        grad_bias_bc,
+        grad_dt_bias,
+        grad_a_log,
+        grad_skip,
+        grad_out_gain,
         grad_w_out,
     )
 

time: 327 us -> 318 us (0.972)
  local copies, waits for them, and re-layouts: 36.6 us -> 14 us
  waiting for transfers between devices: 33.3 us -> 39.8 us
  Pallas kernels: 176 us -> 182 us
    unnamed x192 -> x189, local copies, waits for them, and re-layouts: 18.9 us -> 10.9 us
    ppermute x39, waiting for transfers between devices: 31.3 us -> 38.2 us  [flip(): return lax.ppermute(value, axis, [(a, a ^ bit) for a in range(count)])]
    slice x16 -> x2, local copies, waits for them, and re-layouts: 6.01 us -> 0.04 us  [the longest x1 0.04 us: per_device(): px = flip(vb[..., 128:], 'tensor', 2)]
    pallas_call x1, Pallas kernels: 10.5 us -> 14.7 us  [per_device(): call(k6_body, (2,), [full((erows, dim)), full((rows, dim))] + [pl.BlockSp...]
    convert_element_type x13, other arithmetic: 6.46 us -> 2.63 us  [summed(): return (a.astype(F32) + b.astype(F32)).astype(BF)]
    pallas_call x0 -> x2, Pallas kernels: none -> 3.66 us  [the longest x1 2.25 us: per_device(): call(k0_body, (1,), [full(v.shape) for v in (conv_x, bias_x, out_gain, dt...]
  transfers between devices with their start and end apart: 47 -> 47, of which waited for: 15 -> 15; matrix products, arithmetic and copies ran while one was open for 8% -> 5% of each run, Pallas kernels for 42% -> 45%
where the time goes in v3:
time: 318 us; the launch traced here: 315 us
  Pallas kernels  182 us (57%)
  starting transfers between devices  63.1 us (20%)
  waiting for transfers between devices  39.8 us (13%)
  local copies, waits for them, and re-layouts  14 us (4%)
  other arithmetic  13.4 us (4%)
    ppermute x39, starting transfers between devices, flip(): return lax.ppermute(value, axis, [(a, a ^ bit) for a in range(count)])  41.3 us
    pallas_call x2, Pallas kernels, states_backward(): call(functools.partial(k8_body, g, last), (slots,), in_specs, [full(shape...  40.4 us
    pallas_call x1, Pallas kernels, per_device(): call(k5_body, (2, 2, slots), [pl.BlockSpec(group, p_gs(0)), pl.BlockSpec(...  38.5 us
    ppermute x39, waiting for transfers between devices, flip(): return lax.ppermute(value, axis, [(a, a ^ bit) for a in range(count)])  38.2 us
    pallas_call x2, Pallas kernels, within_backward(): call(functools.partial(k7_body, g), (slots,), [pl.BlockSpec(group, gsel(g...  17.8 us
    pallas_call x2, Pallas kernels, conv_and_states(): call(functools.partial(k2_body, g), (slots,), [pl.BlockSpec(group, gsel(g...  15.2 us
    pallas_call x1, Pallas kernels, per_device(): call(k6_body, (2,), [full((erows, dim)), full((rows, dim))] + [pl.BlockSp...  14.7 us
    pallas_call x1, Pallas kernels, per_device(): call(k1_body, (2,), [full((rows, dim)), full((64, dim)), full((1, dim))]...  13.8 us
  transfers between devices with their start and end apart: 47, of which 15 were waited for; matrix products, arithmetic and copies ran while one was open for 5% of the time, Pallas kernels for 45%

profile of v3, /device:TPU:0, one launch (start us, length us, event | category | flops | bytes accessed | tf_op | source)
XLA Modules:
  0.0 315.2 jit_solution(5490122618732066040)
XLA Ops:
  1.6 1.0 fusion.24
  2.6 4.1 %collective-permute-start = (bf16[1,96,512]{2,1,0:T(8,128)(2,1)S(1)}, bf16[1,96,512]{2,1,0:T(8,128)(2,1)S(1)}, u32[]{:S(2)}, u32[]{:S(2)}) collective-permute-start(bf16[1,96,512]{2,1,0:T(8,128)(2,1)S(1)} %get-tuple-element.335), channel_id=1, source_target_pairs={{0,16},{4,20},{8,24},{12,28},{16,0},{20,4},{24,8},{28,12},{1,17},{... | collective-permute-start | bytes 294920 | tf_op jit(solution)/shard_map/ppermute | solution.py:1004
  9.2 2.2 parameters.1
  12.4 1.6 collective-permute-start.1
  14.1 1.3 collective-permute-start.3
  15.3 2.2 collective-permute-start.2
  17.5 2.0 collective-permute-done.2
  19.7 1.6 collective-permute-start.5
  21.3 2.3 collective-permute-start.4
  23.5 1.8 collective-permute-start.7
  25.3 1.2 collective-permute-done.6
  26.5 6.2 %collective-permute-done.7 = bf16[1,2,96,384]{3,2,1,0:T(8,128)(2,1)S(1)} collective-permute-done((bf16[1,2,96,384]{3,2,1,0:T(8,128)(2,1)S(1)}, bf16[1,2,96,384]{3,2,1,0:T(8,128)(2,1)S(1)}, u32[]{:S(2)}, u32[]{:S(2)}) %collective-permute-start.7) | collective-permute-done | bytes 147488 | tf_op jit(solution)/shard_map/ppermute | solution.py:1004
  34.3 8.3 %collective-permute-done.10 = bf16[2,2,96,384]{3,2,1,0:T(8,128)(2,1)S(1)} collective-permute-done((bf16[2,2,96,384]{3,2,1,0:T(8,128)(2,1)S(1)}, bf16[2,2,96,384]{3,2,1,0:T(8,128)(2,1)S(1)}, u32[]{:S(2)}, u32[]{:S(2)}) %collective-permute-start.10) | collective-permute-done | bytes 294944 | tf_op jit(solution)/shard_map/ppermute | solution.py:1004
  42.7 1.3 collective-permute-done.8
  45.4 1.6 collective-permute-start.14
  48.1 13.8 %projections.1 = (bf16[1088,768]{1,0:T(8,128)(2,1)}, bf16[2,1088,768]{2,1,0:T(8,128)(2,1)}, bf16[1024,128]{1,0:T(8,128)(2,1)}, bf16[1024,128]{1,0:T(8,128)(2,1)}...) custom-call(s32[16]{0:T(128)S(1)} %copy-done.67, ...), custom_call_target="tpu_custom_call" | custom-call | flops 7000000000 | bytes 20000000 | tf_op jit(solution)/shard_map/projections/pallas_call | solution.py:1127
  62.1 1.6 collective-permute-start.15
  64.5 1.9 copy-done.2
  66.5 7.6 %conv_and_states_0.1 = (bf16[2,1024,768]{2,1,0:T(8,128)(2,1)}, bf16[2,1024,768]{2,1,0:T(8,128)(2,1)}, bf16[2,1024,768]{2,1,0:T(8,128)(2,1)}, bf16[528,1536]{1,0:T(8,128)(2,1)}) custom-call(s32[16]{0:T(128)S(1)} %copy-done.67, bf16[2,1088,768]{2,1,0:T(8,128)(2,1)S(1)} %copy-done.2, bf16[2,1088,768]{2,1,0:T(8,128)(2,1)S(1)} %copy-done.2, ...), custom_call_target="tpu_custom_call" | custom-call | flops 1 | bytes 1 | tf_op jit(solution)/shard_map/conv_and_states_0/pallas_call | solution.py:1185
  74.0 7.6 %conv_and_states_1.1 = (bf16[2,1024,768]{2,1,0:T(8,128)(2,1)}, bf16[2,1024,768]{2,1,0:T(8,128)(2,1)}, bf16[2,1024,768]{2,1,0:T(8,128)(2,1)}, bf16[528,1536]{1,0:T(8,128)(2,1)}) custom-call(s32[16]{0:T(128)S(1)} %copy-done.67, bf16[2,1088,768]{2,1,0:T(8,128)(2,1)S(1)} %copy-done.2, ...), custom_call_target="tpu_custom_call", output_to_operand_aliasing={{0}: (9, {}), {1}: (10, {}), {2}: (11, {}), {3}: (12, {})} | custom-call | flops 5000000000 | bytes 20000000 | tf_op jit(solution)/shard_map/conv_and_states_1/pallas_call | solution.py:1185
  81.7 1.6 collective-permute-start.17
  84.3 1.5 copy-done.83
  87.7 1.0 collective-permute-start.20
  88.8 5.8 %within_0.1.rest_0_ = f32[2,1024,768]{2,1,0:T(8,128)} custom-call(s32[16]{0:T(128)S(1)} %copy-done.67, bf16[2,1024,768]{2,1,0:T(8,128)(2,1)S(1)} %copy-done.5, bf16[1024,128]{1,0:T(8,128)(2,1)S(1)} %copy-done.33, bf16[1024,128]{1,0:T(8,128)(2,1)S(1)} %copy-done.50, f32[256,128]{1,0:T(8,128)S(1)} %copy-done.55, f32[256,128]{1,0:T(8,128)S(1)} %copy-done.57, ...), custom_call_target="tpu_custom_call" | custom-call | flops 5000000000 | bytes 10000000 | tf_op jit(solution)/shard_map/within_0/pallas_call | solution.py:1244
  94.5 5.9 %within_1.1.within = f32[2,1024,768]{2,1,0:T(8,128)} custom-call(s32[16]{0:T(128)S(1)} %copy-done.67, bf16[2,1024,768]{2,1,0:T(8,128)(2,1)S(1)} %copy-done.5, bf16[1024,128]{1,0:T(8,128)(2,1)S(1)} %copy-done.33, bf16[1024,128]{1,0:T(8,128)(2,1)S(1)} %copy-done.50, f32[256,128]{1,0:T(8,128)S(1)} %copy-done.55, ...), custom_call_target="tpu_custom_call", output_to_operand_aliasing={{}: (7, {})} | custom-call | flops 5000000000 | bytes 10000000 | tf_op jit(solution)/shard_map/within_1/pallas_call | solution.py:1244
  100.5 8.5 %gate_and_out_backward.1 = (bf16[2,1024,768]{2,1,0:T(8,128)(2,1)}, bf16[2,1024,768]{2,1,0:T(8,128)(2,1)}, bf16[1024,768]{1,0:T(8,128)(2,1)}) custom-call(s32[16]{0:T(128)S(1)} %copy-done.67, bf16[1088,768]{1,0:T(8,128)(2,1)S(1)} %copy-done.80, bf16[1024,768]{1,0:T(8,128)(2,1)S(1)} %bitcast.198, bf16[2,8,96,384]{3,2,1,0:T(8,128)(2,1)S(1)} %bitcast.186, ...), custom_call_target="tpu_custom_call" | custom-call | flops 5000000000 | bytes 20000000 | tf_op jit(solution)/shard_map/gate_and_out_backward/pallas_call | solution.py:1274
  109.1 1.1 copy-done.92
  111.0 1.2 copy-done.93
  112.1 38.5 %gated_norm.1 = (bf16[1024,768]{1,0:T(8,128)(2,1)}, bf16[2,1024,768]{2,1,0:T(8,128)(2,1)}, bf16[2,1024,768]{2,1,0:T(8,128)(2,1)}, bf16[2,1024,768]{2,1,0:T(8,128...) custom-call(s32[16]{0:T(128)} %pad_add_fusion.1.sc, ...), custom_call_target="tpu_custom_call" | custom-call | flops 15000000512 | bytes 40000000 | tf_op jit(solution)/shard_map/gated_norm/pallas_call | solution.py:1310
  150.6 1.3 collective-permute-start.22
  151.9 14.7 %outer_weight_grads.1 = (bf16[2,8,96,384]{3,2,1,0:T(8,128)(2,1)}, bf16[2,8,96,384]{3,2,1,0:T(8,128)(2,1)}, bf16[2,8,96,384]{3,2,1,0:T(8,128)(2,1)}, bf16[2,8,96,...) custom-call(s32[16]{0:T(128)} %pad_add_fusion.1.sc, bf16[1088,768]{1,0:T(8,128)(2,1)} %get-tuple-element.209.nrm, ...), custom_call_target="tpu_custom_call" | custom-call | flops 5000000000 | bytes 20000000 | tf_op jit(solution)/shard_map/outer_weight_grads/pallas_call | solution.py:1374
  166.7 2.9 collective-permute-start.24
  170.6 2.1 fusion.1
  172.8 13.4 %collective-permute-start.25 = (bf16[512,1536]{1,0:T(8,128)(2,1)S(1)}, bf16[512,1536]{1,0:T(8,128)(2,1)S(1)}, u32[]{:S(2)}, u32[]{:S(2)}) collective-permute-start(bf16[512,1536]{1,0:T(8,128)(2,1)S(1)} %fusion.1), channel_id=1, source_target_pairs={{2,1},{6,5},{10,9},{14,13},{18,17},{22,21},{26,25},{30,29}} | collective-permute-start | bytes 4718600 | tf_op jit(solution)/shard_map/ppermute | solution.py:1390
  186.2 8.8 %within_backward_1.1 = (f32[2,1024,768]{2,1,0:T(8,128)}, f32[2,1024,128]{2,1,0:T(8,128)}, f32[256,128]{1,0:T(8,128)}) custom-call(s32[16]{0:T(128)S(1)} %copy-done.68, bf16[2,1024,768]{2,1,0:T(8,128)(2,1)S(1)} %copy-done.5, bf16[2,1024,768]{2,1,0:T(8,128)(2,1)S(1)} %copy-done.3, bf16[1024,128]{1,0:T(8,128)(2,1)S(1)} %copy-done.33, ...), custom_call_target="tpu_custom_call" | custom-call | flops 10000000000 | bytes 20000000 | tf_op jit(solution)/shard_map/within_backward_1/pallas_call | solution.py:1428
  195.0 1.0 copy-done.86
  197.0 9.0 %within_backward_0.1 = (f32[2,1024,768]{2,1,0:T(8,128)}, f32[2,1024,128]{2,1,0:T(8,128)}, f32[256,128]{1,0:T(8,128)}) custom-call(s32[16]{0:T(128)S(1)} %copy-done.68, bf16[2,1024,768]{2,1,0:T(8,128)(2,1)S(1)} %copy-done.5, bf16[2,1024,768]{2,1,0:T(8,128)(2,1)S(1)} %copy-done.3, bf16[1024,128]{1,0:T(8,128)(2,1)S(1)} %copy-done.34, ...), custom_call_target="tpu_custom_call", output_to_operand_aliasing={{0}: (8, {})} | custom-call | flops 1 | bytes 1 | tf_op jit(solution)/shard_map/within_backward_0/pallas_call | solution.py:1428
  206.0 3.7 %normed_grad_z1.1.dna = f32[1024,768]{1,0:T(8,128)} custom-call(s32[16]{0:T(128)S(1)} %copy-done.68, bf16[2,1024,768]{2,1,0:T(8,128)(2,1)S(1)} %copy-done.4, bf16[2,8,96,384]{3,2,1,0:T(8,128)(2,1)S(1)} %bitcast.188, bf16[2,8,96,384]{3,2,1,0:T(8,128)(2,1)S(1)} %copy-done.10), custom_call_target="tpu_custom_call" | custom-call | flops 1 | bytes 1 | tf_op jit(solution)/shard_map/normed_grad_z1/pallas_call | solution.py:1551
  209.8 2.9 collective-permute-done.26
  212.7 1.3 collective-permute-start.27
  214.3 3.3 %collective-permute-start.28 = (bf16[4,96,384]{2,1,0:T(8,128)(2,1)S(1)}, bf16[4,96,384]{2,1,0:T(8,128)(2,1)S(1)}, u32[]{:S(2)}, u32[]{:S(2)}) collective-permute-start(bf16[4,96,384]{2,1,0:T(8,128)(2,1)S(1)} %slice_bitcast_fusion.9), channel_id=1, source_target_pairs={{0,2},{1,3},{2,0},{3,1},{4,6},{5,7},{6,4},{7,5},{8,10},{9,11},{10,... | collective-permute-start | bytes 884744 | tf_op jit(solution)/shard_map/ppermute | solution.py:1004
  218.7 15.5 %states_backward_1.1 = (bf16[8,96,384]{2,1,0:T(8,128)(2,1)}, bf16[8,96,384]{2,1,0:T(8,128)(2,1)}, bf16[1088,768]{1,0:T(8,128)(2,1)}, f32[256,128]{1,0:T(8,128)},...) custom-call(s32[16]{0:T(128)S(1)} %copy-done.68, ...), custom_call_target="tpu_custom_call" | custom-call | flops 10000000000 | bytes 20000000 | tf_op jit(solution)/shard_map/states_backward_1/pallas_call | solution.py:1539
  234.5 1.8 collective-permute-start.32
  236.5 3.7 %normed_grad_z0.1.dnb = f32[1024,768]{1,0:T(8,128)} custom-call(s32[16]{0:T(128)S(1)} %copy-done.68, bf16[2,1024,768]{2,1,0:T(8,128)(2,1)S(1)} %copy-done.4, bf16[2,8,96,384]{3,2,1,0:T(8,128)(2,1)S(1)} %bitcast.189, bf16[2,8,96,384]{3,2,1,0:T(8,128)(2,1)S(1)} %copy-done.10), custom_call_target="tpu_custom_call" | custom-call | flops 1 | bytes 1 | tf_op jit(solution)/shard_map/normed_grad_z0/pallas_call | solution.py:1551
  241.7 24.9 %states_backward_0.1 = (bf16[8,96,640]{2,1,0:T(8,128)(2,1)}, bf16[8,96,640]{2,1,0:T(8,128)(2,1)}, bf16[1088,768]{1,0:T(8,128)(2,1)}, f32[256,128]{1,0:T(8,128)},...) custom-call(s32[16]{0:T(128)S(1)} %copy-done.68, ...), custom_call_target="tpu_custom_call" | custom-call | flops 10000000000 | bytes 20000000 | tf_op jit(solution)/shard_map/states_backward_0/pallas_call | solution.py:1539
  267.5 2.0 collective-permute-done.34
  270.3 1.1 add_convert_fusion.4
  271.4 1.5 add_convert_fusion.2
  272.9 1.1 collective-permute-start.37
  274.1 1.0 collective-permute-start.35
  275.9 1.4 copy-done.75
  277.4 7.3 %normed_grad.1.dn = f32[1088,768]{1,0:T(8,128)} custom-call(s32[16]{0:T(128)S(1)} %copy-done.68, bf16[1088,768]{1,0:T(8,128)(2,1)S(1)} %copy-done.75, bf16[1088,768]{1,0:T(8,128)(2,1)S(1)} %copy-done.79, bf16[1088,512]{1,0:T(8,128)(2,1)S(1)} %copy-done.77, f32[1024,768]{1,0:T(8,128)S(1)} %copy-done.12, f32[1024,768]{1,0:T(8,128)S(1)} %copy-done.13, ...), custom_call_target="tpu_custom_call" | custom-call | flops 6000000000 | bytes 20000000 | tf_op jit(solution)/shard_map/normed_grad/pallas_call | solution.py:1634
  284.9 1.4 collective-permute-start.41
  286.3 1.1 slice.303
  287.4 1.3 collective-permute-start.39
  289.5 1.1 collective-permute-done.39.hr
  290.6 3.7 %collective-permute-done.40 = bf16[4,96,128]{2,1,0:T(8,128)(2,1)S(1)} collective-permute-done((bf16[4,96,128]{2,1,0:T(8,128)(2,1)S(1)}, bf16[4,96,128]{2,1,0:T(8,128)(2,1)S(1)}, u32[]{:S(2)}, u32[]{:S(2)}) %collective-permute-start.40) | collective-permute-done | bytes 98336 | tf_op jit(solution)/shard_map/ppermute | solution.py:1004
  295.3 1.3 collective-permute-start.43
  296.7 3.3 %input_grad.1 = bf16[1024,768]{1,0:T(8,128)(2,1)} custom-call(s32[16]{0:T(128)S(1)} %copy-done.68, f32[1088,768]{1,0:T(8,128)S(1)} %copy-done.11, bf16[64,768]{1,0:T(8,128)(2,1)S(1)} %collective-permute-done.39.hr, bf16[1024,768]{1,0:T(8,128)(2,1)S(1)} %bitcast.197, bf16[1024,768]{1,0:T(8,128)(2,1)S(1)} %bitcast.199, f32[1,768]{1,0:T(1,128)S(1)} %copy-done.72), custom_call_target="tpu_custom_call" | custom-call | flops 1000000000 | bytes 10000000 | tf_op jit(solution)/shard_map/input_grad/pallas_call | solution.py:1671
  299.9 5.4 %collective-permute-done.43 = f32[24,384]{1,0:T(8,128)S(1)} collective-permute-done((f32[24,384]{1,0:T(8,128)S(1)}, f32[24,384]{1,0:T(8,128)S(1)}, u32[]{:S(2)}, u32[]{:S(2)}) %collective-permute-start.43) | collective-permute-done | bytes 36896 | tf_op jit(solution)/shard_map/ppermute | solution.py:1004
  306.3 2.1 collective-permute-start.45
  309.2 2.8 collective-permute-done.46.got
  311.9 1.5 collective-permute-done.45.vr
  313.5 1.4 last_sums.1
  (309 shorter events, 24.1 us)
Async XLA Ops:
  2.6 9.8 %collective-permute-start = (bf16[1,96,512]{2,1,0:T(8,128)(2,1)S(1)}, bf16[1,96,512]{2,1,0:T(8,128)(2,1)S(1)}, u32[]{:S(2)}, u32[]{:S(2)}) collective-permute-start(bf16[1,96,512]{2,1,0:T(8,128)(2,1)S(1)} %get-tuple-element.335), channel_id=1, source_target_pairs={{0,16},{4,20},{8,24},{12,28},{16,0},{20,4},{24,8},{28,12},{1,17},{... | collective-permute-start | bytes 294920 | tf_op jit(solution)/shard_map/ppermute | solution.py:1004
  12.4 7.1 %collective-permute-start.1 = (bf16[2,96,512]{2,1,0:T(8,128)(2,1)S(1)}, bf16[2,96,512]{2,1,0:T(8,128)(2,1)S(1)}, u32[]{:S(2)}, u32[]{:S(2)}) collective-permute-start(bf16[2,96,512]{2,1,0:T(8,128)(2,1)S(1)} %get-tuple-element.331), channel_id=1, source_target_pairs={{0,8},{4,12},{8,0},{12,4},{16,24},{20,28},{24,16},{28,20},{1,9},{5... | collective-permute-start | bytes 589832 | tf_op jit(solution)/shard_map/ppermute | solution.py:1004
  14.1 5.5 %collective-permute-start.3 = (bf16[64,768]{1,0:T(8,128)(2,1)S(1)}, bf16[64,768]{1,0:T(8,128)(2,1)S(1)}, u32[]{:S(2)}, u32[]{:S(2)}) collective-permute-start(bf16[64,768]{1,0:T(8,128)(2,1)S(1)} %bitcast.232), channel_id=1, source_target_pairs={{0,1},{1,2},{2,3},{4,5},{5,6},{6,7},{8,9},{9,10},{10,11},{12,13},{... | collective-permute-start | bytes 294920 | tf_op jit(solution)/shard_map/ppermute | solution.py:1089
  15.3 4.2 %collective-permute-start.2 = (f32[16,384]{1,0:T(8,128)}, f32[16,384]{1,0:T(8,128)S(1)}, u32[]{:S(2)}, u32[]{:S(2)}) collective-permute-start(f32[16,384]{1,0:T(8,128)} %get-tuple-element.169), channel_id=1, source_target_pairs={{0,2},{1,3},{2,0},{3,1},{4,6},{5,7},{6,4},{7,5},{8,10},{9,11},{10,... | collective-permute-start | bytes 73736 | tf_op jit(solution)/shard_map/ppermute | solution.py:1004
  19.7 13.1 %collective-permute-start.5 = (bf16[4,96,256]{2,1,0:T(8,128)(2,1)S(1)}, bf16[4,96,256]{2,1,0:T(8,128)(2,1)S(1)}, u32[]{:S(2)}, u32[]{:S(2)}) collective-permute-start(bf16[4,96,256]{2,1,0:T(8,128)(2,1)S(1)} %get-tuple-element.324), channel_id=1, source_target_pairs={{0,4},{4,0},{8,12},{12,8},{16,20},{20,16},{24,28},{28,24},{1,5},{5... | collective-permute-start | bytes 589832 | tf_op jit(solution)/shard_map/ppermute | solution.py:1004
  21.3 11.5 %collective-permute-start.4 = (bf16[4,96,256]{2,1,0:T(8,128)(2,1)S(1)}, bf16[4,96,256]{2,1,0:T(8,128)(2,1)S(1)}, u32[]{:S(2)}, u32[]{:S(2)}) collective-permute-start(bf16[4,96,256]{2,1,0:T(8,128)(2,1)S(1)} %get-tuple-element.325), channel_id=1, source_target_pairs={{0,2},{1,3},{2,0},{3,1},{4,6},{5,7},{6,4},{7,5},{8,10},{9,11},{10,... | collective-permute-start | bytes 589832 | tf_op jit(solution)/shard_map/ppermute | solution.py:1004
  23.5 9.3 %collective-permute-start.7 = (bf16[1,2,96,384]{3,2,1,0:T(8,128)(2,1)S(1)}, bf16[1,2,96,384]{3,2,1,0:T(8,128)(2,1)S(1)}, u32[]{:S(2)}, u32[]{:S(2)}) collective-permute-start(bf16[1,2,96,384]{3,2,1,0:T(8,128)(2,1)S(1)} %maximum_bitcast_fusion), channel_id=1, source_target_pairs={{0,16},{4,20},{8,24},{12,28},{16,0},{20,4},{24,8},{28,12},{1,17},{... | collective-permute-start | bytes 442376 | tf_op jit(solution)/shard_map/ppermute | solution.py:1004
  25.3 1.2 collective-permute-start.6
  32.8 11.1 %collective-permute-start.8 = (bf16[2,4,96,256]{3,2,1,0:T(8,128)(2,1)S(1)}, bf16[2,4,96,256]{3,2,1,0:T(8,128)(2,1)S(1)}, u32[]{:S(2)}, u32[]{:S(2)}) collective-permute-start(bf16[2,4,96,256]{3,2,1,0:T(8,128)(2,1)S(1)} %get-tuple-element.321), channel_id=1, source_target_pairs={{0,4},{4,0},{8,12},{12,8},{16,20},{20,16},{24,28},{28,24},{1,5},{5... | collective-permute-start | bytes 1179656 | tf_op jit(solution)/shard_map/ppermute | solution.py:1004
  33.5 10.8 %collective-permute-start.9 = (bf16[4,2,96,256]{3,2,0,1:T(8,128)(2,1)S(1)}, bf16[4,2,96,256]{3,2,0,1:T(8,128)(2,1)S(1)}, u32[]{:S(2)}, u32[]{:S(2)}) collective-permute-start(bf16[4,2,96,256]{3,2,0,1:T(8,128)(2,1)S(1)} %pad_maximum_fusion.9), channel_id=1, source_target_pairs={{0,2},{1,3},{2,0},{3,1},{4,6},{5,7},{6,4},{7,5},{8,10},{9,11},{10,... | collective-permute-start | bytes 1179656 | tf_op jit(solution)/shard_map/ppermute | solution.py:1004
  34.2 8.5 %collective-permute-start.10 = (bf16[2,2,96,384]{3,2,1,0:T(8,128)(2,1)S(1)}, bf16[2,2,96,384]{3,2,1,0:T(8,128)(2,1)S(1)}, u32[]{:S(2)}, u32[]{:S(2)}) collective-permute-start(bf16[2,2,96,384]{3,2,1,0:T(8,128)(2,1)S(1)} %get-tuple-element.327), channel_id=1, source_target_pairs={{0,8},{4,12},{8,0},{12,4},{16,24},{20,28},{24,16},{28,20},{1,9},{5... | collective-permute-start | bytes 884744 | tf_op jit(solution)/shard_map/ppermute | solution.py:1004
  34.3 39.7 %copy-start.35 = (f32[2,16,768]{2,1,0:T(8,128)}, f32[2,16,768]{2,1,0:T(8,128)S(1)}, u32[]{:S(2)}) copy-start(f32[2,16,768]{2,1,0:T(8,128)S(1)} %pad_maximum_fusion.14.par) | copy-start | bytes 294916
  44.5 17.4 %copy-start.16 = (bf16[2,8,96,256]{3,2,1,0:T(8,128)(2,1)}, bf16[2,8,96,256]{3,2,1,0:T(8,128)(2,1)S(1)}, u32[]{:S(2)}) copy-start(bf16[2,8,96,256]{3,2,1,0:T(8,128)(2,1)S(1)} %pad_maximum_fusion.3.bm) | copy-start | bytes 2359300
  44.6 3.0 collective-permute-start.12
  44.7 3.4 %collective-permute-start.11 = (bf16[2,8,96,256]{3,2,1,0:T(8,128)(2,1)S(1)}, bf16[2,8,96,256]{3,2,1,0:T(8,128)(2,1)S(1)}, u32[]{:S(2)}, u32[]{:S(2)}) collective-permute-start(bf16[2,8,96,256]{3,2,1,0:T(8,128)(2,1)S(1)} %bitcast.190), channel_id=1, source_target_pairs={{0,1},{1,0},{2,3},{3,2},{4,5},{5,4},{6,7},{7,6},{8,9},{9,8},{10,11... | collective-permute-start | bytes 2359304 | tf_op jit(solution)/shard_map/ppermute | solution.py:1004
  45.4 16.6 %collective-permute-start.14 = (bf16[4,96,384]{2,1,0:T(8,128)(2,1)S(1)}, bf16[4,96,384]{2,1,0:T(8,128)(2,1)S(1)}, u32[]{:S(2)}, u32[]{:S(2)}) collective-permute-start(bf16[4,96,384]{2,1,0:T(8,128)(2,1)S(1)} %get-tuple-element.317), channel_id=1, source_target_pairs={{0,4},{4,0},{8,12},{12,8},{16,20},{20,16},{24,28},{28,24},{1,5},{5... | collective-permute-start | bytes 884744 | tf_op jit(solution)/shard_map/ppermute | solution.py:1004
  47.0 15.0 %collective-permute-start.13 = (bf16[4,96,384]{2,1,0:T(8,128)(2,1)S(1)}, bf16[4,96,384]{2,1,0:T(8,128)(2,1)S(1)}, u32[]{:S(2)}, u32[]{:S(2)}) collective-permute-start(bf16[4,96,384]{2,1,0:T(8,128)(2,1)S(1)} %get-tuple-element.319), channel_id=1, source_target_pairs={{0,2},{1,3},{2,0},{3,1},{4,6},{5,7},{6,4},{7,5},{8,10},{9,11},{10,... | collective-permute-start | bytes 884744 | tf_op jit(solution)/shard_map/ppermute | solution.py:1004
  62.1 19.5 %collective-permute-start.15 = (bf16[2,4,96,384]{3,2,1,0:T(8,128)(2,1)S(1)}, bf16[2,4,96,384]{3,2,1,0:T(8,128)(2,1)S(1)}, u32[]{:S(2)}, u32[]{:S(2)}) collective-permute-start(bf16[2,4,96,384]{3,2,1,0:T(8,128)(2,1)S(1)} %get-tuple-element.315), channel_id=1, source_target_pairs={{0,4},{4,0},{8,12},{12,8},{16,20},{20,16},{24,28},{28,24},{1,5},{5... | collective-permute-start | bytes 1769480 | tf_op jit(solution)/shard_map/ppermute | solution.py:1004
  63.8 17.9 %collective-permute-start.16 = (bf16[4,2,96,384]{3,2,1,0:T(8,128)(2,1)S(1)}, bf16[4,2,96,384]{3,2,1,0:T(8,128)(2,1)S(1)}, u32[]{:S(2)}, u32[]{:S(2)}) collective-permute-start(bf16[4,2,96,384]{3,2,1,0:T(8,128)(2,1)S(1)} %pad_maximum_fusion.6), channel_id=1, source_target_pairs={{0,2},{1,3},{2,0},{3,1},{4,6},{5,7},{6,4},{7,5},{8,10},{9,11},{10,... | collective-permute-start | bytes 1769480 | tf_op jit(solution)/shard_map/ppermute | solution.py:1004
  81.7 4.8 %collective-permute-start.17 = (bf16[528,1536]{1,0:T(8,128)(2,1)}, bf16[528,1536]{1,0:T(8,128)(2,1)S(1)}, u32[]{:S(2)}, u32[]{:S(2)}) collective-permute-start(bf16[528,1536]{1,0:T(8,128)(2,1)} %get-tuple-element.201), channel_id=1, source_target_pairs={{0,1},{2,3},{4,5},{6,7},{8,9},{10,11},{12,13},{14,15},{16,17},{18,... | collective-permute-start | bytes 4866056 | tf_op jit(solution)/shard_map/ppermute | solution.py:1238
  83.6 16.9 %copy-start.6 = (bf16[2,4,2,96,384]{4,3,2,1,0:T(8,128)(2,1)}, bf16[2,4,2,96,384]{4,3,2,1,0:T(8,128)(2,1)S(1)}, u32[]{:S(2)}) copy-start(bf16[2,4,2,96,384]{4,3,2,1,0:T(8,128)(2,1)S(1)} %copy.59) | copy-start | bytes 3538948
  83.7 16.7 %copy-start.28 = (bf16[2,8,96,384]{3,2,1,0:T(8,128)(2,1)}, bf16[2,8,96,384]{3,2,1,0:T(8,128)(2,1)S(1)}, u32[]{:S(2)}) copy-start(bf16[2,8,96,384]{3,2,1,0:T(8,128)(2,1)S(1)} %pad_maximum_fusion.1.wom) | copy-start | bytes 3538948
  83.7 16.7 %collective-permute-start.19 = (bf16[2,8,96,384]{3,2,1,0:T(8,128)(2,1)S(1)}, bf16[2,8,96,384]{3,2,1,0:T(8,128)(2,1)S(1)}, u32[]{:S(2)}, u32[]{:S(2)}) collective-permute-start(bf16[2,8,96,384]{3,2,1,0:T(8,128)(2,1)S(1)} %pad_maximum_fusion.1.wom), channel_id=1, source_target_pairs={{0,1},{1,0},{2,3},{3,2},{4,5},{5,4},{6,7},{7,6},{8,9},{9,8},{10,11... | collective-permute-start | bytes 3538952 | tf_op jit(solution)/shard_map/ppermute | solution.py:1004
  83.8 16.6 %collective-permute-start.18 = (bf16[2,8,96,384]{3,2,1,0:T(8,128)(2,1)S(1)}, bf16[2,8,96,384]{3,2,1,0:T(8,128)(2,1)S(1)}, u32[]{:S(2)}, u32[]{:S(2)}) collective-permute-start(bf16[2,8,96,384]{3,2,1,0:T(8,128)(2,1)S(1)} %bitcast.185), channel_id=1, source_target_pairs={{0,1},{1,0},{2,3},{3,2},{4,5},{5,4},{6,7},{7,6},{8,9},{9,8},{10,11... | collective-permute-start | bytes 3538952 | tf_op jit(solution)/shard_map/ppermute | solution.py:1004
  87.7 21.4 %collective-permute-start.20 = (bf16[512,1536]{1,0:T(8,128)(2,1)S(1)}, bf16[512,1536]{1,0:T(8,128)(2,1)S(1)}, u32[]{:S(2)}, u32[]{:S(2)}) collective-permute-start(bf16[512,1536]{1,0:T(8,128)(2,1)S(1)} %fusion.3), channel_id=1, source_target_pairs={{1,2},{5,6},{9,10},{13,14},{17,18},{21,22},{25,26},{29,30}} | collective-permute-start | bytes 4718600 | tf_op jit(solution)/shard_map/ppermute | solution.py:1240
  110.2 0.8 collective-permute-start.21
  150.6 19.0 %collective-permute-start.22 = (bf16[528,1536]{1,0:T(8,128)(2,1)}, bf16[528,1536]{1,0:T(8,128)(2,1)S(1)}, u32[]{:S(2)}, u32[]{:S(2)}) collective-permute-start(bf16[528,1536]{1,0:T(8,128)(2,1)} %get-tuple-element.226), channel_id=1, source_target_pairs={{1,0},{3,2},{5,4},{7,6},{9,8},{11,10},{13,12},{15,14},{17,16},{19,... | collective-permute-start | bytes 4866056 | tf_op jit(solution)/shard_map/ppermute | solution.py:1371
  166.7 28.4 %collective-permute-start.24 = (bf16[2,8,96,384]{3,2,1,0:T(8,128)(2,1)}, bf16[2,8,96,384]{3,2,1,0:T(8,128)(2,1)S(1)}, u32[]{:S(2)}, u32[]{:S(2)}) collective-permute-start(bf16[2,8,96,384]{3,2,1,0:T(8,128)(2,1)} %get-tuple-element.228), channel_id=1, source_target_pairs={{0,1},{1,0},{2,3},{3,2},{4,5},{5,4},{6,7},{7,6},{8,9},{9,8},{10,11... | collective-permute-start | bytes 3538952 | tf_op jit(solution)/shard_map/ppermute | solution.py:1004
  169.6 49.0 %copy-start.8 = (bf16[528,1536]{1,0:T(8,128)(2,1)}, bf16[528,1536]{1,0:T(8,128)(2,1)S(1)}, u32[]{:S(2)}) copy-start(bf16[528,1536]{1,0:T(8,128)(2,1)S(1)} %collective-permute-done.22.q1) | copy-start | bytes 4866052
  169.6 25.4 %collective-permute-start.23 = (bf16[2,8,96,384]{3,2,1,0:T(8,128)(2,1)}, bf16[2,8,96,384]{3,2,1,0:T(8,128)(2,1)S(1)}, u32[]{:S(2)}, u32[]{:S(2)}) collective-permute-start(bf16[2,8,96,384]{3,2,1,0:T(8,128)(2,1)} %get-tuple-element.227), channel_id=1, source_target_pairs={{0,1},{1,0},{2,3},{3,2},{4,5},{5,4},{6,7},{7,6},{8,9},{9,8},{10,11... | collective-permute-start | bytes 3538952 | tf_op jit(solution)/shard_map/ppermute | solution.py:1004
  170.5 15.6 %copy-start.3 = (bf16[2,1024,768]{2,1,0:T(8,128)(2,1)S(1)}, bf16[2,1024,768]{2,1,0:T(8,128)(2,1)}, u32[]{:S(2)}) copy-start(bf16[2,1024,768]{2,1,0:T(8,128)(2,1)} %get-tuple-element.232.dy) | copy-start | bytes 9437188
  170.6 15.6 %copy-start.51 = (bf16[1024,128]{1,0:T(8,128)(2,1)S(1)}, bf16[1024,128]{1,0:T(8,128)(2,1)}, u32[]{:S(2)}) copy-start(bf16[1024,128]{1,0:T(8,128)(2,1)} %get-tuple-element.204.clow) | copy-start | bytes 786436
  170.6 15.6 %copy-start.56 = (f32[256,128]{1,0:T(8,128)S(1)}, f32[256,128]{1,0:T(8,128)}, u32[]{:S(2)}) copy-start(f32[256,128]{1,0:T(8,128)} %get-tuple-element.205.cump) | copy-start | bytes 393220
  170.6 15.6 %copy-start.58 = (f32[256,128]{1,0:T(8,128)S(1)}, f32[256,128]{1,0:T(8,128)}, u32[]{:S(2)}) copy-start(f32[256,128]{1,0:T(8,128)} %get-tuple-element.206.uvp) | copy-start | bytes 393220
  170.6 15.6 %copy-start.60 = (f32[128,256]{1,0:T(8,128)S(1)}, f32[128,256]{1,0:T(8,128)}, u32[]{:S(2)}) copy-start(f32[128,256]{1,0:T(8,128)} %get-tuple-element.207.ct) | copy-start | bytes 393220
  170.6 15.6 %copy-start.68 = (s32[16]{0:T(128)S(1)}, s32[16]{0:T(128)}, u32[]{:S(2)}) copy-start(s32[16]{0:T(128)} %pad_add_fusion.1.sc) | copy-start | bytes 196
  172.7 23.3 %copy-start.88 = (bf16[2,8,96,384]{3,2,1,0:T(8,128)(2,1)S(1)}, bf16[2,8,96,384]{3,2,1,0:T(8,128)(2,1)}, u32[]{:S(2)}) copy-start(bf16[2,8,96,384]{3,2,1,0:T(8,128)(2,1)} %get-tuple-element.238) | copy-start | bytes 3538948
  172.8 37.0 %collective-permute-start.25 = (bf16[512,1536]{1,0:T(8,128)(2,1)S(1)}, bf16[512,1536]{1,0:T(8,128)(2,1)S(1)}, u32[]{:S(2)}, u32[]{:S(2)}) collective-permute-start(bf16[512,1536]{1,0:T(8,128)(2,1)S(1)} %fusion.1), channel_id=1, source_target_pairs={{2,1},{6,5},{10,9},{14,13},{18,17},{22,21},{26,25},{30,29}} | collective-permute-start | bytes 4718600 | tf_op jit(solution)/shard_map/ppermute | solution.py:1390
  196.4 16.2 %collective-permute-start.26 = (bf16[2,4,96,384]{3,2,1,0:T(8,128)(2,1)S(1)}, bf16[2,4,96,384]{3,2,1,0:T(8,128)(2,1)S(1)}, u32[]{:S(2)}, u32[]{:S(2)}) collective-permute-start(bf16[2,4,96,384]{3,2,1,0:T(8,128)(2,1)S(1)} %slice_bitcast_fusion.3), channel_id=1, source_target_pairs={{0,4},{4,0},{8,12},{12,8},{16,20},{20,16},{24,28},{28,24},{1,5},{5... | collective-permute-start | bytes 1769480 | tf_op jit(solution)/shard_map/ppermute | solution.py:1004
  212.7 5.9 %collective-permute-start.27 = (bf16[512,1536]{1,0:T(8,128)(2,1)S(1)}, bf16[512,1536]{1,0:T(8,128)(2,1)S(1)}, u32[]{:S(2)}, u32[]{:S(2)}) collective-permute-start(bf16[512,1536]{1,0:T(8,128)(2,1)S(1)} %collective-permute-done.25.q2), channel_id=1, source_target_pairs={{1,0},{5,4},{9,8},{13,12},{17,16},{21,20},{25,24},{29,28}} | collective-permute-start | bytes 4718600 | tf_op jit(solution)/shard_map/ppermute | solution.py:1576
  214.3 20.0 %collective-permute-start.28 = (bf16[4,96,384]{2,1,0:T(8,128)(2,1)S(1)}, bf16[4,96,384]{2,1,0:T(8,128)(2,1)S(1)}, u32[]{:S(2)}, u32[]{:S(2)}) collective-permute-start(bf16[4,96,384]{2,1,0:T(8,128)(2,1)S(1)} %slice_bitcast_fusion.9), channel_id=1, source_target_pairs={{0,2},{1,3},{2,0},{3,1},{4,6},{5,7},{6,4},{7,5},{8,10},{9,11},{10,... | collective-permute-start | bytes 884744 | tf_op jit(solution)/shard_map/ppermute | solution.py:1004
  217.9 16.3 %collective-permute-start.29 = (bf16[2,4,96,384]{3,2,1,0:T(8,128)(2,1)S(1)}, bf16[2,4,96,384]{3,2,1,0:T(8,128)(2,1)S(1)}, u32[]{:S(2)}, u32[]{:S(2)}) collective-permute-start(bf16[2,4,96,384]{3,2,1,0:T(8,128)(2,1)S(1)} %slice_bitcast_fusion.1), channel_id=1, source_target_pairs={{0,4},{4,0},{8,12},{12,8},{16,20},{20,16},{24,28},{28,24},{1,5},{5... | collective-permute-start | bytes 1769480 | tf_op jit(solution)/shard_map/ppermute | solution.py:1004
  218.6 15.6 %copy-start.24 = (bf16[512,1536]{1,0:T(8,128)(2,1)}, bf16[512,1536]{1,0:T(8,128)(2,1)S(1)}, u32[]{:S(2)}) copy-start(bf16[512,1536]{1,0:T(8,128)(2,1)S(1)} %collective-permute-done.27.q3) | copy-start | bytes 4718596
  234.2 6.0 %collective-permute-start.30 = (bf16[8,96,384]{2,1,0:T(8,128)(2,1)}, bf16[8,96,384]{2,1,0:T(8,128)(2,1)S(1)}, u32[]{:S(2)}, u32[]{:S(2)}) collective-permute-start(bf16[8,96,384]{2,1,0:T(8,128)(2,1)} %get-tuple-element.249), channel_id=1, source_target_pairs={{0,1},{1,0},{2,3},{3,2},{4,5},{5,4},{6,7},{7,6},{8,9},{9,8},{10,11... | collective-permute-start | bytes 1769480 | tf_op jit(solution)/shard_map/ppermute | solution.py:1004
  234.5 32.1 %collective-permute-start.32 = (bf16[4,96,384]{2,1,0:T(8,128)(2,1)S(1)}, bf16[4,96,384]{2,1,0:T(8,128)(2,1)S(1)}, u32[]{:S(2)}, u32[]{:S(2)}) collective-permute-start(bf16[4,96,384]{2,1,0:T(8,128)(2,1)S(1)} %slice_bitcast_fusion.8), channel_id=1, source_target_pairs={{0,2},{1,3},{2,0},{3,1},{4,6},{5,7},{6,4},{7,5},{8,10},{9,11},{10,... | collective-permute-start | bytes 884744 | tf_op jit(solution)/shard_map/ppermute | solution.py:1004
  240.4 26.2 %collective-permute-start.31 = (bf16[8,96,384]{2,1,0:T(8,128)(2,1)S(1)}, bf16[8,96,384]{2,1,0:T(8,128)(2,1)S(1)}, u32[]{:S(2)}, u32[]{:S(2)}) collective-permute-start(bf16[8,96,384]{2,1,0:T(8,128)(2,1)S(1)} %add_convert_fusion.3), channel_id=1, source_target_pairs={{0,2},{1,3},{2,0},{3,1},{4,6},{5,7},{6,4},{7,5},{8,10},{9,11},{10,... | collective-permute-start | bytes 1769480 | tf_op jit(solution)/shard_map/ppermute | solution.py:1004
  241.6 25.3 %copy-start.82 = (bf16[2,4,96,384]{3,2,1,0:T(8,128)(2,1)S(1)}, bf16[2,4,96,384]{3,2,1,0:T(8,128)(2,1)}, u32[]{:S(2)}) copy-start(bf16[2,4,96,384]{3,2,1,0:T(8,128)(2,1)} %copy-done.81) | copy-start | bytes 1769476
  241.6 34.2 %copy-start.79 = (bf16[1088,768]{1,0:T(8,128)(2,1)S(1)}, bf16[1088,768]{1,0:T(8,128)(2,1)}, u32[]{:S(2)}) copy-start(bf16[1088,768]{1,0:T(8,128)(2,1)} %get-tuple-element.277.din1) | copy-start | bytes 5013508
  266.6 2.9 collective-permute-start.33
  267.0 2.6 collective-permute-start.34
  267.5 17.2 %collective-permute-start.38 = (bf16[2,2,96,384]{3,2,1,0:T(8,128)(2,1)S(1)}, bf16[2,2,96,384]{3,2,1,0:T(8,128)(2,1)S(1)}, u32[]{:S(2)}, u32[]{:S(2)}) collective-permute-start(bf16[2,2,96,384]{3,2,1,0:T(8,128)(2,1)S(1)} %fusion.13), channel_id=1, source_target_pairs={{0,8},{4,12},{8,0},{12,4},{16,24},{20,28},{24,16},{28,20},{1,9},{5... | collective-permute-start | bytes 884744 | tf_op jit(solution)/shard_map/ppermute | solution.py:1004
  272.9 11.8 %collective-permute-start.37 = (f32[24,384]{1,0:T(8,128)S(1)}, f32[24,384]{1,0:T(8,128)S(1)}, u32[]{:S(2)}, u32[]{:S(2)}) collective-permute-start(f32[24,384]{1,0:T(8,128)S(1)} %pad_maximum_fusion.17), channel_id=1, source_target_pairs={{0,2},{1,3},{2,0},{3,1},{4,6},{5,7},{6,4},{7,5},{8,10},{9,11},{10,... | collective-permute-start | bytes 110600 | tf_op jit(solution)/shard_map/ppermute | solution.py:1004
  274.1 10.6 %collective-permute-start.35 = (bf16[8,96,128]{2,1,0:T(8,128)(2,1)S(1)}, bf16[8,96,128]{2,1,0:T(8,128)(2,1)S(1)}, u32[]{:S(2)}, u32[]{:S(2)}) collective-permute-start(bf16[8,96,128]{2,1,0:T(8,128)(2,1)S(1)} %slice.210), channel_id=1, source_target_pairs={{0,2},{1,3},{2,0},{3,1},{4,6},{5,7},{6,4},{7,5},{8,10},{9,11},{10,... | collective-permute-start | bytes 589832 | tf_op jit(solution)/shard_map/ppermute | solution.py:1004
  275.1 9.5 %collective-permute-start.36 = (bf16[4,96,384]{2,1,0:T(8,128)(2,1)S(1)}, bf16[4,96,384]{2,1,0:T(8,128)(2,1)S(1)}, u32[]{:S(2)}, u32[]{:S(2)}) collective-permute-start(bf16[4,96,384]{2,1,0:T(8,128)(2,1)S(1)} %slice_bitcast_fusion.7), channel_id=1, source_target_pairs={{0,4},{4,0},{8,12},{12,8},{16,20},{20,16},{24,28},{28,24},{1,5},{5... | collective-permute-start | bytes 884744 | tf_op jit(solution)/shard_map/ppermute | solution.py:1004
  277.3 19.3 %copy-start.27 = (bf16[4,256,768]{2,1,0:T(8,128)(2,1)S(1)}, bf16[4,256,768]{2,1,0:T(8,128)(2,1)}, u32[]{:S(2)}) copy-start(bf16[4,256,768]{2,1,0:T(8,128)(2,1)} %param.19) | copy-start | bytes 4718596
  284.9 4.6 %collective-permute-start.41 = (f32[24,384]{1,0:T(8,128)S(1)}, f32[24,384]{1,0:T(8,128)S(1)}, u32[]{:S(2)}, u32[]{:S(2)}) collective-permute-start(f32[24,384]{1,0:T(8,128)S(1)} %fusion.23), channel_id=1, source_target_pairs={{0,4},{4,0},{8,12},{12,8},{16,20},{20,16},{24,28},{28,24},{1,5},{5... | collective-permute-start | bytes 110600 | tf_op jit(solution)/shard_map/ppermute | solution.py:1004
  287.4 3.2 %collective-permute-start.39 = (bf16[64,768]{1,0:T(8,128)(2,1)S(1)}, bf16[64,768]{1,0:T(8,128)(2,1)S(1)}, u32[]{:S(2)}, u32[]{:S(2)}) collective-permute-start(bf16[64,768]{1,0:T(8,128)(2,1)S(1)} %slice.303), channel_id=1, source_target_pairs={{1,0},{2,1},{3,2},{5,4},{6,5},{7,6},{9,8},{10,9},{11,10},{13,12},{... | collective-permute-start | bytes 294920 | tf_op jit(solution)/shard_map/ppermute | solution.py:1662
  288.7 5.6 %collective-permute-start.40 = (bf16[4,96,128]{2,1,0:T(8,128)(2,1)S(1)}, bf16[4,96,128]{2,1,0:T(8,128)(2,1)S(1)}, u32[]{:S(2)}, u32[]{:S(2)}) collective-permute-start(bf16[4,96,128]{2,1,0:T(8,128)(2,1)S(1)} %slice_bitcast_fusion.19), channel_id=1, source_target_pairs={{0,4},{4,0},{8,12},{12,8},{16,20},{20,16},{24,28},{28,24},{1,5},{5... | collective-permute-start | bytes 294920 | tf_op jit(solution)/shard_map/ppermute | solution.py:1004
  294.4 10.9 %collective-permute-start.42 = (bf16[2,96,512]{2,1,0:T(8,128)(2,1)S(1)}, bf16[2,96,512]{2,1,0:T(8,128)(2,1)S(1)}, u32[]{:S(2)}, u32[]{:S(2)}) collective-permute-start(bf16[2,96,512]{2,1,0:T(8,128)(2,1)S(1)} %slice_bitcast_fusion.13), channel_id=1, source_target_pairs={{0,8},{4,12},{8,0},{12,4},{16,24},{20,28},{24,16},{28,20},{1,9},{5... | collective-permute-start | bytes 589832 | tf_op jit(solution)/shard_map/ppermute | solution.py:1004
  294.5 10.8 %collective-permute-start.44 = (bf16[2,1,96,384]{3,2,0,1:T(8,128)(2,1)S(1)}, bf16[2,1,96,384]{3,2,0,1:T(8,128)(2,1)S(1)}, u32[]{:S(2)}, u32[]{:S(2)}) collective-permute-start(bf16[2,1,96,384]{3,2,0,1:T(8,128)(2,1)S(1)} %slice_bitcast_fusion.15), channel_id=1, source_target_pairs={{0,16},{4,20},{8,24},{12,28},{16,0},{20,4},{24,8},{28,12},{1,17},{... | collective-permute-start | bytes 442376 | tf_op jit(solution)/shard_map/ppermute | solution.py:1004
  295.3 10.0 %collective-permute-start.43 = (f32[24,384]{1,0:T(8,128)S(1)}, f32[24,384]{1,0:T(8,128)S(1)}, u32[]{:S(2)}, u32[]{:S(2)}) collective-permute-start(f32[24,384]{1,0:T(8,128)S(1)} %add.106), channel_id=1, source_target_pairs={{0,8},{4,12},{8,0},{12,4},{16,24},{20,28},{24,16},{28,20},{1,9},{5... | collective-permute-start | bytes 110600 | tf_op jit(solution)/shard_map/ppermute | solution.py:1004
  296.6 18.3 %copy-start.1 = (bf16[96,256]{1,0:T(8,128)(2,1)S(1)}, bf16[96,256]{1,0:T(8,128)(2,1)}, u32[]{:S(2)}) copy-start(bf16[96,256]{1,0:T(8,128)(2,1)} %param.23) | copy-start | bytes 147460
  305.5 6.5 %collective-permute-start.46 = (f32[24,384]{1,0:T(8,128)S(1)}, f32[24,384]{1,0:T(8,128)S(1)}, u32[]{:S(2)}, u32[]{:S(2)}) collective-permute-start(f32[24,384]{1,0:T(8,128)S(1)} %add.109.both), channel_id=1, source_target_pairs={{0,16},{4,20},{8,24},{12,28},{16,0},{20,4},{24,8},{28,12},{1,17},{... | collective-permute-start | bytes 110600 | tf_op jit(solution)/shard_map/ppermute | solution.py:1004
  306.3 7.2 %collective-permute-start.45 = (bf16[96,512]{1,0:T(8,128)(2,1)S(1)}, bf16[96,512]{1,0:T(8,128)(2,1)S(1)}, u32[]{:S(2)}, u32[]{:S(2)}) collective-permute-start(bf16[96,512]{1,0:T(8,128)(2,1)S(1)} %get-tuple-element.328), channel_id=1, source_target_pairs={{0,16},{4,20},{8,24},{12,28},{16,0},{20,4},{24,8},{28,12},{1,17},{... | collective-permute-start | bytes 294920 | tf_op jit(solution)/shard_map/ppermute | solution.py:1004
  (77 other events, 386.4 us)
